TPU v7x, 512 devices: a whole 4x4x16 slice. The times are simulated.
512 devices in a mesh: seg: 16 (over x, y), op: 32 (over z, core).
Axes of the slice: x: 4, y: 4, z: 16, core: 2. Of those that a mesh axis runs over, the one named last changes fastest.
Arguments:
- theta: bfloat16 [16, 32, 512, 512], P('seg', 'op'), may hold values from -21 to 21
- left_edge: bfloat16 [32, 512, 512], P('op'), may hold values from -1 to 4
- transfer: bfloat16 [16, 32, 512, 512], P('seg', 'op'), may hold values from -1 to 2
- right_env: bfloat16 [16, 32, 512, 512], P('seg', 'op'), may hold values from -1 to 4
- coupling: bfloat16 [16, 32, 512, 512], P('seg', 'op'), may hold values from -0.25 to 0.25
- left_sizes: int32 [32], P('op'), may hold values from 1 to 512, 12288 in all
- right_sizes: int32 [32], P('op'), may hold values from 1 to 512, 12288 in all
Outputs:
- theta_out: float32 [16, 32, 512, 512], P('seg', 'op')
- left_env: bfloat16 [16, 32, 512, 512], P('seg', 'op')
- energy: float32 [16], P('seg')
- first_energy: float32 [16], P('seg')
All inputs are finite; a program needn't handle non-finite values. No bound on the sum of `left_sizes` or of `right_sizes` on one device may be relied on, other than what follows from the above.
Results may differ from a plain program's by a relative error of at most 0.0085.
Values may be sent and summed in bfloat16 or wider, within the bound.
No kernel may reach another device: no remote copies, remote signals or barrier semaphores. Data moves between devices by JAX's collectives and lax.ppermute only.
A program may use at most 128 MiB of HBM per device.

v0:
```python
import jax
import jax.numpy as jnp
from jax import lax
from jax.sharding import PartitionSpec as P

DAVIDSON = 4


epsilon = 1e-06


def carried_in(value, axis, join, neutral):
    count, mine = (lax.axis_size(axis), lax.axis_index(axis))
    pieces = lax.all_gather(value, axis)
    so_far = jnp.full_like(value, 0) + jnp.asarray(neutral, value.dtype)

    def lap(position, so_far):
        longer = join(so_far, pieces[position])
        return jnp.where(position < mine, longer, so_far)

    return lax.fori_loop(0, count - 1, lap, so_far)


def from_behind(block, axis, distance):
    devices = range(lax.axis_size(axis))
    route = [(i - distance, i) for i in devices if i - distance in devices]
    return lax.ppermute(block, axis, route)


def symmetric(block):
    return 0.5 * (block + jnp.swapaxes(block, -1, -2))


def compose(earlier, later):
    return jnp.einsum("kij,kjl->kil", earlier, later, precision=lax.Precision.HIGHEST)


def on_device(theta, left_edge, transfer, right_env, coupling, left_sizes, right_sizes):
    sectors_here = theta.shape[1]
    block_size = theta.shape[3]
    highest = lax.Precision.HIGHEST
    transfers = transfer[0].astype(jnp.float32)
    identity = jnp.broadcast_to(
        jnp.eye(block_size, dtype=jnp.float32), (sectors_here, block_size, block_size)
    )
    prefix = carried_in(transfers, "seg", compose, identity)
    edge_sym = symmetric(left_edge.astype(jnp.float32))
    left_block = jnp.einsum("kji,kjl->kil", prefix, edge_sym, precision=highest)
    left_block = jnp.einsum("kij,kjl->kil", left_block, prefix, precision=highest).astype(
        jnp.bfloat16
    )
    right_block = symmetric(right_env[0].astype(jnp.float32)).astype(jnp.bfloat16)
    coupling_blk = coupling[0]
    row_index = lax.broadcasted_iota(jnp.int32, (sectors_here, block_size, block_size), 1)
    col_index = lax.broadcasted_iota(jnp.int32, (sectors_here, block_size, block_size), 2)
    live_mask = (
        (row_index < left_sizes[:, None, None]) & (col_index < right_sizes[:, None, None])
    ).astype(jnp.float32)

    def apply_field(field):
        middle = jnp.einsum(
            "kij,kjl->kil", left_block, field, preferred_element_type=jnp.float32
        ).astype(jnp.bfloat16)
        diagonal_term = jnp.einsum(
            "kij,kjl->kil", middle, right_block, preferred_element_type=jnp.float32
        )
        received_low = from_behind(field[-1], "op", 1)
        previous = jnp.concatenate([received_low[None], field[:-1]], 0)
        lifted = jnp.einsum("kji,kjl->kil", coupling_blk, field, preferred_element_type=jnp.float32)
        received_up = from_behind(lifted[0], "op", -1)
        upper_part = jnp.concatenate([lifted[1:], received_up[None]], 0)
        lower_term = jnp.einsum(
            "kij,kjl->kil", coupling_blk, previous, preferred_element_type=jnp.float32
        )
        return live_mask * (diagonal_term + lower_term + upper_part)

    start = live_mask * theta[0].astype(jnp.float32)
    start_total = lax.psum(jnp.sum(start * start), "op")
    vector = start / jnp.sqrt(start_total + epsilon)
    image = apply_field(vector.astype(jnp.bfloat16))
    energy = lax.psum(jnp.sum(vector * image), "op")
    first_value = energy
    for sweep_step in range(DAVIDSON):
        residual = image - energy * vector
        correction = residual.astype(jnp.bfloat16)
        corr_wide = correction.astype(jnp.float32)
        corr_norm, cross_term = lax.psum(
            (jnp.sum(corr_wide * corr_wide), jnp.sum(image * corr_wide)), "op"
        )
        applied = apply_field(correction)
        curv_term = lax.psum(jnp.sum(corr_wide * applied), "op")
        scale_norm = jnp.sqrt(corr_norm + epsilon)
        offdiag = cross_term / scale_norm
        diag_value = curv_term / (corr_norm + epsilon)
        half_gap = (diag_value - energy) / 2
        lowest = (energy + diag_value) / 2 - jnp.sqrt(half_gap * half_gap + offdiag * offdiag)
        rotation = lowest - energy
        radius = jnp.sqrt(offdiag * offdiag + rotation * rotation + epsilon)
        vector = (offdiag * vector + rotation * corr_wide / scale_norm) / radius
        image = (offdiag * image + rotation * applied / scale_norm) / radius
        energy = lowest
    return (
        vector[None],
        left_block[None],
        jnp.reshape(energy, (1,)),
        jnp.reshape(first_value, (1,)),
    )


def solution(mesh):
    placed = (
        P("seg", "op", None, None),
        P("op", None, None),
        P("seg", "op", None, None),
        P("seg", "op", None, None),
        P("seg", "op", None, None),
        P("op"),
        P("op"),
    )
    return jax.shard_map(
        on_device,
        mesh=mesh,
        in_specs=placed,
        out_specs=(P("seg", "op", None, None), P("seg", "op", None, None), P("seg"), P("seg")),
        check_vma=False,
    )
```

profile of v0, /device:TPU:6, one launch (start us, length us, event | category | flops | bytes accessed | tf_op | source)
XLA Modules:
  0.0 549.2 jit_solution(17615740072336588663)
XLA Ops:
  7.2 2.3 convert_element_type.154
  10.8 1.9 fusion.30
  12.8 56.5 %psum.98 = f32[]{:T(128)} all-reduce(f32[]{:T(128)} %fusion.30), channel_id=1, replica_groups=mesh['seg'=16,'op'=32] {'op'}, use_global_device_ids=true, to_apply=%region_3.4 | all-reduce | flops 1 | bytes 8 | tf_op jit(solution)/shard_map/psum | solution.py:78
  70.0 2.1 fusion.89
  72.1 2.1 collective-permute-start
  74.2 2.5 convolution_bitcast_fusion.10
  83.1 2.2 fusion.68
  85.3 56.8 %all-gather.2.cloned.1.call-done = f32[16,1,512,512]{3,2,1,0:T(8,128)} async-done(((f32[1,1,512,512]{3,2,1,0:T(8,128)}), f32[16,1,512,512]{3,2,1,0:T(8,128)}) %all-gather.2.cloned.1.call-update) | async-done | bytes 16777232 | tf_op jit(solution)/shard_map/all_gather | solution.py:14
  142.1 47.9 %while.13 = (s32[]{:T(128)}, f32[1,512,512]{1,2,0:T(8,128)S(1)}, s32[]{:T(128)}, f32[16,1,512,512]{3,2,1,0:T(8,128)}, s32[]{:T(128)}) while((s32[]{:T(128)}, f32[1,512,512]{1,2,0:T(8,128)S(1)}, s32[]{:T(128)}, f32[16,1,512,512]{3,2,1,0:T(8,128)}, s32[]{:T(128)}) %tuple.47), condition=%wide.region_1.2_spmd, body=%wide.region_0.1_spmd.sunk | while | flops 1610874880 | bytes 6292039 | solution.py:21
  142.2 3.1 fusion.121
  145.4 3.1 fusion.121
  148.6 3.1 fusion.121
  151.8 3.1 fusion.121
  155.0 3.1 fusion.121
  158.2 3.1 fusion.121
  161.3 3.1 fusion.121
  164.5 3.1 fusion.121
  167.7 3.1 fusion.121
  170.9 3.1 fusion.121
  174.1 3.1 fusion.121
  177.3 3.1 fusion.121
  180.5 3.1 fusion.121
  183.7 3.1 fusion.121
  186.9 3.1 fusion.121
  190.0 3.1 fusion.57
  193.1 1.9 convolution_convert_fusion.5
  195.0 3.1 fusion.20
  198.1 3.0 multiply_reduce_fusion
  201.1 49.9 %psum.99 = f32[]{:T(128)} all-reduce(f32[]{:T(128)} %get-tuple-element.121), channel_id=1, replica_groups=mesh['seg'=16,'op'=32] {'op'}, use_global_device_ids=true, to_apply=%region_5.6 | all-reduce | flops 1 | bytes 8 | tf_op jit(solution)/shard_map/psum | solution.py:81
  254.6 3.8 collective-permute-start.2
  258.5 2.7 fusion.21
  261.2 3.9 fusion.34
  265.1 52.8 %all-reduce.3 = (f32[]{:T(128)}, f32[]{:T(128)}, f32[]{:T(128)}) all-reduce(f32[]{:T(128)} %get-tuple-element.94, f32[]{:T(128)} %get-tuple-element.93, f32[]{:T(128)} %get-tuple-element.92), channel_id=1, replica_groups=mesh['seg'=16,'op'=32] {'op'}, use_global_device_ids=true, to_apply=%region_7.8 | all-reduce | flops 3 | bytes 24 | tf_op jit(solution)/shard_map/psum | solution.py:87
  321.9 2.2 subtract_convert_fusion.2
  326.9 3.9 collective-permute-start.4
  330.8 2.9 fusion.22
  333.7 3.9 fusion.40
  337.6 52.5 %all-reduce.2 = (f32[]{:T(128)}, f32[]{:T(128)}, f32[]{:T(128)}) all-reduce(f32[]{:T(128)} %get-tuple-element.91, f32[]{:T(128)} %get-tuple-element.90, f32[]{:T(128)} %get-tuple-element.89), channel_id=1, replica_groups=mesh['seg'=16,'op'=32] {'op'}, use_global_device_ids=true, to_apply=%region_13.14 | all-reduce | flops 3 | bytes 24 | tf_op jit(solution)/shard_map/psum | solution.py:87
  392.2 3.6 subtract_convert_fusion.1
  397.5 3.8 collective-permute-start.6
  401.4 2.9 fusion.23
  404.3 4.3 fusion.46
  408.6 55.8 %all-reduce.1 = (f32[]{:T(128)}, f32[]{:T(128)}, f32[]{:T(128)}) all-reduce(f32[]{:T(128)} %get-tuple-element.88, f32[]{:T(128)} %get-tuple-element.87, f32[]{:T(128)} %get-tuple-element.86), channel_id=1, replica_groups=mesh['seg'=16,'op'=32] {'op'}, use_global_device_ids=true, to_apply=%region_19.20 | all-reduce | flops 3 | bytes 24 | tf_op jit(solution)/shard_map/psum | solution.py:87
  466.5 2.8 fusion.51
  472.0 3.1 collective-permute-start.8
  475.1 2.9 fusion.24
  478.1 2.8 fusion.67
  480.9 56.8 %all-reduce = (f32[]{:T(128)}, f32[]{:T(128)}, f32[]{:T(128)}) all-reduce(f32[]{:T(128)} %get-tuple-element.85, f32[]{:T(128)} %get-tuple-element.84, f32[]{:T(128)} %fusion.67), channel_id=1, replica_groups=mesh['seg'=16,'op'=32] {'op'}, use_global_device_ids=true, to_apply=%region_25.26 | all-reduce | flops 3 | bytes 24 | tf_op jit(solution)/shard_map/psum | solution.py:87
  (57 shorter events, 19.8 us)
Async XLA Ops:
  7.2 67.0 %copy-start = (bf16[1,1,512,512]{3,2,1,0:T(8,128)(2,1)S(1)}, bf16[1,1,512,512]{3,2,1,0:T(8,128)(2,1)}, u32[]{:S(2)}) copy-start(bf16[1,1,512,512]{3,2,1,0:T(8,128)(2,1)} %param.13) | copy-start | bytes 1572868
  7.2 75.9 %copy-start.5 = (bf16[1,1,512,512]{3,2,1,0:T(8,128)(2,1)S(1)}, bf16[1,1,512,512]{3,2,1,0:T(8,128)(2,1)}, u32[]{:S(2)}) copy-start(bf16[1,1,512,512]{3,2,1,0:T(8,128)(2,1)} %param.12) | copy-start | bytes 1572868
  7.2 134.9 %all-gather.2.cloned.1.call-start = ((), (), s32[]{:S(2)}) async-start(), calls=%async_computation | async-start | bytes 17825792 | tf_op jit(solution)/shard_map/all_gather | solution.py:14
  72.1 126.0 %collective-permute-start = (bf16[512,512]{1,0:T(8,128)(2,1)}, bf16[512,512]{1,0:T(8,128)(2,1)}, u32[]{:S(2)}, u32[]{:S(2)}) collective-permute-start(bf16[512,512]{1,0:T(8,128)(2,1)} %fusion.89), channel_id=1, source_target_pairs={{0,1},{1,2},{2,3},{3,4},{4,5},{5,6},{6,7},{7,8},{8,9},{9,10},{10,1... | collective-permute-start | bytes 1572872 | tf_op jit(solution)/shard_map/ppermute | solution.py:27
  76.7 121.4 %collective-permute-start.1 = (f32[512,512]{1,0:T(8,128)}, f32[512,512]{1,0:T(8,128)}, u32[]{:S(2)}, u32[]{:S(2)}) collective-permute-start(f32[512,512]{1,0:T(8,128)} %convolution_bitcast_fusion.10), channel_id=1, source_target_pairs={{1,0},{2,1},{3,2},{4,3},{5,4},{6,5},{7,6},{8,7},{9,8},{10,9},{11,1... | collective-permute-start | bytes 3145736 | tf_op jit(solution)/shard_map/ppermute | solution.py:27
  142.1 56.0 %copy-start.1 = (bf16[1,1,512,512]{3,2,1,0:T(8,128)(2,1)S(1)}, bf16[1,1,512,512]{3,2,1,0:T(8,128)(2,1)}, u32[]{:S(2)}) copy-start(bf16[1,1,512,512]{3,2,1,0:T(8,128)(2,1)} %param.9) | copy-start | bytes 1572868
  195.0 127.0 %copy-start.6 = (bf16[512,512]{1,0:T(8,128)(2,1)}, bf16[512,512]{1,0:T(8,128)(2,1)S(1)}, u32[]{:S(2)}) copy-start(bf16[512,512]{1,0:T(8,128)(2,1)S(1)} %convolution_convert_fusion.5) | copy-start | bytes 1572868
  201.1 120.9 %copy-start.3 = (f32[512,512]{1,0:T(8,128)}, f32[512,512]{1,0:T(8,128)S(1)}, u32[]{:S(2)}) copy-start(f32[512,512]{1,0:T(8,128)S(1)} %get-tuple-element.122) | copy-start | bytes 3145732
  253.4 7.9 %collective-permute-start.3 = (f32[512,512]{1,0:T(8,128)}, f32[512,512]{1,0:T(8,128)}, u32[]{:S(2)}, u32[]{:S(2)}) collective-permute-start(f32[512,512]{1,0:T(8,128)} %convolution_bitcast_fusion.9), channel_id=1, source_target_pairs={{1,0},{2,1},{3,2},{4,3},{5,4},{6,5},{7,6},{8,7},{9,8},{10,9},{11,1... | collective-permute-start | bytes 3145736 | tf_op jit(solution)/shard_map/ppermute | solution.py:27
  254.6 6.6 %collective-permute-start.2 = (bf16[512,512]{1,0:T(8,128)(2,1)S(1)}, bf16[512,512]{1,0:T(8,128)(2,1)}, u32[]{:S(2)}, u32[]{:S(2)}) collective-permute-start(bf16[512,512]{1,0:T(8,128)(2,1)S(1)} %subtract_convert_fusion.3), channel_id=1, source_target_pairs={{0,1},{1,2},{2,3},{3,4},{4,5},{5,6},{6,7},{7,8},{8,9},{9,10},{10,1... | collective-permute-start | bytes 1572872 | tf_op jit(solution)/shard_map/ppermute | solution.py:27
  324.2 68.0 %copy-start.2 = (f32[512,512]{1,0:T(8,128)}, f32[512,512]{1,0:T(8,128)S(1)}, u32[]{:S(2)}) copy-start(f32[512,512]{1,0:T(8,128)S(1)} %get-tuple-element.120) | copy-start | bytes 3145732
  324.2 68.0 %copy-start.4 = (bf16[512,512]{1,0:T(8,128)(2,1)}, bf16[512,512]{1,0:T(8,128)(2,1)S(1)}, u32[]{:S(2)}) copy-start(bf16[512,512]{1,0:T(8,128)(2,1)S(1)} %get-tuple-element.119) | copy-start | bytes 1572868
  325.7 8.0 %collective-permute-start.5 = (f32[512,512]{1,0:T(8,128)}, f32[512,512]{1,0:T(8,128)}, u32[]{:S(2)}, u32[]{:S(2)}) collective-permute-start(f32[512,512]{1,0:T(8,128)} %convolution_bitcast_fusion.8), channel_id=1, source_target_pairs={{1,0},{2,1},{3,2},{4,3},{5,4},{6,5},{7,6},{8,7},{9,8},{10,9},{11,1... | collective-permute-start | bytes 3145736 | tf_op jit(solution)/shard_map/ppermute | solution.py:27
  326.9 6.8 %collective-permute-start.4 = (bf16[512,512]{1,0:T(8,128)(2,1)S(1)}, bf16[512,512]{1,0:T(8,128)(2,1)}, u32[]{:S(2)}, u32[]{:S(2)}) collective-permute-start(bf16[512,512]{1,0:T(8,128)(2,1)S(1)} %get-tuple-element.119), channel_id=1, source_target_pairs={{0,1},{1,2},{2,3},{3,4},{4,5},{5,6},{6,7},{7,8},{8,9},{9,10},{10,1... | collective-permute-start | bytes 1572872 | tf_op jit(solution)/shard_map/ppermute | solution.py:27
  396.2 8.1 %collective-permute-start.7 = (f32[512,512]{1,0:T(8,128)S(1)}, f32[512,512]{1,0:T(8,128)}, u32[]{:S(2)}, u32[]{:S(2)}) collective-permute-start(f32[512,512]{1,0:T(8,128)S(1)} %convolution_bitcast_fusion.7), channel_id=1, source_target_pairs={{1,0},{2,1},{3,2},{4,3},{5,4},{6,5},{7,6},{8,7},{9,8},{10,9},{11,1... | collective-permute-start | bytes 3145736 | tf_op jit(solution)/shard_map/ppermute | solution.py:27
  397.5 6.8 %collective-permute-start.6 = (bf16[512,512]{1,0:T(8,128)(2,1)S(1)}, bf16[512,512]{1,0:T(8,128)(2,1)}, u32[]{:S(2)}, u32[]{:S(2)}) collective-permute-start(bf16[512,512]{1,0:T(8,128)(2,1)S(1)} %get-tuple-element.116), channel_id=1, source_target_pairs={{0,1},{1,2},{2,3},{3,4},{4,5},{5,6},{6,7},{7,8},{8,9},{9,10},{10,1... | collective-permute-start | bytes 1572872 | tf_op jit(solution)/shard_map/ppermute | solution.py:27
  470.8 7.3 %collective-permute-start.9 = (f32[512,512]{1,0:T(8,128)}, f32[512,512]{1,0:T(8,128)}, u32[]{:S(2)}, u32[]{:S(2)}) collective-permute-start(f32[512,512]{1,0:T(8,128)} %convolution_bitcast_fusion.6), channel_id=1, source_target_pairs={{1,0},{2,1},{3,2},{4,3},{5,4},{6,5},{7,6},{8,7},{9,8},{10,9},{11,1... | collective-permute-start | bytes 3145736 | tf_op jit(solution)/shard_map/ppermute | solution.py:27
  472.0 6.0 %collective-permute-start.8 = (bf16[512,512]{1,0:T(8,128)(2,1)S(1)}, bf16[512,512]{1,0:T(8,128)(2,1)S(1)}, u32[]{:S(2)}, u32[]{:S(2)}) collective-permute-start(bf16[512,512]{1,0:T(8,128)(2,1)S(1)} %get-tuple-element.115), channel_id=1, source_target_pairs={{0,1},{1,2},{2,3},{3,4},{4,5},{5,6},{6,7},{7,8},{8,9},{9,10},{10,1... | collective-permute-start | bytes 1572872 | tf_op jit(solution)/shard_map/ppermute | solution.py:27
Sparse Core Ops, SparseCore 0:
  11.0 131.0 all-gather.1
where the time goes:
time: 554 us; the launch traced here: 549 us
  blocking collectives  324 us (58%)
  matrix products  91.1 us (16%)
  waiting for transfers between devices  56.8 us (10%)
  between operations  27.7 us (5%)
  starting transfers between devices  23.1 us (4%)
  other arithmetic  20.7 us (4%)
    psum x4, blocking collectives, on_device(): lax.psum((jnp.sum(corr_wide * corr_wide), jnp.sum(image * corr_wide)), 'op')  218 us
    all_gather x1, waiting for transfers between devices, carried_in(): pieces = lax.all_gather(value, axis)  56.8 us
    psum x1, blocking collectives, on_device(): start_total = lax.psum(jnp.sum(start * start), 'op')  56.5 us
    psum x1, blocking collectives, on_device(): energy = lax.psum(jnp.sum(vector * image), 'op')  49.9 us
    dot_general x15, matrix products, compose(): jnp.einsum('kij,kjl->kil', earlier, later, precision=lax.Precision.HIGHEST)  46.3 us
    ppermute x10, starting transfers between devices, from_behind(): return lax.ppermute(block, axis, route)  23.1 us
    dot_general x5, matrix products, apply_field(): jnp.einsum('kij,kjl->kil', coupling_blk, previous, preferred_element_type...  17.8 us
    dot_general x5, matrix products, apply_field(): jnp.einsum('kij,kjl->kil', middle, right_block, preferred_element_type=jn...  14.6 us
  transfers between devices with their start and end apart: 11, of which 1 were waited for; matrix products, arithmetic and copies ran while one was open for 15% of the time, Pallas kernels for 0%

commit v1 on v0

v1 whole, which is shorter than its diff:
```python
import functools

import jax
import jax.numpy as jnp
from jax import lax
from jax.experimental import pallas as pl
from jax.experimental.pallas import tpu as pltpu
from jax.sharding import PartitionSpec as P

DAVIDSON = 4
ROW = 4
LANES = 128
STEP = 128
BAND = 32
SHIFT = 2.0
epsilon = 1e-06

f32, bf16 = jnp.float32, jnp.bfloat16
VMEM = pl.BlockSpec(memory_space=pltpu.VMEM)
SMEM = pl.BlockSpec(memory_space=pltpu.SMEM)


def wide_dot(a, b):
    return jnp.dot(a, b, preferred_element_type=f32)


def left_transposed_dot(a, b):
    return lax.dot_general(a, b, (((0,), (0,)), ((), ())), preferred_element_type=f32)


def split(x):
    high = x.astype(bf16)
    return high, (x - high.astype(f32)).astype(bf16)


def total(x):
    return jnp.sum(jnp.sum(x, axis=0, keepdims=True), axis=1, keepdims=True)


def in_lanes(first, values):
    lane = lax.broadcasted_iota(jnp.int32, (1, LANES), 1)
    out = jnp.zeros((1, LANES), f32)
    for i, value in enumerate(values):
        out = jnp.where(lane == first + i, value, out)
    return out


def live(start, rows, cols, sizes):
    row = lax.broadcasted_iota(jnp.int32, (rows, cols), 0) + start
    col = lax.broadcasted_iota(jnp.int32, (rows, cols), 1)
    return (row < sizes[0]) & (col < sizes[1])


def banded_dots(fields, last):
    n, cols = last.shape

    def band(i, sums):
        at = pl.ds(pl.multiple_of(i * BAND, BAND), BAND)
        mine = last[at, :].astype(f32)
        return tuple(
            s + jnp.sum((f[at, :].astype(f32) * mine).reshape(BAND // 8, 8, cols), axis=0)
            for s, f in zip(sums, fields, strict=True)
        )

    sums = lax.fori_loop(0, n // BAND, band, tuple(jnp.zeros((8, cols), f32) for _ in fields))
    return [total(s) for s in sums]


def call(kernel, out, flops=2e8, bytes_accessed=3e6, smem=1, scratch=()):
    def run(*args):
        return pl.pallas_call(
            kernel,
            out_shape=out,
            in_specs=[SMEM] * smem + [VMEM] * (len(args) - smem),
            out_specs=jax.tree.map(lambda _: VMEM, out),
            scratch_shapes=list(scratch),
            cost_estimate=pl.CostEstimate(
                flops=int(flops), bytes_accessed=int(bytes_accessed), transcendentals=0
            ),
            compiler_params=pltpu.CompilerParams(vmem_limit_bytes=48 * 1024 * 1024),
        )(*args)

    return run


def prepare_kernel(sizes, theta, edge, right, field, edge_out, right_out, lifted, stats):
    n = theta.shape[0]
    for c in range(0, n, STEP):
        keep = live(c, STEP, n, sizes)
        field[c : c + STEP, :] = jnp.where(
            keep, theta[c : c + STEP, :].astype(f32), 0.0
        ).astype(bf16)
    for source, out in ((edge, edge_out), (right, right_out)):
        for c in range(0, n, STEP):
            turned = source[:, c : c + STEP].astype(f32).T
            out[c : c + STEP, :] = (0.5 * (source[c : c + STEP, :].astype(f32) + turned)).astype(
                out.dtype
            )
    for c in range(0, n, STEP):
        lifted[c : c + STEP, :] = wide_dot(field[c : c + STEP, :], right_out[...]).astype(bf16)
    stats[...] = in_lanes(0, banded_dots([field], field))


def survey_kernel(transfer, edge, right, coupling, stats):
    n = transfer.shape[0]
    (grown,), (edge_sq,), (right_sq,), (coupling_sq,) = (
        banded_dots([x], x) for x in (transfer, edge, right, coupling)
    )
    edge_trace = right_trace = jnp.zeros((1, 1), f32)
    for c in range(0, n, LANES):
        diagonal = lax.broadcasted_iota(jnp.int32, (LANES, LANES), 0) == lax.broadcasted_iota(
            jnp.int32, (LANES, LANES), 1
        )
        at = slice(c, c + LANES)
        edge_trace += total(jnp.where(diagonal, edge[at, at].astype(f32), 0.0))
        right_trace += total(jnp.where(diagonal, right[at, at].astype(f32), 0.0))
    values = (
        grown / n,
        jnp.sqrt(edge_sq / n) * jnp.sqrt(right_sq / n),
        coupling_sq / n,
        edge_trace / n * (right_trace / n),
    )
    stats[...] = jnp.broadcast_to(in_lanes(0, values), stats.shape)


def couple_kernel(place, coupling, above, field_a, field_b, near, far, image):
    n = coupling.shape[0]
    odd = place[0] == 1

    @pl.when(odd)
    def _():
        near[...] = coupling[...]
        for c in range(0, n, STEP):
            far[c : c + STEP, :] = above[:, c : c + STEP].astype(f32).T.astype(bf16)

    @pl.when(jnp.logical_not(odd))
    def _():
        far[...] = coupling[...]
        for c in range(0, n, STEP):
            near[c : c + STEP, :] = above[:, c : c + STEP].astype(f32).T.astype(bf16)

    for c in range(0, n, STEP):
        at = slice(c, c + STEP)
        image[at, :] = wide_dot(near[at, :], field_a[...]) + wide_dot(far[at, :], field_b[...])


def in_order(place, own, behind, ahead, across, held):
    held[place] = own[...]
    held[lax.rem(place + 1, ROW)] = ahead[...]
    held[lax.rem(place + 2, ROW)] = across[...]
    held[lax.rem(place + 3, ROW)] = behind[...]


def row_kernel(place, own, behind, ahead, across, whole, high, low, held):
    y = place[0]
    in_order(y, own, behind, ahead, across, held)
    n = own.shape[0]

    @pl.when(y == 0)
    def _():
        row = lax.broadcasted_iota(jnp.int32, (n, n), 0)
        col = lax.broadcasted_iota(jnp.int32, (n, n), 1)
        high[...] = jnp.where(row == col, 1.0, 0.0).astype(bf16)
        low[...] = jnp.zeros((n, n), bf16)

    @pl.when(y == 1)
    def _():
        high[...] = held[0]
        low[...] = jnp.zeros((n, n), bf16)

    product = wide_dot(held[0], held[1])
    for position in range(2, ROW):
        upper, lower = split(product)

        @pl.when(y == position)
        def _(upper=upper, lower=lower):
            high[...] = upper
            low[...] = lower

        product = wide_dot(upper, held[position]) + wide_dot(lower, held[position])
    whole[...] = product.astype(bf16)


def segment_kernel(
    place, tune, own, behind, ahead, across, high_in, low_in, edge, lifted, couplings, field,
    left, next_field, held, high, low,
):
    x = place[0]
    sizes = (place[1], place[2])
    n = own.shape[0]
    in_order(x, own, behind, ahead, across, held)
    high[...] = high_in[...]
    low[...] = low_in[...]
    for position in range(ROW - 2, -1, -1):

        @pl.when(position < x)
        def _(position=position):
            product = wide_dot(held[position], high[...]) + wide_dot(held[position], low[...])
            upper, lower = split(product)
            high[...] = upper
            low[...] = lower

    edge_high, edge_low = split(edge[...])
    turned = (
        wide_dot(edge_high, high[...]) + wide_dot(edge_high, low[...]) + wide_dot(edge_low, high[...])
    )
    upper, lower = split(turned)
    block = (
        left_transposed_dot(high[...], upper)
        + left_transposed_dot(low[...], upper)
        + left_transposed_dot(high[...], lower)
    ).astype(bf16)
    left[...] = block
    for c in range(0, n, STEP):
        at = slice(c, c + STEP)
        image = wide_dot(left[at, :], lifted[...]) + couplings[at, :]
        moved = (image - tune[0] * field[at, :].astype(f32)) * tune[1]
        next_field[at, :] = jnp.where(live(c, STEP, n, sizes), moved, 0.0).astype(bf16)


def local_kernel(count, left, right, near, field_a, *rest):
    fields, (partial, stats) = rest[:count], rest[count:]
    field = fields[-1]
    n = field.shape[0]
    for c in range(0, n, STEP):
        at = slice(c, c + STEP)
        middle = wide_dot(left[at, :], field[...]).astype(bf16)
        partial[at, :] = wide_dot(middle, right[...]) + wide_dot(near[at, :], field_a[...])
    k = count - 1
    stats[...] = in_lanes(k * (k + 1) // 2, banded_dots(list(fields), field))


def advance_kernel(place, tune, partial, far, field_b, field, next_field):
    sizes = (place[1], place[2])
    n = field.shape[0]
    for c in range(0, n, STEP):
        at = slice(c, c + STEP)
        image = partial[at, :] + wide_dot(far[at, :], field_b[...])
        moved = (image - tune[0] * field[at, :].astype(f32)) * tune[1]
        next_field[at, :] = jnp.where(live(c, STEP, n, sizes), moved, 0.0).astype(bf16)


def advance_last_kernel(place, tune, partial, far, field_b, field, next_field, sent, kept):
    advance_kernel(place, tune, partial, far, field_b, field, next_field)
    half = field.shape[1] // 2

    @pl.when(place[0] == 1)
    def _():
        sent[...] = next_field[:, :half]
        kept[...] = next_field[:, half:]

    @pl.when(place[0] != 1)
    def _():
        sent[...] = next_field[:, half:]
        kept[...] = next_field[:, :half]


def close_kernel(count, far, got, kept, partial, last, *rest):
    stats_in, out = rest[:count], rest[count]
    n = last.shape[0]
    inner = jnp.zeros((1, 1), f32)
    for c in range(0, n, STEP):
        at = slice(c, c + STEP)
        crossing = wide_dot(far[at, :], got[...]) * kept[at, :].astype(f32)
        inner += 2.0 * total(crossing) + total(partial[at, :] * last[at, :].astype(f32))
    k = DAVIDSON + 1
    sums = in_lanes(k * (k + 1) // 2, [inner])
    for piece in stats_in:
        sums += piece[...]
    out[...] = jnp.broadcast_to(sums, out.shape)


def solve_kernel(tune, sums, *rest):
    size = DAVIDSON + 1
    fields, (vector, energies) = rest[:size], rest[size:]
    shift = jnp.full((1, 1), tune[0], f32)
    scale = jnp.full((1, 1), tune[2], f32)
    row = jnp.sum(sums[...], axis=0, keepdims=True)
    lane = lax.broadcasted_iota(jnp.int32, (1, LANES), 1)

    def entry(i):
        return jnp.sum(jnp.where(lane == i, row, 0.0), axis=1, keepdims=True)

    gram = {}
    for k in range(size):
        for j in range(k + 1):
            gram[j, k] = gram[k, j] = entry(k * (k + 1) // 2 + j)
    image_gram = {}
    for j in range(size):
        for k in range(j, size):
            if j < size - 1:
                value = scale * gram[j + 1, k] + shift * gram[j, k]
            else:
                value = entry(size * (size + 1) // 2)
            image_gram[j, k] = image_gram[k, j] = value

    def form(table, a, b):
        out = jnp.zeros((1, 1), f32)
        for j, aj in enumerate(a):
            if aj is None:
                continue
            inner = jnp.zeros((1, 1), f32)
            for k, bk in enumerate(b):
                if bk is not None:
                    inner = inner + table[j, k] * bk
            out = out + aj * inner
        return out

    weights = [1.0 / jnp.sqrt(gram[0, 0] + epsilon)] + [None] * (size - 1)
    energy = first = form(image_gram, weights, weights)
    for step in range(DAVIDSON):
        turn = [None] * size
        for k in range(step + 2):
            value = None
            if weights[k] is not None:
                value = (shift - energy) * weights[k]
            if k > 0 and weights[k - 1] is not None:
                carried = scale * weights[k - 1]
                value = carried if value is None else value + carried
            turn[k] = value
        corr_norm = jnp.maximum(form(gram, turn, turn), 0.0)
        cross_term = form(image_gram, weights, turn)
        curv_term = form(image_gram, turn, turn)
        scale_norm = jnp.sqrt(corr_norm + epsilon)
        offdiag = cross_term / scale_norm
        diag_value = curv_term / (corr_norm + epsilon)
        half_gap = (diag_value - energy) / 2
        lowest = (energy + diag_value) / 2 - jnp.sqrt(half_gap * half_gap + offdiag * offdiag)
        rotation = lowest - energy
        radius = jnp.sqrt(offdiag * offdiag + rotation * rotation + epsilon)
        keep, add = offdiag / radius, rotation / scale_norm / radius
        weights = [
            None
            if t is None
            else add * t if w is None else keep * w + add * t
            for w, t in zip(weights, turn, strict=True)
        ]
        energy = lowest
    energies[...] = in_lanes(0, [energy, first])
    n = vector.shape[0]

    def band(i, carry):
        at = pl.ds(pl.multiple_of(i * BAND, BAND), BAND)
        out = weights[0] * fields[0][at, :].astype(f32)
        for w, field in zip(weights[1:], fields[1:], strict=True):
            out = out + w * field[at, :].astype(f32)
        vector[at, :] = out
        return carry

    lax.fori_loop(0, n // BAND, band, 0)


def routes(axis_size):
    def along_y(d):
        return [(s, s - s % ROW + (s + d) % ROW) for s in range(axis_size)]

    def along_x(d):
        return [(s, (s + ROW * d) % axis_size) for s in range(axis_size)]

    return along_y, along_x


def on_device(theta, left_edge, transfer, right_env, coupling, left_sizes, right_sizes):
    n = theta.shape[-1]
    theta, left_edge = theta[0, 0], left_edge[0]
    transfer, right_env, coupling = transfer[0, 0], right_env[0, 0], coupling[0, 0]
    seg, op = lax.axis_index("seg"), lax.axis_index("op")
    segments, sectors = lax.axis_size("seg"), lax.axis_size("op")
    along_y, along_x = routes(segments)
    near_swap = [(i, i ^ 1) for i in range(sectors)]
    far_swap = [(i, i + 1 if i % 2 else i - 1) for i in range(1, sectors - 1)]
    down = [(i + 1, i) for i in range(sectors - 1)]
    square, wide = jax.ShapeDtypeStruct((n, n), bf16), jax.ShapeDtypeStruct((n, n), f32)
    tall = jax.ShapeDtypeStruct((n, n // 2), bf16)
    lanes = jax.ShapeDtypeStruct((1, LANES), f32)
    spread = jax.ShapeDtypeStruct((sectors, LANES), f32)
    sizes = jnp.concatenate([left_sizes, right_sizes])
    odd = lax.rem(op, 2)
    place = jnp.concatenate([jnp.reshape(odd, (1,)), sizes])

    def seg_send(x, route):
        return lax.ppermute(x, "seg", route)

    def op_send(x, route):
        return lax.ppermute(x, "op", route)

    def op_sum(x):
        return lax.all_to_all(x[:, None], "op", 0, 0)[:, 0]

    t_behind = seg_send(transfer, along_y(1))
    t_ahead = seg_send(transfer, along_y(-1))
    t_across = seg_send(transfer, along_y(2))

    field, edge_sym, right, lifted, stats = call(
        prepare_kernel, (square, wide, square, square, lanes)
    )(sizes, theta, left_edge, right_env)
    above = op_send(coupling, down)
    field_b = op_send(field, far_swap)
    field_a = op_send(field, near_swap)
    near, far, couplings = call(couple_kernel, (square, square, wide))(
        place, coupling, above, field_a, field_b
    )
    survey = call(survey_kernel, spread, smem=0)(transfer, left_edge, right_env, coupling)

    whole, high, low = call(
        row_kernel,
        (square, square, square),
        scratch=[pltpu.VMEM((ROW, n, n), bf16)],
    )(jnp.reshape(lax.rem(seg, ROW), (1,)), transfer, t_behind, t_ahead, t_across)
    r_behind = seg_send(whole, along_x(1))
    r_ahead = seg_send(whole, along_x(-1))
    r_across = seg_send(whole, along_x(2))

    found = jnp.sum(op_sum(survey), axis=0) / sectors
    growth = jnp.exp(
        jnp.clip(seg.astype(f32) * jnp.log(jnp.maximum(found[0], 1e-30)), -30.0, 30.0)
    )
    scale = found[1] * growth + 2.0 * jnp.sqrt(found[2]) + 1e-12
    shift = SHIFT * found[3] * growth
    tune = jnp.stack([shift, 1.0 / scale, scale])

    left, following = call(
        segment_kernel,
        (square, square),
        smem=2,
        scratch=[
            pltpu.VMEM((ROW, n, n), bf16),
            pltpu.VMEM((n, n), bf16),
            pltpu.VMEM((n, n), bf16),
        ],
    )(
        jnp.concatenate([jnp.reshape(seg // ROW, (1,)), sizes]), tune,
        whole, r_behind, r_ahead, r_across, high, low, edge_sym, lifted, couplings, field,
    )
    fields, pieces = [field, following], [stats]
    sent = kept = None
    for k in range(1, DAVIDSON + 1):
        last = k == DAVIDSON
        newest = fields[-1]
        field_b = op_send(sent if last else newest, far_swap)
        field_a = op_send(newest, near_swap)
        partial, stats = call(functools.partial(local_kernel, k + 1), (wide, lanes), smem=0)(
            left, right, near, field_a, *fields
        )
        pieces.append(stats)
        if last:
            sums = call(functools.partial(close_kernel, len(pieces)), spread, smem=0)(
                far, field_b, kept, partial, newest, *pieces
            )
        elif k == DAVIDSON - 1:
            following, sent, kept = call(advance_last_kernel, (square, tall, tall), smem=2)(
                place, tune, partial, far, field_b, newest
            )
            fields.append(following)
        else:
            following = call(advance_kernel, square, smem=2)(
                place, tune, partial, far, field_b, newest
            )
            fields.append(following)
    vector, energies = call(solve_kernel, (wide, lanes))(tune, op_sum(sums), *fields)
    return (
        vector[None, None],
        left[None, None],
        energies[0, 0:1],
        energies[0, 1:2],
    )


def solution(mesh):
    placed = (
        P("seg", "op", None, None),
        P("op", None, None),
        P("seg", "op", None, None),
        P("seg", "op", None, None),
        P("seg", "op", None, None),
        P("op"),
        P("op"),
    )
    return jax.shard_map(
        on_device,
        mesh=mesh,
        in_specs=placed,
        out_specs=(P("seg", "op", None, None), P("seg", "op", None, None), P("seg"), P("seg")),
        check_vma=False,
    )
```

time: 554 us -> 170 us (0.31)
  blocking collectives: 324 us -> 33.1 us
  matrix products: 91.1 us -> 0 us
  starting transfers between devices: 23.1 us -> 73.8 us
  waiting for transfers between devices: 56.8 us -> 19 us
  Pallas kernels: 0 us -> 29 us
  between operations: 27.7 us -> 4.98 us
  other arithmetic: 20.7 us -> 0.36 us
    psum x6 -> x0, blocking collectives: 324 us -> none  [the longest x4 218 us: on_device(): lax.psum((jnp.sum(corr_wide * corr_wide), jnp.sum(image * corr_wide)), 'op')]
    dot_general x32 -> x0, matrix products: 91.1 us -> none  [the longest x15 46.3 us: compose(): jnp.einsum('kij,kjl->kil', earlier, later, precision=lax.Precision.HIGHEST)]
    all_gather x1 -> x0, waiting for transfers between devices: 56.8 us -> none  [carried_in(): pieces = lax.all_gather(value, axis)]
    ppermute x10 -> x17, starting transfers between devices: 23.1 us -> 57.2 us  [the longest x11 37.1 us: op_send(): return lax.ppermute(x, 'op', route)]
    all_to_all x0 -> x1, blocking collectives: none -> 33.1 us  [op_sum(): return lax.all_to_all(x[:, None], 'op', 0, 0)[:, 0]]
    pallas_call x0 -> x14, Pallas kernels: none -> 29 us  [run(): pl.pallas_call(kernel, out_shape=out, in_specs=[SMEM] * smem + [VMEM] * (...]
    ppermute x10 -> x17, waiting for transfers between devices: 0.03 us -> 19 us  [the longest x6 15.5 us: seg_send(): return lax.ppermute(x, 'seg', route)]
    all_to_all x0 -> x1, starting transfers between devices: none -> 16.7 us  [op_sum(): return lax.all_to_all(x[:, None], 'op', 0, 0)[:, 0]]
  transfers between devices with their start and end apart: 11 -> 18, of which waited for: 1 -> 6; matrix products, arithmetic and copies ran while one was open for 15% -> 1% of each run, Pallas kernels for 0% -> 10%
where the time goes in v1:
time: 170 us; the launch traced here: 169 us
  starting transfers between devices  73.8 us (43%)
  blocking collectives  33.1 us (19%)
  Pallas kernels  29 us (17%)
  waiting for transfers between devices  19 us (11%)
  local copies, waits for them, and re-layouts  8.71 us (5%)
  between operations  4.98 us (3%)
    ppermute x11, starting transfers between devices, op_send(): return lax.ppermute(x, 'op', route)  37.1 us
    all_to_all x1, blocking collectives, op_sum(): return lax.all_to_all(x[:, None], 'op', 0, 0)[:, 0]  33.1 us
    pallas_call x14, Pallas kernels, run(): pl.pallas_call(kernel, out_shape=out, in_specs=[SMEM] * smem + [VMEM] * (...  29 us
    ppermute x6, starting transfers between devices, seg_send(): return lax.ppermute(x, 'seg', route)  20.1 us
    all_to_all x1, starting transfers between devices, op_sum(): return lax.all_to_all(x[:, None], 'op', 0, 0)[:, 0]  16.7 us
    ppermute x6, waiting for transfers between devices, seg_send(): return lax.ppermute(x, 'seg', route)  15.5 us
    unnamed x28, local copies, waits for them, and re-layouts  7.53 us
    ppermute x11, waiting for transfers between devices, op_send(): return lax.ppermute(x, 'op', route)  3.47 us
  transfers between devices with their start and end apart: 18, of which 6 were waited for; matrix products, arithmetic and copies ran while one was open for 1% of the time, Pallas kernels for 10%

profile of v1, /device:TPU:6, one launch (start us, length us, event | category | flops | bytes accessed | tf_op | source)
XLA Modules:
  0.0 168.9 jit_solution(1290547994442552757)
XLA Ops:
  0.6 3.5 %collective-permute-start.3 = (bf16[512,512]{1,0:T(8,128)(2,1)}, bf16[512,512]{1,0:T(8,128)(2,1)}, u32[]{:S(2)}, u32[]{:S(2)}) collective-permute-start(bf16[512,512]{1,0:T(8,128)(2,1)} %bitcast.27), channel_id=1, source_target_pairs={{0,32},{32,64},{64,96},{96,0},{128,160},{160,192},{192,224},{224,1... | collective-permute-start | bytes 1572872 | tf_op jit(solution)/shard_map/ppermute | solution.py:382
  4.1 3.6 %collective-permute-start.4 = (bf16[512,512]{1,0:T(8,128)(2,1)}, bf16[512,512]{1,0:T(8,128)(2,1)}, u32[]{:S(2)}, u32[]{:S(2)}) collective-permute-start(bf16[512,512]{1,0:T(8,128)(2,1)} %bitcast.28), channel_id=1, source_target_pairs={{0,96},{32,0},{64,32},{96,64},{128,224},{160,128},{192,160},{224,1... | collective-permute-start | bytes 1572872 | tf_op jit(solution)/shard_map/ppermute | solution.py:382
  7.7 3.9 %collective-permute-start.5 = (bf16[512,512]{1,0:T(8,128)(2,1)}, bf16[512,512]{1,0:T(8,128)(2,1)}, u32[]{:S(2)}, u32[]{:S(2)}) collective-permute-start(bf16[512,512]{1,0:T(8,128)(2,1)} %bitcast.29), channel_id=1, source_target_pairs={{0,64},{32,96},{64,0},{96,32},{128,192},{160,224},{192,128},{224,1... | collective-permute-start | bytes 1572872 | tf_op jit(solution)/shard_map/ppermute | solution.py:382
  13.0 1.0 copy-done.4
  14.0 1.0 copy-done.5
  15.1 1.0 copy-done.7
  16.1 1.5 shard_map.103
  17.6 0.8 copy-done.8
  18.4 1.9 %collective-permute-start.1 = (bf16[512,512]{1,0:T(8,128)(2,1)S(1)}, bf16[512,512]{1,0:T(8,128)(2,1)}, u32[]{:S(2)}, u32[]{:S(2)}) collective-permute-start(bf16[512,512]{1,0:T(8,128)(2,1)S(1)} %get-tuple-element.30.field.rest_0_), channel_id=1, source_target_pairs={{0,1},{1,0},{2,3},{3,2},{4,5},{5,4},{6,7},{7,6},{8,9},{9,8},{10,11... | collective-permute-start | bytes 1572872 | tf_op jit(solution)/shard_map/ppermute | solution.py:385
  20.3 1.5 collective-permute-start.2
  21.8 1.6 shard_map.102
  23.5 16.7 %all-to-all-start = ((f32[32,1,128]{2,1,0:T(1,128)}), f32[32,1,128]{2,1,0:T(1,128)S(1)}, u32[]{:S(2)}, u32[]{:S(2)}) async-start(f32[32,1,128]{2,1,0:T(1,128)} %bitcast.5), calls=%async_computation | async-start | bytes 32768 | tf_op jit(solution)/shard_map/all_to_all | solution.py:388
  40.2 1.3 collective-permute-start
  41.6 4.4 %shard_map.105 = (bf16[512,512]{1,0:T(8,128)(2,1)}, bf16[512,512]{1,0:T(8,128)(2,1)S(1)}, bf16[512,512]{1,0:T(8,128)(2,1)S(1)}) custom-call(s32[1]{0:T(128)} %bitcast.16.place, bf16[512,512]{1,0:T(8,128)(2,1)S(1)} %bitcast.31, bf16[512,512]{1,0:T(8,128)(2,1)} %collective-permute-done.3.behind, bf16[512,512]{1,0:T(8,128)(2,1)} %collective-permute-done.4.ahead, ...), custom_call_target="tpu_custom_call" | custom-call | flops 200000000 | bytes 3000000 | tf_op jit(solution)/shard_map/pallas_call | solution.py:71
  46.0 0.8 copy-done.10
  46.8 0.8 copy-done.12
  47.6 2.4 %collective-permute-start.6 = (bf16[512,512]{1,0:T(8,128)(2,1)}, bf16[512,512]{1,0:T(8,128)(2,1)S(1)}, u32[]{:S(2)}, u32[]{:S(2)}) collective-permute-start(bf16[512,512]{1,0:T(8,128)(2,1)} %get-tuple-element.32.own), channel_id=1, source_target_pairs={{0,128},{32,160},{64,192},{96,224},{128,256},{160,288},{192,320},{... | collective-permute-start | bytes 1572872 | tf_op jit(solution)/shard_map/ppermute | solution.py:382
  50.0 3.5 %collective-permute-start.7 = (bf16[512,512]{1,0:T(8,128)(2,1)}, bf16[512,512]{1,0:T(8,128)(2,1)}, u32[]{:S(2)}, u32[]{:S(2)}) collective-permute-start(bf16[512,512]{1,0:T(8,128)(2,1)} %get-tuple-element.32.own), channel_id=1, source_target_pairs={{0,384},{32,416},{64,448},{96,480},{128,0},{160,32},{192,64},{224,... | collective-permute-start | bytes 1572872 | tf_op jit(solution)/shard_map/ppermute | solution.py:382
  53.5 3.3 %collective-permute-start.8 = (bf16[512,512]{1,0:T(8,128)(2,1)}, bf16[512,512]{1,0:T(8,128)(2,1)}, u32[]{:S(2)}, u32[]{:S(2)}) collective-permute-start(bf16[512,512]{1,0:T(8,128)(2,1)} %get-tuple-element.32.own), channel_id=1, source_target_pairs={{0,256},{32,288},{64,320},{96,352},{128,384},{160,416},{192,448},{... | collective-permute-start | bytes 1572872 | tf_op jit(solution)/shard_map/ppermute | solution.py:382
  56.9 0.6 fusion.1
  60.4 2.4 %shard_map.104 = (bf16[512,512]{1,0:T(8,128)(2,1)S(1)}, bf16[512,512]{1,0:T(8,128)(2,1)S(1)}, f32[512,512]{1,0:T(8,128)S(1)}) custom-call(s32[3]{0:T(128)S(1)} %add_add_fusion.place, bf16[512,512]{1,0:T(8,128)(2,1)S(1)} %bitcast.34, bf16[512,512]{1,0:T(8,128)(2,1)} %collective-permute-done.above, bf16[512,512]{1,0:T(8,128)(2,1)} %collective-permute-done.1.field_a, ...), custom_call_target="tpu_custom_call" | custom-call | flops 200000000 | bytes 3000000 | tf_op jit(solution)/shard_map/pallas_call | solution.py:71
  62.8 1.0 copy-done.6
  63.8 0.5 collective-permute-done.6.behind
  64.3 15.0 %collective-permute-done.7.ahead = bf16[512,512]{1,0:T(8,128)(2,1)} collective-permute-done((bf16[512,512]{1,0:T(8,128)(2,1)}, bf16[512,512]{1,0:T(8,128)(2,1)}, u32[]{:S(2)}, u32[]{:S(2)}) %collective-permute-start.7) | collective-permute-done | bytes 524320 | tf_op jit(solution)/shard_map/ppermute | solution.py:382
  79.3 6.7 %shard_map.106 = (bf16[512,512]{1,0:T(8,128)(2,1)}, bf16[512,512]{1,0:T(8,128)(2,1)S(1)}) custom-call(s32[3]{0:T(128)S(1)} %add_add_fusion.1.place, f32[3]{0:T(128)S(1)} %pad_maximum_fusion.tune, bf16[512,512]{1,0:T(8,128)(2,1)} %get-tuple-element.32.own, bf16[512,512]{1,0:T(8,128)(2,1)S(1)} %collective-permute-done.6.behind, ...), custom_call_target="tpu_custom_call" | custom-call | flops 200000000 | bytes 3000000 | tf_op jit(solution)/shard_map/pallas_call | solution.py:71
  86.1 1.9 %collective-permute-start.9 = (bf16[512,512]{1,0:T(8,128)(2,1)S(1)}, bf16[512,512]{1,0:T(8,128)(2,1)S(1)}, u32[]{:S(2)}, u32[]{:S(2)}) collective-permute-start(bf16[512,512]{1,0:T(8,128)(2,1)S(1)} %get-tuple-element.41.rest_1_.field), channel_id=1, source_target_pairs={{0,1},{1,0},{2,3},{3,2},{4,5},{5,4},{6,7},{7,6},{8,9},{9,8},{10,11... | collective-permute-start | bytes 1572872 | tf_op jit(solution)/shard_map/ppermute | solution.py:385
  88.0 0.7 collective-permute-start.10
  88.7 1.2 collective-permute-done.9.field_a
  89.8 1.0 copy-done
  90.9 1.4 shard_map.107
  92.3 1.1 shard_map.108.rest_2_.field
  93.3 8.6 %collective-permute-start.11 = (bf16[512,512]{1,0:T(8,128)(2,1)S(1)}, bf16[512,512]{1,0:T(8,128)(2,1)S(1)}, u32[]{:S(2)}, u32[]{:S(2)}) collective-permute-start(bf16[512,512]{1,0:T(8,128)(2,1)S(1)} %shard_map.108.rest_2_.field), channel_id=1, source_target_pairs={{0,1},{1,0},{2,3},{3,2},{4,5},{5,4},{6,7},{7,6},{8,9},{9,8},{10,11... | collective-permute-start | bytes 1572872 | tf_op jit(solution)/shard_map/ppermute | solution.py:385
  101.9 0.7 collective-permute-start.12
  102.7 0.8 collective-permute-done.11.field_a
  103.5 1.5 shard_map.109
  105.0 1.1 shard_map.110.rest_3_.field
  106.0 9.6 %collective-permute-start.13 = (bf16[512,512]{1,0:T(8,128)(2,1)S(1)}, bf16[512,512]{1,0:T(8,128)(2,1)S(1)}, u32[]{:S(2)}, u32[]{:S(2)}) collective-permute-start(bf16[512,512]{1,0:T(8,128)(2,1)S(1)} %shard_map.110.rest_3_.field), channel_id=1, source_target_pairs={{0,1},{1,0},{2,3},{3,2},{4,5},{5,4},{6,7},{7,6},{8,9},{9,8},{10,11... | collective-permute-start | bytes 1572872 | tf_op jit(solution)/shard_map/ppermute | solution.py:385
  115.6 0.9 collective-permute-start.14
  116.5 0.6 collective-permute-done.13.field_a
  117.1 1.6 shard_map.111
  118.7 1.1 shard_map.112
  119.8 9.4 %collective-permute-start.16 = (bf16[512,512]{1,0:T(8,128)(2,1)S(1)}, bf16[512,512]{1,0:T(8,128)(2,1)S(1)}, u32[]{:S(2)}, u32[]{:S(2)}) collective-permute-start(bf16[512,512]{1,0:T(8,128)(2,1)S(1)} %get-tuple-element.47.rest_4_.last), channel_id=1, source_target_pairs={{0,1},{1,0},{2,3},{3,2},{4,5},{5,4},{6,7},{7,6},{8,9},{9,8},{10,11... | collective-permute-start | bytes 1572872 | tf_op jit(solution)/shard_map/ppermute | solution.py:385
  129.2 0.7 collective-permute-start.15
  129.9 0.8 collective-permute-done.16.field_a
  130.7 1.6 shard_map.113
  132.8 33.1 %all_to_all.10 = f32[32,1,128]{2,1,0:T(1,128)S(1)} all-to-all(f32[32,1,128]{2,1,0:T(1,128)S(1)} %bitcast.40), channel_id=1, replica_groups=mesh['seg'=16,'op'=32] {'op'}, dimensions={0} | all-to-all | bytes 32768 | tf_op jit(solution)/shard_map/all_to_all | solution.py:388
  165.9 2.4 %shard_map.115 = (f32[512,512]{1,0:T(8,128)}, f32[1,128]{1,0:T(1,128)S(1)}) custom-call(f32[3]{0:T(128)S(1)} %pad_maximum_fusion.tune, f32[32,128]{1,0:T(8,128)S(1)} %bitcast.41, bf16[512,512]{1,0:T(8,128)(2,1)S(1)} %get-tuple-element.30.field.rest_0_, bf16[512,512]{1,0:T(8,128)(2,1)S(1)} %get-tuple-element.41.rest_1_.field, ...), custom_call_target="tpu_custom_call" | custom-call | flops 200000000 | bytes 3000000 | tf_op jit(solution)/shard_map/pallas_call | solution.py:71
  168.3 0.6 fusion
  (39 shorter events, 0.9 us)
Async XLA Ops:
  0.6 39.6 %collective-permute-start.3 = (bf16[512,512]{1,0:T(8,128)(2,1)}, bf16[512,512]{1,0:T(8,128)(2,1)}, u32[]{:S(2)}, u32[]{:S(2)}) collective-permute-start(bf16[512,512]{1,0:T(8,128)(2,1)} %bitcast.27), channel_id=1, source_target_pairs={{0,32},{32,64},{64,96},{96,0},{128,160},{160,192},{192,224},{224,1... | collective-permute-start | bytes 1572872 | tf_op jit(solution)/shard_map/ppermute | solution.py:382
  4.1 37.4 %collective-permute-start.4 = (bf16[512,512]{1,0:T(8,128)(2,1)}, bf16[512,512]{1,0:T(8,128)(2,1)}, u32[]{:S(2)}, u32[]{:S(2)}) collective-permute-start(bf16[512,512]{1,0:T(8,128)(2,1)} %bitcast.28), channel_id=1, source_target_pairs={{0,96},{32,0},{64,32},{96,64},{128,224},{160,128},{192,160},{224,1... | collective-permute-start | bytes 1572872 | tf_op jit(solution)/shard_map/ppermute | solution.py:382
  7.7 33.8 %collective-permute-start.5 = (bf16[512,512]{1,0:T(8,128)(2,1)}, bf16[512,512]{1,0:T(8,128)(2,1)}, u32[]{:S(2)}, u32[]{:S(2)}) collective-permute-start(bf16[512,512]{1,0:T(8,128)(2,1)} %bitcast.29), channel_id=1, source_target_pairs={{0,64},{32,96},{64,0},{96,32},{128,192},{160,224},{192,128},{224,1... | collective-permute-start | bytes 1572872 | tf_op jit(solution)/shard_map/ppermute | solution.py:382
  13.0 1.0 copy-start.4
  14.0 1.0 copy-start.5
  15.1 1.0 copy-start.7
  16.1 5.7 %copy-start.2 = (bf16[1,1,512,512]{3,2,1,0:T(8,128)(2,1)S(1)}, bf16[1,1,512,512]{3,2,1,0:T(8,128)(2,1)}, u32[]{:S(2)}) copy-start(bf16[1,1,512,512]{3,2,1,0:T(8,128)(2,1)} %param.9) | copy-start | bytes 1572868
  16.1 5.7 %copy-start.3 = (bf16[1,1,512,512]{3,2,1,0:T(8,128)(2,1)S(1)}, bf16[1,1,512,512]{3,2,1,0:T(8,128)(2,1)}, u32[]{:S(2)}) copy-start(bf16[1,1,512,512]{3,2,1,0:T(8,128)(2,1)} %param.11) | copy-start | bytes 1572868
  17.6 0.8 copy-start.8
  18.4 35.0 %collective-permute-start.1 = (bf16[512,512]{1,0:T(8,128)(2,1)S(1)}, bf16[512,512]{1,0:T(8,128)(2,1)}, u32[]{:S(2)}, u32[]{:S(2)}) collective-permute-start(bf16[512,512]{1,0:T(8,128)(2,1)S(1)} %get-tuple-element.30.field.rest_0_), channel_id=1, source_target_pairs={{0,1},{1,0},{2,3},{3,2},{4,5},{5,4},{6,7},{7,6},{8,9},{9,8},{10,11... | collective-permute-start | bytes 1572872 | tf_op jit(solution)/shard_map/ppermute | solution.py:385
  20.3 40.0 %collective-permute-start.2 = (bf16[512,512]{1,0:T(8,128)(2,1)S(1)}, bf16[512,512]{1,0:T(8,128)(2,1)}, u32[]{:S(2)}, u32[]{:S(2)}) collective-permute-start(bf16[512,512]{1,0:T(8,128)(2,1)S(1)} %get-tuple-element.30.field.rest_0_), channel_id=1, source_target_pairs={{1,2},{2,1},{3,4},{4,3},{5,6},{6,5},{7,8},{8,7},{9,10},{10,9},{11,... | collective-permute-start | bytes 1572872 | tf_op jit(solution)/shard_map/ppermute | solution.py:385
  23.5 33.4 %all-to-all-start = ((f32[32,1,128]{2,1,0:T(1,128)}), f32[32,1,128]{2,1,0:T(1,128)S(1)}, u32[]{:S(2)}, u32[]{:S(2)}) async-start(f32[32,1,128]{2,1,0:T(1,128)} %bitcast.5), calls=%async_computation | async-start | bytes 32768 | tf_op jit(solution)/shard_map/all_to_all | solution.py:388
  40.2 20.2 %collective-permute-start = (bf16[512,512]{1,0:T(8,128)(2,1)S(1)}, bf16[512,512]{1,0:T(8,128)(2,1)}, u32[]{:S(2)}, u32[]{:S(2)}) collective-permute-start(bf16[512,512]{1,0:T(8,128)(2,1)S(1)} %bitcast.33), channel_id=1, source_target_pairs={{1,0},{2,1},{3,2},{4,3},{5,4},{6,5},{7,6},{8,7},{9,8},{10,9},{11,1... | collective-permute-start | bytes 1572872 | tf_op jit(solution)/shard_map/ppermute | solution.py:385
  46.0 0.8 copy-start.10
  46.8 0.8 copy-start.12
  47.6 16.7 %collective-permute-start.6 = (bf16[512,512]{1,0:T(8,128)(2,1)}, bf16[512,512]{1,0:T(8,128)(2,1)S(1)}, u32[]{:S(2)}, u32[]{:S(2)}) collective-permute-start(bf16[512,512]{1,0:T(8,128)(2,1)} %get-tuple-element.32.own), channel_id=1, source_target_pairs={{0,128},{32,160},{64,192},{96,224},{128,256},{160,288},{192,320},{... | collective-permute-start | bytes 1572872 | tf_op jit(solution)/shard_map/ppermute | solution.py:382
  50.0 29.3 %collective-permute-start.7 = (bf16[512,512]{1,0:T(8,128)(2,1)}, bf16[512,512]{1,0:T(8,128)(2,1)}, u32[]{:S(2)}, u32[]{:S(2)}) collective-permute-start(bf16[512,512]{1,0:T(8,128)(2,1)} %get-tuple-element.32.own), channel_id=1, source_target_pairs={{0,384},{32,416},{64,448},{96,480},{128,0},{160,32},{192,64},{224,... | collective-permute-start | bytes 1572872 | tf_op jit(solution)/shard_map/ppermute | solution.py:382
  53.5 25.9 %collective-permute-start.8 = (bf16[512,512]{1,0:T(8,128)(2,1)}, bf16[512,512]{1,0:T(8,128)(2,1)}, u32[]{:S(2)}, u32[]{:S(2)}) collective-permute-start(bf16[512,512]{1,0:T(8,128)(2,1)} %get-tuple-element.32.own), channel_id=1, source_target_pairs={{0,256},{32,288},{64,320},{96,352},{128,384},{160,416},{192,448},{... | collective-permute-start | bytes 1572872 | tf_op jit(solution)/shard_map/ppermute | solution.py:382
  60.4 18.9 %copy-start.9 = (bf16[512,512]{1,0:T(8,128)(2,1)S(1)}, bf16[512,512]{1,0:T(8,128)(2,1)}, u32[]{:S(2)}) copy-start(bf16[512,512]{1,0:T(8,128)(2,1)} %copy-done.8) | copy-start | bytes 1572868
  60.4 18.9 %copy-start.11 = (bf16[512,512]{1,0:T(8,128)(2,1)S(1)}, bf16[512,512]{1,0:T(8,128)(2,1)}, u32[]{:S(2)}) copy-start(bf16[512,512]{1,0:T(8,128)(2,1)} %copy-done.10) | copy-start | bytes 1572868
  60.4 18.9 %copy-start.13 = (bf16[512,512]{1,0:T(8,128)(2,1)S(1)}, bf16[512,512]{1,0:T(8,128)(2,1)}, u32[]{:S(2)}) copy-start(bf16[512,512]{1,0:T(8,128)(2,1)} %copy-done.12) | copy-start | bytes 1572868
  62.8 1.0 copy-start.6
  86.1 3.8 %collective-permute-start.9 = (bf16[512,512]{1,0:T(8,128)(2,1)S(1)}, bf16[512,512]{1,0:T(8,128)(2,1)S(1)}, u32[]{:S(2)}, u32[]{:S(2)}) collective-permute-start(bf16[512,512]{1,0:T(8,128)(2,1)S(1)} %get-tuple-element.41.rest_1_.field), channel_id=1, source_target_pairs={{0,1},{1,0},{2,3},{3,2},{4,5},{5,4},{6,7},{7,6},{8,9},{9,8},{10,11... | collective-permute-start | bytes 1572872 | tf_op jit(solution)/shard_map/ppermute | solution.py:385
  88.0 4.3 %collective-permute-start.10 = (bf16[512,512]{1,0:T(8,128)(2,1)S(1)}, bf16[512,512]{1,0:T(8,128)(2,1)S(1)}, u32[]{:S(2)}, u32[]{:S(2)}) collective-permute-start(bf16[512,512]{1,0:T(8,128)(2,1)S(1)} %get-tuple-element.41.rest_1_.field), channel_id=1, source_target_pairs={{1,2},{2,1},{3,4},{4,3},{5,6},{6,5},{7,8},{8,7},{9,10},{10,9},{11,... | collective-permute-start | bytes 1572872 | tf_op jit(solution)/shard_map/ppermute | solution.py:385
  89.8 1.0 copy-start
  92.3 11.2 %copy-start.1 = (bf16[512,512]{1,0:T(8,128)(2,1)S(1)}, bf16[512,512]{1,0:T(8,128)(2,1)}, u32[]{:S(2)}) copy-start(bf16[512,512]{1,0:T(8,128)(2,1)} %get-tuple-element.38.left) | copy-start | bytes 1572868
  93.3 10.1 %collective-permute-start.11 = (bf16[512,512]{1,0:T(8,128)(2,1)S(1)}, bf16[512,512]{1,0:T(8,128)(2,1)S(1)}, u32[]{:S(2)}, u32[]{:S(2)}) collective-permute-start(bf16[512,512]{1,0:T(8,128)(2,1)S(1)} %shard_map.108.rest_2_.field), channel_id=1, source_target_pairs={{0,1},{1,0},{2,3},{3,2},{4,5},{5,4},{6,7},{7,6},{8,9},{9,8},{10,11... | collective-permute-start | bytes 1572872 | tf_op jit(solution)/shard_map/ppermute | solution.py:385
  101.9 3.0 %collective-permute-start.12 = (bf16[512,512]{1,0:T(8,128)(2,1)S(1)}, bf16[512,512]{1,0:T(8,128)(2,1)S(1)}, u32[]{:S(2)}, u32[]{:S(2)}) collective-permute-start(bf16[512,512]{1,0:T(8,128)(2,1)S(1)} %shard_map.108.rest_2_.field), channel_id=1, source_target_pairs={{1,2},{2,1},{3,4},{4,3},{5,6},{6,5},{7,8},{8,7},{9,10},{10,9},{11,... | collective-permute-start | bytes 1572872 | tf_op jit(solution)/shard_map/ppermute | solution.py:385
  106.0 11.1 %collective-permute-start.13 = (bf16[512,512]{1,0:T(8,128)(2,1)S(1)}, bf16[512,512]{1,0:T(8,128)(2,1)S(1)}, u32[]{:S(2)}, u32[]{:S(2)}) collective-permute-start(bf16[512,512]{1,0:T(8,128)(2,1)S(1)} %shard_map.110.rest_3_.field), channel_id=1, source_target_pairs={{0,1},{1,0},{2,3},{3,2},{4,5},{5,4},{6,7},{7,6},{8,9},{9,8},{10,11... | collective-permute-start | bytes 1572872 | tf_op jit(solution)/shard_map/ppermute | solution.py:385
  115.6 3.1 %collective-permute-start.14 = (bf16[512,512]{1,0:T(8,128)(2,1)S(1)}, bf16[512,512]{1,0:T(8,128)(2,1)S(1)}, u32[]{:S(2)}, u32[]{:S(2)}) collective-permute-start(bf16[512,512]{1,0:T(8,128)(2,1)S(1)} %shard_map.110.rest_3_.field), channel_id=1, source_target_pairs={{1,2},{2,1},{3,4},{4,3},{5,6},{6,5},{7,8},{8,7},{9,10},{10,9},{11,... | collective-permute-start | bytes 1572872 | tf_op jit(solution)/shard_map/ppermute | solution.py:385
  119.8 10.9 %collective-permute-start.16 = (bf16[512,512]{1,0:T(8,128)(2,1)S(1)}, bf16[512,512]{1,0:T(8,128)(2,1)S(1)}, u32[]{:S(2)}, u32[]{:S(2)}) collective-permute-start(bf16[512,512]{1,0:T(8,128)(2,1)S(1)} %get-tuple-element.47.rest_4_.last), channel_id=1, source_target_pairs={{0,1},{1,0},{2,3},{3,2},{4,5},{5,4},{6,7},{7,6},{8,9},{9,8},{10,11... | collective-permute-start | bytes 1572872 | tf_op jit(solution)/shard_map/ppermute | solution.py:385
  129.2 3.2 %collective-permute-start.15 = (bf16[512,256]{1,0:T(8,128)(2,1)S(1)}, bf16[512,256]{1,0:T(8,128)(2,1)S(1)}, u32[]{:S(2)}, u32[]{:S(2)}) collective-permute-start(bf16[512,256]{1,0:T(8,128)(2,1)S(1)} %get-tuple-element.45), channel_id=1, source_target_pairs={{1,2},{2,1},{3,4},{4,3},{5,6},{6,5},{7,8},{8,7},{9,10},{10,9},{11,... | collective-permute-start | bytes 786440 | tf_op jit(solution)/shard_map/ppermute | solution.py:385

commit v2 on v1

v2 whole, which is shorter than its diff:
```python
import functools

import jax
import jax.numpy as jnp
from jax import lax
from jax.experimental import pallas as pl
from jax.experimental.pallas import tpu as pltpu
from jax.sharding import PartitionSpec as P

DAVIDSON = 4
ROW = 4
LANES = 128
STEP = 256
BAND = 32
SHIFT = 2.0
GRANT = 52
epsilon = 1e-06

f32, bf16 = jnp.float32, jnp.bfloat16
VMEM = pl.BlockSpec(memory_space=pltpu.VMEM)
SMEM = pl.BlockSpec(memory_space=pltpu.SMEM)
LOOSE = pl.BlockSpec(memory_space=pl.ANY)
HBM = pl.BlockSpec(memory_space=pltpu.HBM)
DMA = pltpu.SemaphoreType.DMA


def wide_dot(a, b):
    return jnp.dot(a, b, preferred_element_type=f32)


def left_transposed_dot(a, b):
    return lax.dot_general(a, b, (((0,), (0,)), ((), ())), preferred_element_type=f32)


def split(x):
    high = x.astype(bf16)
    return high, (x - high.astype(f32)).astype(bf16)


def total(x):
    return jnp.sum(jnp.sum(x, axis=0, keepdims=True), axis=1, keepdims=True)


def in_lanes(first, values):
    lane = lax.broadcasted_iota(jnp.int32, (1, LANES), 1)
    out = jnp.zeros((1, LANES), f32)
    for i, value in enumerate(values):
        out = jnp.where(lane == first + i, value, out)
    return out


def live(start, rows, cols, sizes):
    row = lax.broadcasted_iota(jnp.int32, (rows, cols), 0) + start
    col = lax.broadcasted_iota(jnp.int32, (rows, cols), 1)
    return (row < sizes[0]) & (col < sizes[1])


def banded_dots(fields, last):
    n, cols = last.shape

    def band(i, sums):
        at = pl.ds(pl.multiple_of(i * BAND, BAND), BAND)
        mine = last[at, :].astype(f32)
        return tuple(
            s + jnp.sum((f[at, :].astype(f32) * mine).reshape(BAND // 8, 8, cols), axis=0)
            for s, f in zip(sums, fields, strict=True)
        )

    sums = lax.fori_loop(0, n // BAND, band, tuple(jnp.zeros((8, cols), f32) for _ in fields))
    return [total(s) for s in sums]


def call(kernel, out, smem=1, loose=0, far=0, scratch=(), out_specs=None, grant=20):
    def run(*args):
        return pl.pallas_call(
            kernel,
            out_shape=out,
            in_specs=[SMEM] * smem
            + [VMEM] * (len(args) - smem - loose - far)
            + [LOOSE] * loose
            + [HBM] * far,
            out_specs=jax.tree.map(lambda _: VMEM, out) if out_specs is None else out_specs,
            scratch_shapes=list(scratch),
            cost_estimate=pl.CostEstimate(
                flops=1, bytes_accessed=1, transcendentals=0
            ),
            compiler_params=pltpu.CompilerParams(vmem_limit_bytes=grant * 1024 * 1024),
        )(*args)

    return run


def survey(transfer, edge, right, coupling):
    n = transfer.shape[0]
    (grown,), (edge_sq,), (right_sq,), (coupling_sq,) = (
        banded_dots([x], x) for x in (transfer, edge, right, coupling)
    )
    edge_trace = right_trace = jnp.zeros((1, 1), f32)
    for c in range(0, n, LANES):
        diagonal = lax.broadcasted_iota(jnp.int32, (LANES, LANES), 0) == lax.broadcasted_iota(
            jnp.int32, (LANES, LANES), 1
        )
        at = slice(c, c + LANES)
        edge_trace += total(jnp.where(diagonal, edge[at, at].astype(f32), 0.0))
        right_trace += total(jnp.where(diagonal, right[at, at].astype(f32), 0.0))
    values = (
        grown / n,
        jnp.sqrt(edge_sq / n) * jnp.sqrt(right_sq / n),
        coupling_sq / n,
        edge_trace / n * (right_trace / n),
    )
    return in_lanes(0, values)


def prepare_kernel(
    place, transfer, theta, edge, right, coupling,
    transfer_out, field_out, right_out, stats, found, bundle_far, edge_far, lifted_far,
    bundle, edge_out, lifted, sems,
):
    n = theta.shape[0]
    sizes = (place[1], place[2])
    moves = [
        pltpu.make_async_copy(*pair, sems.at[i])
        for i, pair in enumerate(((bundle, bundle_far), (edge_out, edge_far), (lifted, lifted_far)))
    ]
    for c in range(0, n, STEP):
        at = slice(c, c + STEP)
        kept = jnp.where(live(c, STEP, n, sizes), theta[at, :].astype(f32), 0.0).astype(bf16)
        field_out[at, :] = kept
        bundle[n + c : n + c + STEP, :] = kept
        bundle[at, :] = coupling[at, :]
    moves[0].start()
    for source, out in ((edge, edge_out), (right, right_out)):
        for c in range(0, n, STEP):
            turned = source[:, c : c + STEP].astype(f32).T
            out[c : c + STEP, :] = (0.5 * (source[c : c + STEP, :].astype(f32) + turned)).astype(
                out.dtype
            )
    moves[1].start()
    for c in range(0, n, STEP):
        lifted[c : c + STEP, :] = wide_dot(field_out[c : c + STEP, :], right_out[...]).astype(bf16)
    moves[2].start()
    transfer_out[...] = transfer[...]
    stats[...] = in_lanes(0, banded_dots([field_out], field_out))
    found[...] = survey(transfer, edge, right, coupling)
    for move in moves:
        move.wait()


def spread_kernel(found, after, out):
    out[...] = jnp.broadcast_to(found[...], out.shape)


def lane_entry(row, i):
    lane = lax.broadcasted_iota(jnp.int32, (1, LANES), 1)
    return jnp.sum(jnp.where(lane == i, row, 0.0), axis=1, keepdims=True)


def tuning(place, found):
    row = jnp.sum(found[...], axis=0, keepdims=True) / found.shape[0]
    grown, size, coupling_sq, trace = (lane_entry(row, i) for i in range(4))
    segment = (place[3] * ROW + place[4]).astype(f32)
    growth = jnp.exp(jnp.clip(segment * jnp.log(jnp.maximum(grown, 1e-30)), -30.0, 30.0))
    scale = size * growth + 2.0 * jnp.sqrt(coupling_sq) + 1e-12
    return in_lanes(0, (SHIFT * trace * growth, 1.0 / scale, scale))


def couple_kernel(place, coupling, bundle, below, near, far, image_far, image, sem):
    n = coupling.shape[0]
    odd = place[0] == 1

    def write(own, turned):
        own[...] = coupling[...]
        for c in range(0, n, STEP):
            turned[c : c + STEP, :] = bundle[:n, c : c + STEP].astype(f32).T.astype(bf16)
        for c in range(0, n, STEP):
            at = slice(c, c + STEP)
            image[at, :] = wide_dot(own[at, :], below[...]) + wide_dot(turned[at, :], bundle[n:, :])

    @pl.when(odd)
    def _():
        write(near, far)

    @pl.when(jnp.logical_not(odd))
    def _():
        write(far, near)

    move = pltpu.make_async_copy(image, image_far, sem)
    move.start()
    move.wait()


def identity_rows(start, rows, cols):
    row = lax.broadcasted_iota(jnp.int32, (rows, cols), 0) + start
    col = lax.broadcasted_iota(jnp.int32, (rows, cols), 1)
    return jnp.where(row == col, 1.0, 0.0)


def pair_kernel(place, own, got, high, low):
    n = own.shape[0]

    def write(first, second):
        for c in range(0, n, STEP):
            at = slice(c, c + STEP)
            product = wide_dot(first[at, :], second[...]) - identity_rows(c, STEP, n)
            high[at, :], low[at, :] = split(product)

    @pl.when(lax.rem(place[4], 2) == 0)
    def _():
        write(own, got)

    @pl.when(lax.rem(place[4], 2) == 1)
    def _():
        write(got, own)


def chain(first, second, c):
    at = slice(c, c + STEP)
    out = sum(x[at, :].astype(f32) for x in first) + sum(x[at, :].astype(f32) for x in second)
    for x in first:
        for y in second:
            out = out + wide_dot(x[at, :], y[...])
    return out


def join_kernel(which, place, own_high, own_low, got, *rest):
    n = got.shape[0]
    outs = rest[-2:] if which == 4 else rest[-1:]
    own = (own_high, own_low)
    leads = place[4] < ROW // 2 if which == 4 else lax.rem(place[3], 2) == 0

    def write(first, second):
        for c in range(0, n, STEP):
            at = slice(c, c + STEP)
            for out, part in zip(outs, split(chain(first, second, c)), strict=False):
                out[at, :] = part

    @pl.when(leads)
    def _():
        write(own, (got,))

    @pl.when(jnp.logical_not(leads))
    def _():
        write((got,), own)


def row_prefix_kernel(place, transfer_got, pair_got, high, low):
    y = place[4]
    n = transfer_got.shape[0]

    @pl.when(y == 0)
    def _():
        high[...] = jnp.zeros((n, n), bf16)
        low[...] = jnp.zeros((n, n), bf16)

    @pl.when(y == 2)
    def _():
        high[...] = pair_got[...]
        low[...] = jnp.zeros((n, n), bf16)

    @pl.when(y == 1)
    def _():
        for c in range(0, n, STEP):
            at = slice(c, c + STEP)
            alone = transfer_got[at, :].astype(f32) - identity_rows(c, STEP, n)
            high[at, :], low[at, :] = split(alone)

    @pl.when(y == 3)
    def _():
        for c in range(0, n, STEP):
            at = slice(c, c + STEP)
            alone = transfer_got[at, :].astype(f32) - identity_rows(c, STEP, n)
            high[at, :], low[at, :] = split(alone + wide_dot(pair_got[at, :], transfer_got[...]))


def segment_prefix_kernel(
    place, whole_got, row_high, row_low, high_far, low_far, high, low, sems
):
    n = whole_got.shape[0]

    @pl.when(lax.rem(place[3], 2) == 0)
    def _():
        high[...] = row_high[...]
        low[...] = row_low[...]

    @pl.when(lax.rem(place[3], 2) == 1)
    def _():
        for c in range(0, n, STEP):
            at = slice(c, c + STEP)
            high[at, :], low[at, :] = split(chain((whole_got,), (row_high, row_low), c))

    moves = [
        pltpu.make_async_copy(high, high_far, sems.at[0]),
        pltpu.make_async_copy(low, low_far, sems.at[1]),
    ]
    for move in moves:
        move.start()
    for move in moves:
        move.wait()


def segment_kernel(
    place, ahead, found, field, high_far, low_far, edge_far, couplings_far, lifted_far,
    left, left_out, next_field, tune,
    high, low, edge, couplings, lifted, prefix, turned, turned_wide, sems,
):
    sizes = (place[1], place[2])
    n = ahead.shape[0]
    pairs = (
        (high_far, high), (low_far, low), (edge_far, edge),
        (lifted_far, lifted), (couplings_far, couplings),
    )
    moves = [pltpu.make_async_copy(*pair, sems.at[i]) for i, pair in enumerate(pairs)]
    for move in moves:
        move.start()
    tuned = tuning(place, found)
    tune[...] = tuned
    shift, gain = lane_entry(tuned, 0), lane_entry(tuned, 1)
    moves[0].wait()
    moves[1].wait()

    @pl.when(place[3] < ROW // 2)
    def _():
        prefix[...] = high[...]

    @pl.when(place[3] >= ROW // 2)
    def _():
        for c in range(0, n, STEP):
            prefix[c : c + STEP, :] = chain((ahead,), (high, low), c).astype(bf16)

    moves[2].wait()
    for c in range(0, n, STEP):
        at = slice(c, c + STEP)
        value = edge[at, :] + wide_dot(edge[at, :].astype(bf16), prefix[...])
        turned_wide[at, :] = value
        turned[at, :] = value.astype(bf16)
    for c in range(0, n, STEP):
        at = slice(c, c + STEP)
        block = turned_wide[at, :] + left_transposed_dot(prefix[:, at], turned[...])
        left[at, :] = block.astype(bf16)
        left_out[at, :] = block.astype(bf16)
    moves[3].wait()
    moves[4].wait()
    for c in range(0, n, STEP):
        at = slice(c, c + STEP)
        image = wide_dot(left[at, :], lifted[...]) + couplings[at, :]
        moved = (image - shift * field[at, :].astype(f32)) * gain
        next_field[at, :] = jnp.where(live(c, STEP, n, sizes), moved, 0.0).astype(bf16)


def local_kernel(count, left, right, *rest):
    fields, (partial, stats) = rest[:count], rest[count:]
    field = fields[-1]
    n = field.shape[0]
    for c in range(0, n, STEP):
        at = slice(c, c + STEP)
        middle = wide_dot(left[at, :], field[...]).astype(bf16)
        partial[at, :] = wide_dot(middle, right[...])
    k = count - 1
    stats[...] = in_lanes(k * (k + 1) // 2, banded_dots(list(fields), field))


def near_last_kernel(near, field_a, partial, last, out):
    n = near.shape[0]
    inner = jnp.zeros((1, 1), f32)
    for c in range(0, n, STEP):
        at = slice(c, c + STEP)
        image = partial[at, :] + wide_dot(near[at, :], field_a[...])
        inner += total(image * last[at, :].astype(f32))
    k = DAVIDSON + 1
    out[...] = in_lanes(k * (k + 1) // 2, [inner])


def far_kernel(partial, far, field_b, out):
    n = far.shape[0]
    for c in range(0, n, STEP):
        at = slice(c, c + STEP)
        out[at, :] = partial[at, :] + wide_dot(far[at, :], field_b[...])


def advance_kernel(place, tune, partial, near, field_a, field, next_field):
    sizes = (place[1], place[2])
    n = field.shape[0]
    shift, gain = lane_entry(tune[...], 0), lane_entry(tune[...], 1)
    for c in range(0, n, STEP):
        at = slice(c, c + STEP)
        image = partial[at, :] + wide_dot(near[at, :], field_a[...])
        moved = (image - shift * field[at, :].astype(f32)) * gain
        next_field[at, :] = jnp.where(live(c, STEP, n, sizes), moved, 0.0).astype(bf16)


def advance_last_kernel(place, tune, partial, near, field_a, field, next_field, sent, kept):
    advance_kernel(place, tune, partial, near, field_a, field, next_field)
    half = field.shape[1] // 2

    @pl.when(place[0] == 1)
    def _():
        sent[...] = next_field[:, :half]
        kept[...] = next_field[:, half:]

    @pl.when(place[0] != 1)
    def _():
        sent[...] = next_field[:, half:]
        kept[...] = next_field[:, :half]


def close_kernel(far, got, kept, *rest):
    stats_in, out = rest[:-1], rest[-1]
    n = far.shape[0]
    inner = jnp.zeros((1, 1), f32)
    for c in range(0, n, STEP):
        at = slice(c, c + STEP)
        inner += total(wide_dot(far[at, :], got[...]) * kept[at, :].astype(f32))
    k = DAVIDSON + 1
    sums = in_lanes(k * (k + 1) // 2, [2.0 * inner])
    for piece in stats_in:
        sums += piece[...]
    out[...] = jnp.broadcast_to(sums, out.shape)


def solve_kernel(tune, sums, *rest):
    size = DAVIDSON + 1
    fields, (vector, last_energy, first_energy) = rest[:size], rest[size:]
    shift, scale = lane_entry(tune[...], 0), lane_entry(tune[...], 2)
    row = jnp.sum(sums[...], axis=0, keepdims=True)
    entry = functools.partial(lane_entry, row)
    gram = {}
    for k in range(size):
        for j in range(k + 1):
            gram[j, k] = gram[k, j] = entry(k * (k + 1) // 2 + j)
    image_gram = {}
    for j in range(size):
        for k in range(j, size):
            if j < size - 1:
                value = scale * gram[j + 1, k] + shift * gram[j, k]
            else:
                value = entry(size * (size + 1) // 2)
            image_gram[j, k] = image_gram[k, j] = value

    def form(table, a, b):
        out = jnp.zeros((1, 1), f32)
        for j, aj in enumerate(a):
            if aj is None:
                continue
            inner = jnp.zeros((1, 1), f32)
            for k, bk in enumerate(b):
                if bk is not None:
                    inner = inner + table[j, k] * bk
            out = out + aj * inner
        return out

    weights = [1.0 / jnp.sqrt(gram[0, 0] + epsilon)] + [None] * (size - 1)
    energy = first = form(image_gram, weights, weights)
    for step in range(DAVIDSON):
        turn = [None] * size
        for k in range(step + 2):
            value = None
            if weights[k] is not None:
                value = (shift - energy) * weights[k]
            if k > 0 and weights[k - 1] is not None:
                carried = scale * weights[k - 1]
                value = carried if value is None else value + carried
            turn[k] = value
        corr_norm = jnp.maximum(form(gram, turn, turn), 0.0)
        cross_term = form(image_gram, weights, turn)
        curv_term = form(image_gram, turn, turn)
        scale_norm = jnp.sqrt(corr_norm + epsilon)
        offdiag = cross_term / scale_norm
        diag_value = curv_term / (corr_norm + epsilon)
        half_gap = (diag_value - energy) / 2
        lowest = (energy + diag_value) / 2 - jnp.sqrt(half_gap * half_gap + offdiag * offdiag)
        rotation = lowest - energy
        radius = jnp.sqrt(offdiag * offdiag + rotation * rotation + epsilon)
        keep, add = offdiag / radius, rotation / scale_norm / radius
        weights = [
            None
            if t is None
            else add * t if w is None else keep * w + add * t
            for w, t in zip(weights, turn, strict=True)
        ]
        energy = lowest
    last_energy[0] = energy[0, 0]
    first_energy[0] = first[0, 0]
    n = vector.shape[0]

    def band(i, carry):
        at = pl.ds(pl.multiple_of(i * BAND, BAND), BAND)
        out = weights[0] * fields[0][at, :].astype(f32)
        for w, field in zip(weights[1:], fields[1:], strict=True):
            out = out + w * field[at, :].astype(f32)
        vector[at, :] = out
        return carry

    lax.fori_loop(0, n // BAND, band, 0)


def on_device(theta, left_edge, transfer, right_env, coupling, left_sizes, right_sizes):
    n = theta.shape[-1]
    theta, left_edge = theta[0, 0], left_edge[0]
    transfer, right_env, coupling = transfer[0, 0], right_env[0, 0], coupling[0, 0]
    seg, op = lax.axis_index("seg"), lax.axis_index("op")
    segments, sectors = lax.axis_size("seg"), lax.axis_size("op")
    y_pair = [(s, s ^ 1) for s in range(segments)]
    y_turn = [(s, s - s % ROW + ROW - 1 - s % ROW) for s in range(segments)]
    x_pair = [(s, s ^ ROW) for s in range(segments)]
    x_turn = [(s, s % ROW + ROW * (ROW - 1 - s // ROW)) for s in range(segments // 2)]
    near_swap = [(i, i ^ 1) for i in range(sectors)]
    far_swap = [(i, i + 1 if i % 2 else i - 1) for i in range(1, sectors - 1)]
    down = [(i + 1, i) for i in range(sectors - 1)]
    up = [(i, i + 1) for i in range(sectors - 1)]
    square, wide = jax.ShapeDtypeStruct((n, n), bf16), jax.ShapeDtypeStruct((n, n), f32)
    tall, double = (jax.ShapeDtypeStruct(d, bf16) for d in ((n, n // 2), (2 * n, n)))
    lanes = jax.ShapeDtypeStruct((1, LANES), f32)
    spread = jax.ShapeDtypeStruct((sectors, LANES), f32)
    number = jax.ShapeDtypeStruct((1,), f32)
    buffer = lambda rows, cols, kind=bf16: pltpu.VMEM((rows, cols), kind)
    place = jnp.stack([op % 2, left_sizes[0], right_sizes[0], seg // ROW, seg % ROW])

    def seg_send(x, route):
        return lax.ppermute(x, "seg", route)

    def op_send(x, route):
        return lax.ppermute(x, "op", route)

    def op_sum(x):
        return lax.all_to_all(x[:, None], "op", 0, 0)[:, 0]

    transfer_got = seg_send(transfer, y_pair)
    held, field, right, stats, found, bundle, edge_sym, lifted = call(
        prepare_kernel,
        (square, square, square, lanes, lanes, double, wide, square),
        out_specs=(VMEM,) * 5 + (HBM,) * 3,
        grant=GRANT,
        scratch=[buffer(2 * n, n), buffer(n, n, f32), buffer(n, n), DMA((3,))],
    )(place, transfer, theta, left_edge, right_env, coupling)
    bundle_got = op_send(bundle, down)
    below = op_send(field, up)

    pair_high, pair_low = call(pair_kernel, (square, square))(place, held, transfer_got)
    pair_got = seg_send(pair_high, y_turn)
    near, far, couplings = call(
        couple_kernel,
        (square, square, wide),
        out_specs=(VMEM, VMEM, HBM),
        grant=GRANT,
        scratch=[buffer(n, n, f32), DMA],
    )(
        place, coupling, bundle_got, below
    )
    whole_high, whole_low = call(functools.partial(join_kernel, 4), (square, square))(
        place, pair_high, pair_low, pair_got
    )
    whole_got = seg_send(whole_high, x_pair)
    row_high, row_low = call(row_prefix_kernel, (square, square))(place, transfer_got, pair_got)
    (double_high,) = call(functools.partial(join_kernel, 3), (square,), loose=2)(
        place, whole_high, whole_low, whole_got, near, row_high
    )
    ahead = seg_send(double_high, x_turn)
    high, low = call(
        segment_prefix_kernel,
        (square, square),
        out_specs=(HBM, HBM),
        grant=GRANT,
        scratch=[buffer(n, n), buffer(n, n), DMA((2,))],
    )(place, whole_got, row_high, row_low)
    found = call(spread_kernel, spread, smem=0, loose=1)(found, double_high)
    left, left_out, following, tune = call(
        segment_kernel,
        (square, square, square, lanes),
        far=5,
        grant=GRANT,
        scratch=[
            *[buffer(n, n)] * 2, *[buffer(n, n, f32)] * 2, *[buffer(n, n)] * 3,
            buffer(n, n, f32), DMA((5,)),
        ],
    )(place, ahead, op_sum(found), field, high, low, edge_sym, couplings, lifted)
    fields, pieces = [field, following], [stats]
    sent = kept = None
    for k in range(1, DAVIDSON + 1):
        last = k == DAVIDSON
        newest = fields[-1]
        field_a = op_send(newest, near_swap)
        field_b = op_send(sent if last else newest, far_swap)
        partial, stats = call(functools.partial(local_kernel, k + 1), (wide, lanes), smem=0)(
            left, right, *fields
        )
        pieces.append(stats)
        if last:
            pieces.append(call(near_last_kernel, lanes, smem=0)(near, field_a, partial, newest))
            sums = call(close_kernel, spread, smem=0)(far, field_b, kept, *pieces)
            break
        partial = call(far_kernel, wide, smem=0)(partial, far, field_b)
        if k == DAVIDSON - 1:
            following, sent, kept = call(advance_last_kernel, (square, tall, tall))(
                place, tune, partial, near, field_a, newest
            )
        else:
            following = call(advance_kernel, square)(place, tune, partial, near, field_a, newest)
        fields.append(following)
    sums = op_sum(sums)
    vector, energy, first = call(
        solve_kernel, (wide, number, number), smem=0, out_specs=(VMEM, SMEM, SMEM)
    )(tune, sums, *fields)
    return vector[None, None], left_out[None, None], energy, first


def solution(mesh):
    placed = (
        P("seg", "op", None, None),
        P("op", None, None),
        P("seg", "op", None, None),
        P("seg", "op", None, None),
        P("seg", "op", None, None),
        P("op"),
        P("op"),
    )
    return jax.shard_map(
        on_device,
        mesh=mesh,
        in_specs=placed,
        out_specs=(P("seg", "op", None, None), P("seg", "op", None, None), P("seg"), P("seg")),
        check_vma=False,
    )
```

time: 170 us -> 157 us (0.924)
  the two profiles are of different devices: /device:TPU:6 before, /device:TPU:1 now
where the time goes in v2:
time: 157 us; the launch traced here: 156 us
  starting transfers between devices  68.3 us (44%)
  waiting for transfers between devices  32.7 us (21%)
  Pallas kernels  30.1 us (19%)
  blocking collectives  19.9 us (13%)
  local copies, waits for them, and re-layouts  2.67 us (2%)
  between operations  2.47 us (2%)
    pallas_call x22, Pallas kernels, run(): pl.pallas_call(kernel, out_shape=out, in_specs=[SMEM] * smem + [VMEM] * (...  30.1 us
    ppermute x10, starting transfers between devices, op_send(): return lax.ppermute(x, 'op', route)  27.1 us
    ppermute x4, starting transfers between devices, seg_send(): return lax.ppermute(x, 'seg', route)  22.3 us
    all_to_all x1, blocking collectives, op_sum(): return lax.all_to_all(x[:, None], 'op', 0, 0)[:, 0]  19.9 us
    all_to_all x1, starting transfers between devices, op_sum(): return lax.all_to_all(x[:, None], 'op', 0, 0)[:, 0]  18.8 us
    ppermute x10, waiting for transfers between devices, op_send(): return lax.ppermute(x, 'op', route)  17.4 us
    all_to_all x1, waiting for transfers between devices, op_sum(): return lax.all_to_all(x[:, None], 'op', 0, 0)[:, 0]  8.73 us
    ppermute x4, waiting for transfers between devices, seg_send(): return lax.ppermute(x, 'seg', route)  6.62 us
  transfers between devices with their start and end apart: 15, of which 9 were waited for; matrix products, arithmetic and copies ran while one was open for 0% of the time, Pallas kernels for 12%

profile of v2, /device:TPU:1, one launch (start us, length us, event | category | flops | bytes accessed | tf_op | source)
XLA Modules:
  0.0 156.1 jit_solution(18203341677742077120)
XLA Ops:
  0.6 4.0 %collective-permute-start = (bf16[512,512]{1,0:T(8,128)(2,1)}, bf16[512,512]{1,0:T(8,128)(2,1)S(1)}, u32[]{:S(2)}, u32[]{:S(2)}) collective-permute-start(bf16[512,512]{1,0:T(8,128)(2,1)} %bitcast.26), channel_id=1, source_target_pairs={{0,32},{32,0},{64,96},{96,64},{128,160},{160,128},{192,224},{224,1... | collective-permute-start | bytes 1572872 | tf_op jit(solution)/shard_map/ppermute | solution.py:520
  6.1 3.9 %shard_map.102 = (bf16[512,512]{1,0:T(8,128)(2,1)S(1)}, bf16[512,512]{1,0:T(8,128)(2,1)S(1)}, bf16[512,512]{1,0:T(8,128)(2,1)S(1)}, f32[1,128]{1,0:T(1,128)S(1)}...) custom-call(s32[5]{0:T(128)S(1)} %stack.15.place, ...), custom_call_target="tpu_custom_call" | custom-call | flops 1 | bytes 1 | tf_op jit(solution)/shard_map/pallas_call | solution.py:75
  10.0 1.7 %collective-permute-done.got.transfer_got = bf16[512,512]{1,0:T(8,128)(2,1)S(1)} collective-permute-done((bf16[512,512]{1,0:T(8,128)(2,1)}, bf16[512,512]{1,0:T(8,128)(2,1)S(1)}, u32[]{:S(2)}, u32[]{:S(2)}) %collective-permute-start) | collective-permute-done | bytes 524320 | tf_op jit(solution)/shard_map/ppermute | solution.py:520
  11.7 1.0 shard_map.103
  12.7 9.3 %collective-permute-start.1 = (bf16[512,512]{1,0:T(8,128)(2,1)S(1)}, bf16[512,512]{1,0:T(8,128)(2,1)S(1)}, u32[]{:S(2)}, u32[]{:S(2)}) collective-permute-start(bf16[512,512]{1,0:T(8,128)(2,1)S(1)} %get-tuple-element.42.own_high), channel_id=1, source_target_pairs={{0,96},{32,64},{64,32},{96,0},{128,224},{160,192},{192,160},{224,1... | collective-permute-start | bytes 1572872 | tf_op jit(solution)/shard_map/ppermute | solution.py:520
  22.0 3.7 %collective-permute-start.3 = (bf16[1024,512]{1,0:T(8,128)(2,1)S(1)}, bf16[1024,512]{1,0:T(8,128)(2,1)S(1)}, u32[]{:S(2)}, u32[]{:S(2)}) collective-permute-start(bf16[1024,512]{1,0:T(8,128)(2,1)S(1)} %copy-done.9), channel_id=1, source_target_pairs={{1,0},{2,1},{3,2},{4,3},{5,4},{6,5},{7,6},{8,7},{9,8},{10,9},{11,1... | collective-permute-start | bytes 3145736 | tf_op jit(solution)/shard_map/ppermute | solution.py:523
  25.8 3.4 %collective-permute-start.4 = (bf16[512,512]{1,0:T(8,128)(2,1)S(1)}, bf16[512,512]{1,0:T(8,128)(2,1)S(1)}, u32[]{:S(2)}, u32[]{:S(2)}) collective-permute-start(bf16[512,512]{1,0:T(8,128)(2,1)S(1)} %get-tuple-element.47.field.rest_0_), channel_id=1, source_target_pairs={{0,1},{1,2},{2,3},{3,4},{4,5},{5,6},{6,7},{7,8},{8,9},{9,10},{10,1... | collective-permute-start | bytes 1572872 | tf_op jit(solution)/shard_map/ppermute | solution.py:523
  29.2 2.4 %collective-permute-done.1.got.pair_got = bf16[512,512]{1,0:T(8,128)(2,1)S(1)} collective-permute-done((bf16[512,512]{1,0:T(8,128)(2,1)S(1)}, bf16[512,512]{1,0:T(8,128)(2,1)S(1)}, u32[]{:S(2)}, u32[]{:S(2)}) %collective-permute-start.1) | collective-permute-done | bytes 524320 | tf_op jit(solution)/shard_map/ppermute | solution.py:520
  31.7 1.3 shard_map.104
  33.0 4.1 %collective-permute-start.2 = (bf16[512,512]{1,0:T(8,128)(2,1)S(1)}, bf16[512,512]{1,0:T(8,128)(2,1)S(1)}, u32[]{:S(2)}, u32[]{:S(2)}) collective-permute-start(bf16[512,512]{1,0:T(8,128)(2,1)S(1)} %get-tuple-element.44.own_high), channel_id=1, source_target_pairs={{0,128},{32,160},{64,192},{96,224},{128,0},{160,32},{192,64},{224,... | collective-permute-start | bytes 1572872 | tf_op jit(solution)/shard_map/ppermute | solution.py:520
  37.1 0.6 shard_map.106
  37.8 2.0 %collective-permute-done.3.bundle = bf16[1024,512]{1,0:T(8,128)(2,1)S(1)} collective-permute-done((bf16[1024,512]{1,0:T(8,128)(2,1)S(1)}, bf16[1024,512]{1,0:T(8,128)(2,1)S(1)}, u32[]{:S(2)}, u32[]{:S(2)}) %collective-permute-start.3) | collective-permute-done | bytes 1048608 | tf_op jit(solution)/shard_map/ppermute | solution.py:523
  39.8 1.0 copy-done.7
  40.7 3.1 %shard_map.105 = (bf16[512,512]{1,0:T(8,128)(2,1)S(1)}, bf16[512,512]{1,0:T(8,128)(2,1)S(1)}, f32[512,512]{1,0:T(8,128)}) custom-call(s32[5]{0:T(128)S(1)} %stack.15.place, bf16[512,512]{1,0:T(8,128)(2,1)S(1)} %bitcast.19, bf16[1024,512]{1,0:T(8,128)(2,1)} %copy-done.7, bf16[512,512]{1,0:T(8,128)(2,1)} %copy-done.8), custom_call_target="tpu_custom_call" | custom-call | flops 1 | bytes 1 | tf_op jit(solution)/shard_map/pallas_call | solution.py:75
  43.9 2.5 %collective-permute-done.2.got.whole_got = bf16[512,512]{1,0:T(8,128)(2,1)S(1)} collective-permute-done((bf16[512,512]{1,0:T(8,128)(2,1)S(1)}, bf16[512,512]{1,0:T(8,128)(2,1)S(1)}, u32[]{:S(2)}, u32[]{:S(2)}) %collective-permute-start.2) | collective-permute-done | bytes 524320 | tf_op jit(solution)/shard_map/ppermute | solution.py:520
  46.4 1.3 shard_map.107.after
  47.7 4.9 %collective-permute-start.5 = (bf16[512,512]{1,0:T(8,128)(2,1)S(1)}, bf16[512,512]{1,0:T(8,128)(2,1)S(1)}, u32[]{:S(2)}, u32[]{:S(2)}) collective-permute-start(bf16[512,512]{1,0:T(8,128)(2,1)S(1)} %shard_map.107.after), channel_id=1, source_target_pairs={{0,384},{32,416},{64,448},{96,480},{128,256},{160,288},{192,320},{... | collective-permute-start | bytes 1572872 | tf_op jit(solution)/shard_map/ppermute | solution.py:520
  52.6 0.6 shard_map.108
  53.2 18.8 %all-to-all-start = ((f32[32,1,128]{2,1,0:T(1,128)}), f32[32,1,128]{2,1,0:T(1,128)S(1)}, u32[]{:S(2)}, u32[]{:S(2)}) async-start(f32[32,1,128]{2,1,0:T(1,128)} %bitcast.9), calls=%async_computation | async-start | bytes 32768 | tf_op jit(solution)/shard_map/all_to_all | solution.py:526
  72.1 1.4 shard_map.109
  73.5 0.8 copy-done.4
  74.3 0.8 copy-done.5
  75.1 8.7 %all-to-all-done = f32[32,1,128]{2,1,0:T(1,128)S(1)} async-done(((f32[32,1,128]{2,1,0:T(1,128)}), f32[32,1,128]{2,1,0:T(1,128)S(1)}, u32[]{:S(2)}, u32[]{:S(2)}) %all-to-all-start) | async-done | bytes 16416 | tf_op jit(solution)/shard_map/all_to_all | solution.py:526
  83.8 4.3 %shard_map.110 = (bf16[512,512]{1,0:T(8,128)(2,1)S(1)}, bf16[512,512]{1,0:T(8,128)(2,1)}, bf16[512,512]{1,0:T(8,128)(2,1)S(1)}, f32[1,128]{1,0:T(1,128)S(1)}) custom-call(s32[5]{0:T(128)S(1)} %stack.15.place, bf16[512,512]{1,0:T(8,128)(2,1)S(1)} %collective-permute-done.5.ahead, f32[32,128]{1,0:T(8,128)S(1)} %bitcast.20, bf16[512,512]{1,0:T(8,128)(2,1)} %copy-done, ...), custom_call_target="tpu_custom_call" | custom-call | flops 1 | bytes 1 | tf_op jit(solution)/shard_map/pallas_call | solution.py:75
  88.1 3.0 %collective-permute-start.6 = (bf16[512,512]{1,0:T(8,128)(2,1)S(1)}, bf16[512,512]{1,0:T(8,128)(2,1)S(1)}, u32[]{:S(2)}, u32[]{:S(2)}) collective-permute-start(bf16[512,512]{1,0:T(8,128)(2,1)S(1)} %get-tuple-element.61.rest_1_.field), channel_id=1, source_target_pairs={{1,2},{2,1},{3,4},{4,3},{5,6},{6,5},{7,8},{8,7},{9,10},{10,9},{11,... | collective-permute-start | bytes 1572872 | tf_op jit(solution)/shard_map/ppermute | solution.py:523
  91.1 1.9 %collective-permute-start.7 = (bf16[512,512]{1,0:T(8,128)(2,1)S(1)}, bf16[512,512]{1,0:T(8,128)(2,1)S(1)}, u32[]{:S(2)}, u32[]{:S(2)}) collective-permute-start(bf16[512,512]{1,0:T(8,128)(2,1)S(1)} %get-tuple-element.61.rest_1_.field), channel_id=1, source_target_pairs={{0,1},{1,0},{2,3},{3,2},{4,5},{5,4},{6,7},{7,6},{8,9},{9,8},{10,11... | collective-permute-start | bytes 1572872 | tf_op jit(solution)/shard_map/ppermute | solution.py:523
  93.0 1.2 shard_map.111
  94.2 4.4 %collective-permute-done.6.field_b = bf16[512,512]{1,0:T(8,128)(2,1)S(1)} collective-permute-done((bf16[512,512]{1,0:T(8,128)(2,1)S(1)}, bf16[512,512]{1,0:T(8,128)(2,1)S(1)}, u32[]{:S(2)}, u32[]{:S(2)}) %collective-permute-start.6) | collective-permute-done | bytes 524320 | tf_op jit(solution)/shard_map/ppermute | solution.py:523
  99.1 1.0 shard_map.113.rest_2_.field
  100.1 3.0 %collective-permute-start.8 = (bf16[512,512]{1,0:T(8,128)(2,1)S(1)}, bf16[512,512]{1,0:T(8,128)(2,1)S(1)}, u32[]{:S(2)}, u32[]{:S(2)}) collective-permute-start(bf16[512,512]{1,0:T(8,128)(2,1)S(1)} %shard_map.113.rest_2_.field), channel_id=1, source_target_pairs={{1,2},{2,1},{3,4},{4,3},{5,6},{6,5},{7,8},{8,7},{9,10},{10,9},{11,... | collective-permute-start | bytes 1572872 | tf_op jit(solution)/shard_map/ppermute | solution.py:523
  103.1 2.1 %collective-permute-start.9 = (bf16[512,512]{1,0:T(8,128)(2,1)S(1)}, bf16[512,512]{1,0:T(8,128)(2,1)S(1)}, u32[]{:S(2)}, u32[]{:S(2)}) collective-permute-start(bf16[512,512]{1,0:T(8,128)(2,1)S(1)} %shard_map.113.rest_2_.field), channel_id=1, source_target_pairs={{0,1},{1,0},{2,3},{3,2},{4,5},{5,4},{6,7},{7,6},{8,9},{9,8},{10,11... | collective-permute-start | bytes 1572872 | tf_op jit(solution)/shard_map/ppermute | solution.py:523
  105.2 1.3 shard_map.114
  106.5 4.1 %collective-permute-done.8.field_b = bf16[512,512]{1,0:T(8,128)(2,1)S(1)} collective-permute-done((bf16[512,512]{1,0:T(8,128)(2,1)S(1)}, bf16[512,512]{1,0:T(8,128)(2,1)S(1)}, u32[]{:S(2)}, u32[]{:S(2)}) %collective-permute-start.8) | collective-permute-done | bytes 524320 | tf_op jit(solution)/shard_map/ppermute | solution.py:523
  110.6 0.4 shard_map.115.partial
  111.1 1.0 shard_map.116.rest_3_.field
  112.1 3.0 %collective-permute-start.10 = (bf16[512,512]{1,0:T(8,128)(2,1)S(1)}, bf16[512,512]{1,0:T(8,128)(2,1)S(1)}, u32[]{:S(2)}, u32[]{:S(2)}) collective-permute-start(bf16[512,512]{1,0:T(8,128)(2,1)S(1)} %shard_map.116.rest_3_.field), channel_id=1, source_target_pairs={{1,2},{2,1},{3,4},{4,3},{5,6},{6,5},{7,8},{8,7},{9,10},{10,9},{11,... | collective-permute-start | bytes 1572872 | tf_op jit(solution)/shard_map/ppermute | solution.py:523
  115.1 1.9 %collective-permute-start.11 = (bf16[512,512]{1,0:T(8,128)(2,1)S(1)}, bf16[512,512]{1,0:T(8,128)(2,1)S(1)}, u32[]{:S(2)}, u32[]{:S(2)}) collective-permute-start(bf16[512,512]{1,0:T(8,128)(2,1)S(1)} %shard_map.116.rest_3_.field), channel_id=1, source_target_pairs={{0,1},{1,0},{2,3},{3,2},{4,5},{5,4},{6,7},{7,6},{8,9},{9,8},{10,11... | collective-permute-start | bytes 1572872 | tf_op jit(solution)/shard_map/ppermute | solution.py:523
  117.0 1.4 shard_map.117
  118.4 4.2 %collective-permute-done.10.field_b = bf16[512,512]{1,0:T(8,128)(2,1)S(1)} collective-permute-done((bf16[512,512]{1,0:T(8,128)(2,1)S(1)}, bf16[512,512]{1,0:T(8,128)(2,1)S(1)}, u32[]{:S(2)}, u32[]{:S(2)}) %collective-permute-start.10) | collective-permute-done | bytes 524320 | tf_op jit(solution)/shard_map/ppermute | solution.py:523
  122.6 0.4 shard_map.118.partial
  123.1 1.1 shard_map.119
  124.2 1.9 %collective-permute-start.13 = (bf16[512,512]{1,0:T(8,128)(2,1)S(1)}, bf16[512,512]{1,0:T(8,128)(2,1)S(1)}, u32[]{:S(2)}, u32[]{:S(2)}) collective-permute-start(bf16[512,512]{1,0:T(8,128)(2,1)S(1)} %get-tuple-element.71.rest_4_.last), channel_id=1, source_target_pairs={{0,1},{1,0},{2,3},{3,2},{4,5},{5,4},{6,7},{7,6},{8,9},{9,8},{10,11... | collective-permute-start | bytes 1572872 | tf_op jit(solution)/shard_map/ppermute | solution.py:523
  126.1 3.1 %collective-permute-start.12 = (bf16[512,256]{1,0:T(8,128)(2,1)S(1)}, bf16[512,256]{1,0:T(8,128)(2,1)S(1)}, u32[]{:S(2)}, u32[]{:S(2)}) collective-permute-start(bf16[512,256]{1,0:T(8,128)(2,1)S(1)} %get-tuple-element.65), channel_id=1, source_target_pairs={{1,2},{2,1},{3,4},{4,3},{5,6},{6,5},{7,8},{8,7},{9,10},{10,9},{11,... | collective-permute-start | bytes 786440 | tf_op jit(solution)/shard_map/ppermute | solution.py:523
  129.2 1.4 shard_map.120
  130.6 0.5 shard_map.121.rest_5_
  131.2 2.6 %collective-permute-done.12.got = bf16[512,256]{1,0:T(8,128)(2,1)S(1)} collective-permute-done((bf16[512,256]{1,0:T(8,128)(2,1)S(1)}, bf16[512,256]{1,0:T(8,128)(2,1)S(1)}, u32[]{:S(2)}, u32[]{:S(2)}) %collective-permute-start.12) | collective-permute-done | bytes 262176 | tf_op jit(solution)/shard_map/ppermute | solution.py:523
  134.2 19.9 %all_to_all.10 = f32[32,1,128]{2,1,0:T(1,128)S(1)} all-to-all(f32[32,1,128]{2,1,0:T(1,128)S(1)} %bitcast.22), channel_id=1, replica_groups=mesh['seg'=16,'op'=32] {'op'}, dimensions={0} | all-to-all | bytes 32768 | tf_op jit(solution)/shard_map/all_to_all | solution.py:526
  154.1 1.9 %shard_map.123 = (f32[512,512]{1,0:T(8,128)}, f32[1]{0:T(128)}, f32[1]{0:T(128)}) custom-call(f32[1,128]{1,0:T(1,128)S(1)} %get-tuple-element.57.tune, f32[32,128]{1,0:T(8,128)S(1)} %bitcast.21, bf16[512,512]{1,0:T(8,128)(2,1)S(1)} %copy-done.1, bf16[512,512]{1,0:T(8,128)(2,1)S(1)} %get-tuple-element.61.rest_1_.field, ...), custom_call_target="tpu_custom_call" | custom-call | flops 1 | bytes 1 | tf_op jit(solution)/shard_map/pallas_call | solution.py:75
  (26 shorter events, 1.0 us)
Async XLA Ops:
  0.6 11.1 %collective-permute-start = (bf16[512,512]{1,0:T(8,128)(2,1)}, bf16[512,512]{1,0:T(8,128)(2,1)S(1)}, u32[]{:S(2)}, u32[]{:S(2)}) collective-permute-start(bf16[512,512]{1,0:T(8,128)(2,1)} %bitcast.26), channel_id=1, source_target_pairs={{0,32},{32,0},{64,96},{96,64},{128,160},{160,128},{192,224},{224,1... | collective-permute-start | bytes 1572872 | tf_op jit(solution)/shard_map/ppermute | solution.py:520
  10.0 15.8 %copy-start = (bf16[512,512]{1,0:T(8,128)(2,1)}, bf16[512,512]{1,0:T(8,128)(2,1)S(1)}, u32[]{:S(2)}) copy-start(bf16[512,512]{1,0:T(8,128)(2,1)S(1)} %get-tuple-element.47.field.rest_0_) | copy-start | bytes 1572868
  10.0 12.0 %copy-start.9 = (bf16[1024,512]{1,0:T(8,128)(2,1)S(1)}, bf16[1024,512]{1,0:T(8,128)(2,1)}, u32[]{:S(2)}) copy-start(bf16[1024,512]{1,0:T(8,128)(2,1)} %get-tuple-element.46) | copy-start | bytes 3145732
  12.7 19.0 %collective-permute-start.1 = (bf16[512,512]{1,0:T(8,128)(2,1)S(1)}, bf16[512,512]{1,0:T(8,128)(2,1)S(1)}, u32[]{:S(2)}, u32[]{:S(2)}) collective-permute-start(bf16[512,512]{1,0:T(8,128)(2,1)S(1)} %get-tuple-element.42.own_high), channel_id=1, source_target_pairs={{0,96},{32,64},{64,32},{96,0},{128,224},{160,192},{192,160},{224,1... | collective-permute-start | bytes 1572872 | tf_op jit(solution)/shard_map/ppermute | solution.py:520
  22.0 17.7 %collective-permute-start.3 = (bf16[1024,512]{1,0:T(8,128)(2,1)S(1)}, bf16[1024,512]{1,0:T(8,128)(2,1)S(1)}, u32[]{:S(2)}, u32[]{:S(2)}) collective-permute-start(bf16[1024,512]{1,0:T(8,128)(2,1)S(1)} %copy-done.9), channel_id=1, source_target_pairs={{1,0},{2,1},{3,2},{4,3},{5,4},{6,5},{7,6},{8,7},{9,8},{10,9},{11,1... | collective-permute-start | bytes 3145736 | tf_op jit(solution)/shard_map/ppermute | solution.py:523
  25.8 12.0 %collective-permute-start.4 = (bf16[512,512]{1,0:T(8,128)(2,1)S(1)}, bf16[512,512]{1,0:T(8,128)(2,1)S(1)}, u32[]{:S(2)}, u32[]{:S(2)}) collective-permute-start(bf16[512,512]{1,0:T(8,128)(2,1)S(1)} %get-tuple-element.47.field.rest_0_), channel_id=1, source_target_pairs={{0,1},{1,2},{2,3},{3,4},{4,5},{5,6},{6,7},{7,8},{8,9},{9,10},{10,1... | collective-permute-start | bytes 1572872 | tf_op jit(solution)/shard_map/ppermute | solution.py:523
  33.0 7.7 %copy-start.2 = (bf16[1,1,512,512]{3,2,1,0:T(8,128)(2,1)S(1)}, bf16[1,1,512,512]{3,2,1,0:T(8,128)(2,1)}, u32[]{:S(2)}) copy-start(bf16[1,1,512,512]{3,2,1,0:T(8,128)(2,1)} %param.11) | copy-start | bytes 1572868
  33.0 13.4 %collective-permute-start.2 = (bf16[512,512]{1,0:T(8,128)(2,1)S(1)}, bf16[512,512]{1,0:T(8,128)(2,1)S(1)}, u32[]{:S(2)}, u32[]{:S(2)}) collective-permute-start(bf16[512,512]{1,0:T(8,128)(2,1)S(1)} %get-tuple-element.44.own_high), channel_id=1, source_target_pairs={{0,128},{32,160},{64,192},{96,224},{128,0},{160,32},{192,64},{224,... | collective-permute-start | bytes 1572872 | tf_op jit(solution)/shard_map/ppermute | solution.py:520
  37.7 6.2 %copy-start.6 = (bf16[512,512]{1,0:T(8,128)(2,1)}, bf16[512,512]{1,0:T(8,128)(2,1)S(1)}, u32[]{:S(2)}) copy-start(bf16[512,512]{1,0:T(8,128)(2,1)S(1)} %get-tuple-element.51.row_low) | copy-start | bytes 1572868
  37.7 8.6 %copy-start.3 = (bf16[512,512]{1,0:T(8,128)(2,1)}, bf16[512,512]{1,0:T(8,128)(2,1)S(1)}, u32[]{:S(2)}) copy-start(bf16[512,512]{1,0:T(8,128)(2,1)S(1)} %get-tuple-element.49.rest_1_.row_high) | copy-start | bytes 1572868
  37.8 2.0 %copy-start.8 = (bf16[512,512]{1,0:T(8,128)(2,1)}, bf16[512,512]{1,0:T(8,128)(2,1)S(1)}, u32[]{:S(2)}) copy-start(bf16[512,512]{1,0:T(8,128)(2,1)S(1)} %collective-permute-done.4.below) | copy-start | bytes 1572868
  39.8 1.0 copy-start.7
  47.7 36.1 %collective-permute-start.5 = (bf16[512,512]{1,0:T(8,128)(2,1)S(1)}, bf16[512,512]{1,0:T(8,128)(2,1)S(1)}, u32[]{:S(2)}, u32[]{:S(2)}) collective-permute-start(bf16[512,512]{1,0:T(8,128)(2,1)S(1)} %shard_map.107.after), channel_id=1, source_target_pairs={{0,384},{32,416},{64,448},{96,480},{128,256},{160,288},{192,320},{... | collective-permute-start | bytes 1572872 | tf_op jit(solution)/shard_map/ppermute | solution.py:520
  53.2 30.6 %all-to-all-start = ((f32[32,1,128]{2,1,0:T(1,128)}), f32[32,1,128]{2,1,0:T(1,128)S(1)}, u32[]{:S(2)}, u32[]{:S(2)}) async-start(f32[32,1,128]{2,1,0:T(1,128)} %bitcast.9), calls=%async_computation | async-start | bytes 32768 | tf_op jit(solution)/shard_map/all_to_all | solution.py:526
  73.5 0.8 copy-start.4
  74.3 0.8 copy-start.5
  83.8 9.2 %copy-start.1 = (bf16[512,512]{1,0:T(8,128)(2,1)S(1)}, bf16[512,512]{1,0:T(8,128)(2,1)}, u32[]{:S(2)}) copy-start(bf16[512,512]{1,0:T(8,128)(2,1)} %copy-done) | copy-start | bytes 1572868
  88.1 10.5 %collective-permute-start.6 = (bf16[512,512]{1,0:T(8,128)(2,1)S(1)}, bf16[512,512]{1,0:T(8,128)(2,1)S(1)}, u32[]{:S(2)}, u32[]{:S(2)}) collective-permute-start(bf16[512,512]{1,0:T(8,128)(2,1)S(1)} %get-tuple-element.61.rest_1_.field), channel_id=1, source_target_pairs={{1,2},{2,1},{3,4},{4,3},{5,6},{6,5},{7,8},{8,7},{9,10},{10,9},{11,... | collective-permute-start | bytes 1572872 | tf_op jit(solution)/shard_map/ppermute | solution.py:523
  91.1 7.9 %collective-permute-start.7 = (bf16[512,512]{1,0:T(8,128)(2,1)S(1)}, bf16[512,512]{1,0:T(8,128)(2,1)S(1)}, u32[]{:S(2)}, u32[]{:S(2)}) collective-permute-start(bf16[512,512]{1,0:T(8,128)(2,1)S(1)} %get-tuple-element.61.rest_1_.field), channel_id=1, source_target_pairs={{0,1},{1,0},{2,3},{3,2},{4,5},{5,4},{6,7},{7,6},{8,9},{9,8},{10,11... | collective-permute-start | bytes 1572872 | tf_op jit(solution)/shard_map/ppermute | solution.py:523
  100.1 10.5 %collective-permute-start.8 = (bf16[512,512]{1,0:T(8,128)(2,1)S(1)}, bf16[512,512]{1,0:T(8,128)(2,1)S(1)}, u32[]{:S(2)}, u32[]{:S(2)}) collective-permute-start(bf16[512,512]{1,0:T(8,128)(2,1)S(1)} %shard_map.113.rest_2_.field), channel_id=1, source_target_pairs={{1,2},{2,1},{3,4},{4,3},{5,6},{6,5},{7,8},{8,7},{9,10},{10,9},{11,... | collective-permute-start | bytes 1572872 | tf_op jit(solution)/shard_map/ppermute | solution.py:523
  103.1 7.9 %collective-permute-start.9 = (bf16[512,512]{1,0:T(8,128)(2,1)S(1)}, bf16[512,512]{1,0:T(8,128)(2,1)S(1)}, u32[]{:S(2)}, u32[]{:S(2)}) collective-permute-start(bf16[512,512]{1,0:T(8,128)(2,1)S(1)} %shard_map.113.rest_2_.field), channel_id=1, source_target_pairs={{0,1},{1,0},{2,3},{3,2},{4,5},{5,4},{6,7},{7,6},{8,9},{9,8},{10,11... | collective-permute-start | bytes 1572872 | tf_op jit(solution)/shard_map/ppermute | solution.py:523
  112.1 10.5 %collective-permute-start.10 = (bf16[512,512]{1,0:T(8,128)(2,1)S(1)}, bf16[512,512]{1,0:T(8,128)(2,1)S(1)}, u32[]{:S(2)}, u32[]{:S(2)}) collective-permute-start(bf16[512,512]{1,0:T(8,128)(2,1)S(1)} %shard_map.116.rest_3_.field), channel_id=1, source_target_pairs={{1,2},{2,1},{3,4},{4,3},{5,6},{6,5},{7,8},{8,7},{9,10},{10,9},{11,... | collective-permute-start | bytes 1572872 | tf_op jit(solution)/shard_map/ppermute | solution.py:523
  115.1 8.0 %collective-permute-start.11 = (bf16[512,512]{1,0:T(8,128)(2,1)S(1)}, bf16[512,512]{1,0:T(8,128)(2,1)S(1)}, u32[]{:S(2)}, u32[]{:S(2)}) collective-permute-start(bf16[512,512]{1,0:T(8,128)(2,1)S(1)} %shard_map.116.rest_3_.field), channel_id=1, source_target_pairs={{0,1},{1,0},{2,3},{3,2},{4,5},{5,4},{6,7},{7,6},{8,9},{9,8},{10,11... | collective-permute-start | bytes 1572872 | tf_op jit(solution)/shard_map/ppermute | solution.py:523
  124.2 6.4 %collective-permute-start.13 = (bf16[512,512]{1,0:T(8,128)(2,1)S(1)}, bf16[512,512]{1,0:T(8,128)(2,1)S(1)}, u32[]{:S(2)}, u32[]{:S(2)}) collective-permute-start(bf16[512,512]{1,0:T(8,128)(2,1)S(1)} %get-tuple-element.71.rest_4_.last), channel_id=1, source_target_pairs={{0,1},{1,0},{2,3},{3,2},{4,5},{5,4},{6,7},{7,6},{8,9},{9,8},{10,11... | collective-permute-start | bytes 1572872 | tf_op jit(solution)/shard_map/ppermute | solution.py:523
  126.1 7.7 %collective-permute-start.12 = (bf16[512,256]{1,0:T(8,128)(2,1)S(1)}, bf16[512,256]{1,0:T(8,128)(2,1)S(1)}, u32[]{:S(2)}, u32[]{:S(2)}) collective-permute-start(bf16[512,256]{1,0:T(8,128)(2,1)S(1)} %get-tuple-element.65), channel_id=1, source_target_pairs={{1,2},{2,1},{3,4},{4,3},{5,6},{6,5},{7,8},{8,7},{9,10},{10,9},{11,... | collective-permute-start | bytes 786440 | tf_op jit(solution)/shard_map/ppermute | solution.py:523

commit v3 on v2

--- a/solution.py
+++ b/solution.py
@@ -12,7 +12,8 @@
 LANES = 128
 STEP = 256
 BAND = 32
-SHIFT = 2.0
+DAMP = 2.0**-14
+PEAK = 32
 GRANT = 52
 epsilon = 1e-06
 
@@ -55,19 +56,42 @@
     return (row < sizes[0]) & (col < sizes[1])
 
 
-def banded_dots(fields, last):
-    n, cols = last.shape
-
-    def band(i, sums):
-        at = pl.ds(pl.multiple_of(i * BAND, BAND), BAND)
-        mine = last[at, :].astype(f32)
+def whole(parts, at):
+    return sum(p[at, :].astype(f32) for p in parts)
+
+
+def over_bands(n, body, start):
+    def band(i, carry):
+        return body(pl.ds(pl.multiple_of(i * BAND, BAND), BAND), carry)
+
+    return lax.fori_loop(0, n // BAND, band, start)
+
+
+def gram_row(fields, peaks):
+    newest = fields[-1]
+    n, cols = newest[0].shape
+
+    def fold(x):
+        return x.reshape(BAND // 8, 8, cols)
+
+    def widest(at, top):
+        return jnp.maximum(top, jnp.max(fold(jnp.abs(whole(newest, at))), axis=0))
+
+    top = over_bands(n, widest, jnp.zeros((8, cols), f32))
+    peak = jnp.max(jnp.max(top, axis=0, keepdims=True), axis=1, keepdims=True)
+    peak = jnp.where(peak > 0.0, peak, 1.0)
+    peaks = [*peaks, peak]
+
+    def products(at, sums):
+        mine = whole(newest, at) / peak
         return tuple(
-            s + jnp.sum((f[at, :].astype(f32) * mine).reshape(BAND // 8, 8, cols), axis=0)
-            for s, f in zip(sums, fields, strict=True)
+            s + jnp.sum(fold(whole(f, at) / p * mine), axis=0)
+            for s, f, p in zip(sums, fields, peaks, strict=True)
         )
 
-    sums = lax.fori_loop(0, n // BAND, band, tuple(jnp.zeros((8, cols), f32) for _ in fields))
-    return [total(s) for s in sums]
+    sums = over_bands(n, products, tuple(jnp.zeros((8, cols), f32) for _ in fields))
+    k = len(fields) - 1
+    return in_lanes(k * (k + 1) // 2, [total(x) for x in sums]) + in_lanes(PEAK + k, [peak])
 
 
 def call(kernel, out, smem=1, loose=0, far=0, scratch=(), out_specs=None, grant=20):
@@ -90,31 +114,9 @@
     return run
 
 
-def survey(transfer, edge, right, coupling):
-    n = transfer.shape[0]
-    (grown,), (edge_sq,), (right_sq,), (coupling_sq,) = (
-        banded_dots([x], x) for x in (transfer, edge, right, coupling)
-    )
-    edge_trace = right_trace = jnp.zeros((1, 1), f32)
-    for c in range(0, n, LANES):
-        diagonal = lax.broadcasted_iota(jnp.int32, (LANES, LANES), 0) == lax.broadcasted_iota(
-            jnp.int32, (LANES, LANES), 1
-        )
-        at = slice(c, c + LANES)
-        edge_trace += total(jnp.where(diagonal, edge[at, at].astype(f32), 0.0))
-        right_trace += total(jnp.where(diagonal, right[at, at].astype(f32), 0.0))
-    values = (
-        grown / n,
-        jnp.sqrt(edge_sq / n) * jnp.sqrt(right_sq / n),
-        coupling_sq / n,
-        edge_trace / n * (right_trace / n),
-    )
-    return in_lanes(0, values)
-
-
 def prepare_kernel(
     place, transfer, theta, edge, right, coupling,
-    transfer_out, field_out, right_out, stats, found, bundle_far, edge_far, lifted_far,
+    transfer_out, field_out, right_out, stats, bundle_far, edge_far, lifted_far,
     bundle, edge_out, lifted, sems,
 ):
     n = theta.shape[0]
@@ -138,31 +140,19 @@
             )
     moves[1].start()
     for c in range(0, n, STEP):
-        lifted[c : c + STEP, :] = wide_dot(field_out[c : c + STEP, :], right_out[...]).astype(bf16)
+        parts = split(wide_dot(field_out[c : c + STEP, :], right_out[...]))
+        for i, part in enumerate(parts):
+            lifted[i * n + c : i * n + c + STEP, :] = part
     moves[2].start()
     transfer_out[...] = transfer[...]
-    stats[...] = in_lanes(0, banded_dots([field_out], field_out))
-    found[...] = survey(transfer, edge, right, coupling)
+    stats[...] = gram_row([(field_out,)], [])
     for move in moves:
         move.wait()
 
 
-def spread_kernel(found, after, out):
-    out[...] = jnp.broadcast_to(found[...], out.shape)
-
-
 def lane_entry(row, i):
-    lane = lax.broadcasted_iota(jnp.int32, (1, LANES), 1)
+    lane = lax.broadcasted_iota(jnp.int32, row.shape, 1)
     return jnp.sum(jnp.where(lane == i, row, 0.0), axis=1, keepdims=True)
-
-
-def tuning(place, found):
-    row = jnp.sum(found[...], axis=0, keepdims=True) / found.shape[0]
-    grown, size, coupling_sq, trace = (lane_entry(row, i) for i in range(4))
-    segment = (place[3] * ROW + place[4]).astype(f32)
-    growth = jnp.exp(jnp.clip(segment * jnp.log(jnp.maximum(grown, 1e-30)), -30.0, 30.0))
-    scale = size * growth + 2.0 * jnp.sqrt(coupling_sq) + 1e-12
-    return in_lanes(0, (SHIFT * trace * growth, 1.0 / scale, scale))
 
 
 def couple_kernel(place, coupling, bundle, below, near, far, image_far, image, sem):
@@ -300,8 +290,8 @@
 
 
 def segment_kernel(
-    place, ahead, found, field, high_far, low_far, edge_far, couplings_far, lifted_far,
-    left, left_out, next_field, tune,
+    place, ahead, high_far, low_far, edge_far, couplings_far, lifted_far,
+    left, left_out, next_high, next_low,
     high, low, edge, couplings, lifted, prefix, turned, turned_wide, sems,
 ):
     sizes = (place[1], place[2])
@@ -313,9 +303,6 @@
     moves = [pltpu.make_async_copy(*pair, sems.at[i]) for i, pair in enumerate(pairs)]
     for move in moves:
         move.start()
-    tuned = tuning(place, found)
-    tune[...] = tuned
-    shift, gain = lane_entry(tuned, 0), lane_entry(tuned, 1)
     moves[0].wait()
     moves[1].wait()
 
@@ -343,32 +330,23 @@
     moves[4].wait()
     for c in range(0, n, STEP):
         at = slice(c, c + STEP)
-        image = wide_dot(left[at, :], lifted[...]) + couplings[at, :]
-        moved = (image - shift * field[at, :].astype(f32)) * gain
-        next_field[at, :] = jnp.where(live(c, STEP, n, sizes), moved, 0.0).astype(bf16)
-
-
-def local_kernel(count, left, right, *rest):
-    fields, (partial, stats) = rest[:count], rest[count:]
-    field = fields[-1]
-    n = field.shape[0]
-    for c in range(0, n, STEP):
-        at = slice(c, c + STEP)
-        middle = wide_dot(left[at, :], field[...]).astype(bf16)
-        partial[at, :] = wide_dot(middle, right[...])
-    k = count - 1
-    stats[...] = in_lanes(k * (k + 1) // 2, banded_dots(list(fields), field))
-
-
-def near_last_kernel(near, field_a, partial, last, out):
-    n = near.shape[0]
-    inner = jnp.zeros((1, 1), f32)
-    for c in range(0, n, STEP):
-        at = slice(c, c + STEP)
-        image = partial[at, :] + wide_dot(near[at, :], field_a[...])
-        inner += total(image * last[at, :].astype(f32))
-    k = DAVIDSON + 1
-    out[...] = in_lanes(k * (k + 1) // 2, [inner])
+        image = wide_dot(left[at, :], lifted[:n, :]) + wide_dot(left[at, :], lifted[n:, :])
+        image = jnp.where(live(c, STEP, n, sizes), image + couplings[at, :], 0.0)
+        next_high[at, :], next_low[at, :] = split(DAMP * image)
+
+
+def local_kernel(count, stats_in, left, right, *rest):
+    parts, (partial, stats) = rest[: 2 * count - 1], rest[2 * count - 1 :]
+    fields = [parts[:1]] + [parts[i : i + 2] for i in range(1, 2 * count - 1, 2)]
+    newest = fields[-1]
+    n = left.shape[0]
+    for c in range(0, n, STEP):
+        at = slice(c, c + STEP)
+        middle = sum(wide_dot(left[at, :], x[...]) for x in newest)
+        partial[at, :] = sum(wide_dot(x, right[...]) for x in split(middle))
+    before = stats_in[...]
+    peaks = [lane_entry(before, PEAK + k) for k in range(count - 1)]
+    stats[...] = before + gram_row(fields, peaks)
 
 
 def far_kernel(partial, far, field_b, out):
@@ -378,63 +356,79 @@
         out[at, :] = partial[at, :] + wide_dot(far[at, :], field_b[...])
 
 
-def advance_kernel(place, tune, partial, near, field_a, field, next_field):
+def advance_kernel(place, partial, near, field_a, next_high, next_low, *halves):
     sizes = (place[1], place[2])
-    n = field.shape[0]
-    shift, gain = lane_entry(tune[...], 0), lane_entry(tune[...], 1)
+    n = near.shape[0]
     for c in range(0, n, STEP):
         at = slice(c, c + STEP)
         image = partial[at, :] + wide_dot(near[at, :], field_a[...])
-        moved = (image - shift * field[at, :].astype(f32)) * gain
-        next_field[at, :] = jnp.where(live(c, STEP, n, sizes), moved, 0.0).astype(bf16)
-
-
-def advance_last_kernel(place, tune, partial, near, field_a, field, next_field, sent, kept):
-    advance_kernel(place, tune, partial, near, field_a, field, next_field)
-    half = field.shape[1] // 2
+        image = jnp.where(live(c, STEP, n, sizes), image, 0.0)
+        next_high[at, :], next_low[at, :] = split(DAMP * image)
+    if not halves:
+        return
+    sent, kept = halves
+    half = n // 2
 
     @pl.when(place[0] == 1)
     def _():
-        sent[...] = next_field[:, :half]
-        kept[...] = next_field[:, half:]
+        sent[...] = next_high[:, :half]
+        kept[...] = next_high[:, half:].astype(f32) + next_low[:, half:].astype(f32)
 
     @pl.when(place[0] != 1)
     def _():
-        sent[...] = next_field[:, half:]
-        kept[...] = next_field[:, :half]
-
-
-def close_kernel(far, got, kept, *rest):
-    stats_in, out = rest[:-1], rest[-1]
+        sent[...] = next_high[:, half:]
+        kept[...] = next_high[:, :half].astype(f32) + next_low[:, :half].astype(f32)
+
+
+def far_last_kernel(stats_in, far, got, kept, out):
     n = far.shape[0]
+    peak = lane_entry(stats_in[...], PEAK + DAVIDSON)
     inner = jnp.zeros((1, 1), f32)
     for c in range(0, n, STEP):
         at = slice(c, c + STEP)
-        inner += total(wide_dot(far[at, :], got[...]) * kept[at, :].astype(f32))
+        inner += total(wide_dot(far[at, :], got[...]) / peak * (kept[at, :] / peak))
     k = DAVIDSON + 1
-    sums = in_lanes(k * (k + 1) // 2, [2.0 * inner])
-    for piece in stats_in:
-        sums += piece[...]
-    out[...] = jnp.broadcast_to(sums, out.shape)
-
-
-def solve_kernel(tune, sums, *rest):
+    out[...] = stats_in[...] + in_lanes(k * (k + 1) // 2, [2.0 * inner])
+
+
+def close_kernel(stats_in, near, field_a, partial, high, low, out):
+    n = near.shape[0]
+    peak = lane_entry(stats_in[...], PEAK + DAVIDSON)
+    inner = jnp.zeros((1, 1), f32)
+    for c in range(0, n, STEP):
+        at = slice(c, c + STEP)
+        image = partial[at, :] + wide_dot(near[at, :], field_a[...])
+        inner += total(image / peak * (whole((high, low), at) / peak))
+    k = DAVIDSON + 1
+    out[...] = jnp.broadcast_to(
+        stats_in[...] + in_lanes(k * (k + 1) // 2, [inner]), out.shape
+    )
+
+
+def solve_kernel(sums, *rest):
     size = DAVIDSON + 1
-    fields, (vector, last_energy, first_energy) = rest[:size], rest[size:]
-    shift, scale = lane_entry(tune[...], 0), lane_entry(tune[...], 2)
-    row = jnp.sum(sums[...], axis=0, keepdims=True)
-    entry = functools.partial(lane_entry, row)
+    parts, (vector, last_energy, first_energy) = rest[: 2 * size - 1], rest[2 * size - 1 :]
+    fields = [parts[:1]] + [parts[i : i + 2] for i in range(1, 2 * size - 1, 2)]
+    table = sums[...]
+    local_peaks = [lane_entry(table, PEAK + k) for k in range(size)]
+    peaks = [jnp.max(p, axis=0, keepdims=True) for p in local_peaks]
+    ratios = [p / top for p, top in zip(local_peaks, peaks, strict=True)]
+    scales = [peaks[k + 1] / peaks[k] * (1.0 / DAMP) for k in range(size - 1)]
+
+    def entry(i, j, k):
+        return jnp.sum(lane_entry(table, i) * ratios[j] * ratios[k], axis=0, keepdims=True)
+
     gram = {}
     for k in range(size):
         for j in range(k + 1):
-            gram[j, k] = gram[k, j] = entry(k * (k + 1) // 2 + j)
+            gram[j, k] = gram[k, j] = entry(k * (k + 1) // 2 + j, j, k)
     image_gram = {}
     for j in range(size):
         for k in range(j, size):
             if j < size - 1:
-                value = scale * gram[j + 1, k] + shift * gram[j, k]
+                value = scales[j] * gram[j + 1, k]
             else:
-                value = entry(size * (size + 1) // 2)
+                value = entry(size * (size + 1) // 2, j, j)
             image_gram[j, k] = image_gram[k, j] = value
 
     def form(table, a, b):
@@ -449,16 +443,17 @@
             out = out + aj * inner
         return out
 
-    weights = [1.0 / jnp.sqrt(gram[0, 0] + epsilon)] + [None] * (size - 1)
+    start_norm = jnp.sqrt(peaks[0] * peaks[0] * gram[0, 0] + epsilon)
+    weights = [peaks[0] / start_norm] + [None] * (size - 1)
     energy = first = form(image_gram, weights, weights)
     for step in range(DAVIDSON):
         turn = [None] * size
         for k in range(step + 2):
             value = None
             if weights[k] is not None:
-                value = (shift - energy) * weights[k]
+                value = -energy * weights[k]
             if k > 0 and weights[k - 1] is not None:
-                carried = scale * weights[k - 1]
+                carried = scales[k - 1] * weights[k - 1]
                 value = carried if value is None else value + carried
             turn[k] = value
         corr_norm = jnp.maximum(form(gram, turn, turn), 0.0)
@@ -481,17 +476,15 @@
         energy = lowest
     last_energy[0] = energy[0, 0]
     first_energy[0] = first[0, 0]
-    n = vector.shape[0]
-
-    def band(i, carry):
-        at = pl.ds(pl.multiple_of(i * BAND, BAND), BAND)
-        out = weights[0] * fields[0][at, :].astype(f32)
-        for w, field in zip(weights[1:], fields[1:], strict=True):
-            out = out + w * field[at, :].astype(f32)
-        vector[at, :] = out
+    weights = [w / p for w, p in zip(weights, peaks, strict=True)]
+
+    def band(at, carry):
+        vector[at, :] = sum(
+            w * whole(field, at) for w, field in zip(weights, fields, strict=True)
+        )
         return carry
 
-    lax.fori_loop(0, n // BAND, band, 0)
+    over_bands(vector.shape[0], band, 0)
 
 
 def on_device(theta, left_edge, transfer, right_env, coupling, left_sizes, right_sizes):
@@ -510,6 +503,7 @@
     up = [(i, i + 1) for i in range(sectors - 1)]
     square, wide = jax.ShapeDtypeStruct((n, n), bf16), jax.ShapeDtypeStruct((n, n), f32)
     tall, double = (jax.ShapeDtypeStruct(d, bf16) for d in ((n, n // 2), (2 * n, n)))
+    tall_wide = jax.ShapeDtypeStruct((n, n // 2), f32)
     lanes = jax.ShapeDtypeStruct((1, LANES), f32)
     spread = jax.ShapeDtypeStruct((sectors, LANES), f32)
     number = jax.ShapeDtypeStruct((1,), f32)
@@ -526,12 +520,12 @@
         return lax.all_to_all(x[:, None], "op", 0, 0)[:, 0]
 
     transfer_got = seg_send(transfer, y_pair)
-    held, field, right, stats, found, bundle, edge_sym, lifted = call(
+    held, field, right, stats, bundle, edge_sym, lifted = call(
         prepare_kernel,
-        (square, square, square, lanes, lanes, double, wide, square),
-        out_specs=(VMEM,) * 5 + (HBM,) * 3,
+        (square, square, square, lanes, double, wide, double),
+        out_specs=(VMEM,) * 4 + (HBM,) * 3,
         grant=GRANT,
-        scratch=[buffer(2 * n, n), buffer(n, n, f32), buffer(n, n), DMA((3,))],
+        scratch=[buffer(2 * n, n), buffer(n, n, f32), buffer(2 * n, n), DMA((3,))],
     )(place, transfer, theta, left_edge, right_env, coupling)
     bundle_got = op_send(bundle, down)
     below = op_send(field, up)
@@ -563,44 +557,41 @@
         grant=GRANT,
         scratch=[buffer(n, n), buffer(n, n), DMA((2,))],
     )(place, whole_got, row_high, row_low)
-    found = call(spread_kernel, spread, smem=0, loose=1)(found, double_high)
-    left, left_out, following, tune = call(
+    left, left_out, *following = call(
         segment_kernel,
-        (square, square, square, lanes),
+        (square, square, square, square),
         far=5,
         grant=GRANT,
         scratch=[
-            *[buffer(n, n)] * 2, *[buffer(n, n, f32)] * 2, *[buffer(n, n)] * 3,
+            *[buffer(n, n)] * 2, *[buffer(n, n, f32)] * 2, buffer(2 * n, n), *[buffer(n, n)] * 2,
             buffer(n, n, f32), DMA((5,)),
         ],
-    )(place, ahead, op_sum(found), field, high, low, edge_sym, couplings, lifted)
-    fields, pieces = [field, following], [stats]
-    sent = kept = None
+    )(place, ahead, high, low, edge_sym, couplings, lifted)
+    fields = [(field,), tuple(following)]
     for k in range(1, DAVIDSON + 1):
+        high, low = fields[-1]
         last = k == DAVIDSON
-        newest = fields[-1]
-        field_a = op_send(newest, near_swap)
-        field_b = op_send(sent if last else newest, far_swap)
+        field_a = op_send(high, near_swap)
+        field_b = op_send(sent if last else high, far_swap)
         partial, stats = call(functools.partial(local_kernel, k + 1), (wide, lanes), smem=0)(
-            left, right, *fields
+            stats, left, right, *sum(fields, ())
         )
-        pieces.append(stats)
         if last:
-            pieces.append(call(near_last_kernel, lanes, smem=0)(near, field_a, partial, newest))
-            sums = call(close_kernel, spread, smem=0)(far, field_b, kept, *pieces)
+            stats = call(far_last_kernel, lanes, smem=0)(stats, far, field_b, kept)
+            sums = call(close_kernel, spread, smem=0)(stats, near, field_a, partial, high, low)
             break
         partial = call(far_kernel, wide, smem=0)(partial, far, field_b)
         if k == DAVIDSON - 1:
-            following, sent, kept = call(advance_last_kernel, (square, tall, tall))(
-                place, tune, partial, near, field_a, newest
+            *following, sent, kept = call(advance_kernel, (square, square, tall, tall_wide))(
+                place, partial, near, field_a
             )
         else:
-            following = call(advance_kernel, square)(place, tune, partial, near, field_a, newest)
-        fields.append(following)
+            following = call(advance_kernel, (square, square))(place, partial, near, field_a)
+        fields.append(tuple(following))
     sums = op_sum(sums)
     vector, energy, first = call(
         solve_kernel, (wide, number, number), smem=0, out_specs=(VMEM, SMEM, SMEM)
-    )(tune, sums, *fields)
+    )(sums, *sum(fields, ()))
     return vector[None, None], left_out[None, None], energy, first
 
 

time: 157 us -> 152 us (0.968)
  the two profiles are of different devices: /device:TPU:1 before, /device:TPU:6 now
where the time goes in v3:
time: 152 us; the launch traced here: 151 us
  starting transfers between devices  43.7 us (29%)
  Pallas kernels  36.7 us (24%)
  blocking collectives  36.3 us (24%)
  waiting for transfers between devices  27.2 us (18%)
  local copies, waits for them, and re-layouts  5.08 us (3%)
  between operations  2.41 us (2%)
    pallas_call x21, Pallas kernels, run(): pl.pallas_call(kernel, out_shape=out, in_specs=[SMEM] * smem + [VMEM] * (...  36.7 us
    all_to_all x1, blocking collectives, op_sum(): return lax.all_to_all(x[:, None], 'op', 0, 0)[:, 0]  36.3 us
    ppermute x10, starting transfers between devices, op_send(): return lax.ppermute(x, 'op', route)  31.1 us
    ppermute x4, waiting for transfers between devices, seg_send(): return lax.ppermute(x, 'seg', route)  27.2 us
    ppermute x4, starting transfers between devices, seg_send(): return lax.ppermute(x, 'seg', route)  12.6 us
    unnamed x18, local copies, waits for them, and re-layouts  4.99 us
  transfers between devices with their start and end apart: 14, of which 4 were waited for; matrix products, arithmetic and copies ran while one was open for 0% of the time, Pallas kernels for 16%

profile of v3, /device:TPU:6, one launch (start us, length us, event | category | flops | bytes accessed | tf_op | source)
XLA Modules:
  0.0 151.2 jit_solution(5114927387159605928)
XLA Ops:
  0.6 3.5 %collective-permute-start = (bf16[512,512]{1,0:T(8,128)(2,1)}, bf16[512,512]{1,0:T(8,128)(2,1)S(1)}, u32[]{:S(2)}, u32[]{:S(2)}) collective-permute-start(bf16[512,512]{1,0:T(8,128)(2,1)} %bitcast.21), channel_id=1, source_target_pairs={{0,32},{32,0},{64,96},{96,64},{128,160},{160,128},{192,224},{224,1... | collective-permute-start | bytes 1572872 | tf_op jit(solution)/shard_map/ppermute | solution.py:514
  5.4 0.1 stack.15.place
  5.5 4.1 %shard_map.102 = (bf16[512,512]{1,0:T(8,128)(2,1)S(1)}, bf16[512,512]{1,0:T(8,128)(2,1)S(1)}, bf16[512,512]{1,0:T(8,128)(2,1)S(1)}, f32[1,128]{1,0:T(1,128)S(1)}...) custom-call(s32[5]{0:T(128)S(1)} %stack.15.place, bf16[512,512]{1,0:T(8,128)(2,1)} %bitcast.22, ...), custom_call_target="tpu_custom_call" | custom-call | flops 1 | bytes 1 | tf_op jit(solution)/shard_map/pallas_call | solution.py:99
  9.7 6.7 %collective-permute-done.got.transfer_got = bf16[512,512]{1,0:T(8,128)(2,1)S(1)} collective-permute-done((bf16[512,512]{1,0:T(8,128)(2,1)}, bf16[512,512]{1,0:T(8,128)(2,1)S(1)}, u32[]{:S(2)}, u32[]{:S(2)}) %collective-permute-start) | collective-permute-done | bytes 524320 | tf_op jit(solution)/shard_map/ppermute | solution.py:514
  16.4 1.0 shard_map.103
  17.4 4.9 %collective-permute-start.1 = (bf16[512,512]{1,0:T(8,128)(2,1)S(1)}, bf16[512,512]{1,0:T(8,128)(2,1)S(1)}, u32[]{:S(2)}, u32[]{:S(2)}) collective-permute-start(bf16[512,512]{1,0:T(8,128)(2,1)S(1)} %get-tuple-element.47.own_high), channel_id=1, source_target_pairs={{0,96},{32,64},{64,32},{96,0},{128,224},{160,192},{192,160},{224,1... | collective-permute-start | bytes 1572872 | tf_op jit(solution)/shard_map/ppermute | solution.py:514
  22.3 1.3 collective-permute-start.3
  23.6 3.1 %collective-permute-start.4 = (bf16[512,512]{1,0:T(8,128)(2,1)S(1)}, bf16[512,512]{1,0:T(8,128)(2,1)S(1)}, u32[]{:S(2)}, u32[]{:S(2)}) collective-permute-start(bf16[512,512]{1,0:T(8,128)(2,1)S(1)} %get-tuple-element.52.rest_0_), channel_id=1, source_target_pairs={{0,1},{1,2},{2,3},{3,4},{4,5},{5,6},{6,7},{7,8},{8,9},{9,10},{10,1... | collective-permute-start | bytes 1572872 | tf_op jit(solution)/shard_map/ppermute | solution.py:517
  26.7 6.7 %collective-permute-done.1.got.pair_got = bf16[512,512]{1,0:T(8,128)(2,1)S(1)} collective-permute-done((bf16[512,512]{1,0:T(8,128)(2,1)S(1)}, bf16[512,512]{1,0:T(8,128)(2,1)S(1)}, u32[]{:S(2)}, u32[]{:S(2)}) %collective-permute-start.1) | collective-permute-done | bytes 524320 | tf_op jit(solution)/shard_map/ppermute | solution.py:514
  33.4 1.4 shard_map.104
  34.7 0.0 copy-start
  34.7 2.9 %collective-permute-start.2 = (bf16[512,512]{1,0:T(8,128)(2,1)S(1)}, bf16[512,512]{1,0:T(8,128)(2,1)S(1)}, u32[]{:S(2)}, u32[]{:S(2)}) collective-permute-start(bf16[512,512]{1,0:T(8,128)(2,1)S(1)} %get-tuple-element.49.own_high), channel_id=1, source_target_pairs={{0,128},{32,160},{64,192},{96,224},{128,0},{160,32},{192,64},{224,... | collective-permute-start | bytes 1572872 | tf_op jit(solution)/shard_map/ppermute | solution.py:514
  37.6 0.6 shard_map.106
  38.3 0.8 copy-done.4
  39.1 0.8 copy-done.6
  39.9 1.0 copy-done.5
  40.9 3.2 %shard_map.105 = (bf16[512,512]{1,0:T(8,128)(2,1)S(1)}, bf16[512,512]{1,0:T(8,128)(2,1)S(1)}, f32[512,512]{1,0:T(8,128)}) custom-call(s32[5]{0:T(128)S(1)} %stack.15.place, bf16[512,512]{1,0:T(8,128)(2,1)S(1)} %bitcast.15, bf16[1024,512]{1,0:T(8,128)(2,1)} %copy-done.5, bf16[512,512]{1,0:T(8,128)(2,1)} %copy-done.6), custom_call_target="tpu_custom_call" | custom-call | flops 1 | bytes 1 | tf_op jit(solution)/shard_map/pallas_call | solution.py:99
  44.0 4.7 %collective-permute-done.2.got.whole_got = bf16[512,512]{1,0:T(8,128)(2,1)S(1)} collective-permute-done((bf16[512,512]{1,0:T(8,128)(2,1)S(1)}, bf16[512,512]{1,0:T(8,128)(2,1)S(1)}, u32[]{:S(2)}, u32[]{:S(2)}) %collective-permute-start.2) | collective-permute-done | bytes 524320 | tf_op jit(solution)/shard_map/ppermute | solution.py:514
  48.7 1.3 shard_map.107
  50.0 1.3 collective-permute-start.5
  51.3 2.1 %shard_map.108 = (bf16[512,512]{1,0:T(8,128)(2,1)S(1)}, bf16[512,512]{1,0:T(8,128)(2,1)S(1)}) custom-call(s32[5]{0:T(128)S(1)} %stack.15.place, bf16[512,512]{1,0:T(8,128)(2,1)S(1)} %collective-permute-done.2.got.whole_got, bf16[512,512]{1,0:T(8,128)(2,1)} %copy-done.1, bf16[512,512]{1,0:T(8,128)(2,1)} %copy-done.4), custom_call_target="tpu_custom_call" | custom-call | flops 1 | bytes 1 | tf_op jit(solution)/shard_map/pallas_call | solution.py:99
  53.5 0.8 copy-done.2
  54.2 0.8 copy-done.3
  55.0 9.1 %collective-permute-done.5.ahead = bf16[512,512]{1,0:T(8,128)(2,1)S(1)} collective-permute-done((bf16[512,512]{1,0:T(8,128)(2,1)S(1)}, bf16[512,512]{1,0:T(8,128)(2,1)S(1)}, u32[]{:S(2)}, u32[]{:S(2)}) %collective-permute-start.5) | collective-permute-done | bytes 524320 | tf_op jit(solution)/shard_map/ppermute | solution.py:514
  64.1 0.8 copy-done.7
  64.9 4.6 %shard_map.109 = (bf16[512,512]{1,0:T(8,128)(2,1)S(1)}, bf16[512,512]{1,0:T(8,128)(2,1)}, bf16[512,512]{1,0:T(8,128)(2,1)S(1)}, bf16[512,512]{1,0:T(8,128)(2,1)S(1)}) custom-call(s32[5]{0:T(128)S(1)} %stack.15.place, bf16[512,512]{1,0:T(8,128)(2,1)} %copy-done.7, bf16[512,512]{1,0:T(8,128)(2,1)} %copy-done.2, bf16[512,512]{1,0:T(8,128)(2,1)} %copy-done.3, ...), custom_call_target="tpu_custom_call" | custom-call | flops 1 | bytes 1 | tf_op jit(solution)/shard_map/pallas_call | solution.py:99
  69.5 0.7 collective-permute-start.6
  70.2 5.2 %collective-permute-start.7 = (bf16[512,512]{1,0:T(8,128)(2,1)S(1)}, bf16[512,512]{1,0:T(8,128)(2,1)S(1)}, u32[]{:S(2)}, u32[]{:S(2)}) collective-permute-start(bf16[512,512]{1,0:T(8,128)(2,1)S(1)} %get-tuple-element.63.rest_1_), channel_id=1, source_target_pairs={{0,1},{1,0},{2,3},{3,2},{4,5},{5,4},{6,7},{7,6},{8,9},{9,8},{10,11... | collective-permute-start | bytes 1572872 | tf_op jit(solution)/shard_map/ppermute | solution.py:517
  75.4 2.2 %shard_map.110 = (f32[512,512]{1,0:T(8,128)S(1)}, f32[1,128]{1,0:T(1,128)S(1)}) custom-call(f32[1,128]{1,0:T(1,128)S(1)} %get-tuple-element.45.stats_in, bf16[512,512]{1,0:T(8,128)(2,1)S(1)} %get-tuple-element.61.left, bf16[512,512]{1,0:T(8,128)(2,1)S(1)} %get-tuple-element.62.right, bf16[512,512]{1,0:T(8,128)(2,1)S(1)} %get-tuple-element.52.rest_0_, ...), custom_call_target="tpu_custom_call" | custom-call | flops 1 | bytes 1 | tf_op jit(solution)/shard_map/pallas_call | solution.py:99
  77.7 0.4 shard_map.111.partial
  78.1 1.1 shard_map.112
  79.2 0.7 collective-permute-start.8
  79.9 7.7 %collective-permute-start.9 = (bf16[512,512]{1,0:T(8,128)(2,1)S(1)}, bf16[512,512]{1,0:T(8,128)(2,1)S(1)}, u32[]{:S(2)}, u32[]{:S(2)}) collective-permute-start(bf16[512,512]{1,0:T(8,128)(2,1)S(1)} %get-tuple-element.68.rest_3_), channel_id=1, source_target_pairs={{0,1},{1,0},{2,3},{3,2},{4,5},{5,4},{6,7},{7,6},{8,9},{9,8},{10,11... | collective-permute-start | bytes 1572872 | tf_op jit(solution)/shard_map/ppermute | solution.py:517
  87.6 2.5 %shard_map.113 = (f32[512,512]{1,0:T(8,128)S(1)}, f32[1,128]{1,0:T(1,128)S(1)}) custom-call(f32[1,128]{1,0:T(1,128)S(1)} %get-tuple-element.65.stats_in, bf16[512,512]{1,0:T(8,128)(2,1)S(1)} %get-tuple-element.61.left, bf16[512,512]{1,0:T(8,128)(2,1)S(1)} %get-tuple-element.62.right, bf16[512,512]{1,0:T(8,128)(2,1)S(1)} %get-tuple-element.52.rest_0_, ...), custom_call_target="tpu_custom_call" | custom-call | flops 1 | bytes 1 | tf_op jit(solution)/shard_map/pallas_call | solution.py:99
  90.2 0.4 shard_map.114.partial
  90.6 1.1 shard_map.115
  91.7 0.7 collective-permute-start.10
  92.4 7.1 %collective-permute-start.11 = (bf16[512,512]{1,0:T(8,128)(2,1)S(1)}, bf16[512,512]{1,0:T(8,128)(2,1)S(1)}, u32[]{:S(2)}, u32[]{:S(2)}) collective-permute-start(bf16[512,512]{1,0:T(8,128)(2,1)S(1)} %get-tuple-element.72.rest_5_), channel_id=1, source_target_pairs={{0,1},{1,0},{2,3},{3,2},{4,5},{5,4},{6,7},{7,6},{8,9},{9,8},{10,11... | collective-permute-start | bytes 1572872 | tf_op jit(solution)/shard_map/ppermute | solution.py:517
  99.5 2.8 %shard_map.116 = (f32[512,512]{1,0:T(8,128)S(1)}, f32[1,128]{1,0:T(1,128)S(1)}) custom-call(f32[1,128]{1,0:T(1,128)S(1)} %get-tuple-element.70.stats_in, bf16[512,512]{1,0:T(8,128)(2,1)S(1)} %get-tuple-element.61.left, bf16[512,512]{1,0:T(8,128)(2,1)S(1)} %get-tuple-element.62.right, bf16[512,512]{1,0:T(8,128)(2,1)S(1)} %get-tuple-element.52.rest_0_, ...), custom_call_target="tpu_custom_call" | custom-call | flops 1 | bytes 1 | tf_op jit(solution)/shard_map/pallas_call | solution.py:99
  102.3 0.4 shard_map.117.partial
  102.7 1.1 shard_map.118
  103.9 4.0 %collective-permute-start.13 = (bf16[512,512]{1,0:T(8,128)(2,1)S(1)}, bf16[512,512]{1,0:T(8,128)(2,1)S(1)}, u32[]{:S(2)}, u32[]{:S(2)}) collective-permute-start(bf16[512,512]{1,0:T(8,128)(2,1)S(1)} %get-tuple-element.76.rest_7_.high), channel_id=1, source_target_pairs={{0,1},{1,0},{2,3},{3,2},{4,5},{5,4},{6,7},{7,6},{8,9},{9,8},{10,11... | collective-permute-start | bytes 1572872 | tf_op jit(solution)/shard_map/ppermute | solution.py:517
  107.9 0.7 collective-permute-start.12
  108.6 3.0 %shard_map.119 = (f32[512,512]{1,0:T(8,128)S(1)}, f32[1,128]{1,0:T(1,128)S(1)}) custom-call(f32[1,128]{1,0:T(1,128)S(1)} %get-tuple-element.74.stats_in, bf16[512,512]{1,0:T(8,128)(2,1)S(1)} %get-tuple-element.61.left, bf16[512,512]{1,0:T(8,128)(2,1)S(1)} %get-tuple-element.62.right, bf16[512,512]{1,0:T(8,128)(2,1)S(1)} %get-tuple-element.52.rest_0_, ...), custom_call_target="tpu_custom_call" | custom-call | flops 1 | bytes 1 | tf_op jit(solution)/shard_map/pallas_call | solution.py:99
  111.6 0.4 shard_map.120.stats_in
  112.0 0.6 shard_map.121
  112.6 36.3 %all_to_all.5 = f32[32,1,128]{2,1,0:T(1,128)S(1)} all-to-all(f32[32,1,128]{2,1,0:T(1,128)S(1)} %bitcast.17), channel_id=1, replica_groups=mesh['seg'=16,'op'=32] {'op'}, dimensions={0} | all-to-all | bytes 32768 | tf_op jit(solution)/shard_map/all_to_all | solution.py:520
  148.9 2.2 %shard_map.122 = (f32[512,512]{1,0:T(8,128)}, f32[1]{0:T(128)}, f32[1]{0:T(128)}) custom-call(f32[32,128]{1,0:T(8,128)S(1)} %bitcast.16, bf16[512,512]{1,0:T(8,128)(2,1)S(1)} %get-tuple-element.52.rest_0_, bf16[512,512]{1,0:T(8,128)(2,1)S(1)} %get-tuple-element.63.rest_1_, bf16[512,512]{1,0:T(8,128)(2,1)S(1)} %get-tuple-element.64.rest_2_, ...), custom_call_target="tpu_custom_call" | custom-call | flops 1 | bytes 1 | tf_op jit(solution)/shard_map/pallas_call | solution.py:99
  (21 shorter events, 0.0 us)
Async XLA Ops:
  0.6 15.8 %collective-permute-start = (bf16[512,512]{1,0:T(8,128)(2,1)}, bf16[512,512]{1,0:T(8,128)(2,1)S(1)}, u32[]{:S(2)}, u32[]{:S(2)}) collective-permute-start(bf16[512,512]{1,0:T(8,128)(2,1)} %bitcast.21), channel_id=1, source_target_pairs={{0,32},{32,0},{64,96},{96,64},{128,160},{160,128},{192,224},{224,1... | collective-permute-start | bytes 1572872 | tf_op jit(solution)/shard_map/ppermute | solution.py:514
  9.6 12.7 %copy-start.8 = (bf16[1024,512]{1,0:T(8,128)(2,1)S(1)}, bf16[1024,512]{1,0:T(8,128)(2,1)}, u32[]{:S(2)}) copy-start(bf16[1024,512]{1,0:T(8,128)(2,1)} %get-tuple-element.51) | copy-start | bytes 3145732
  17.4 16.0 %collective-permute-start.1 = (bf16[512,512]{1,0:T(8,128)(2,1)S(1)}, bf16[512,512]{1,0:T(8,128)(2,1)S(1)}, u32[]{:S(2)}, u32[]{:S(2)}) collective-permute-start(bf16[512,512]{1,0:T(8,128)(2,1)S(1)} %get-tuple-element.47.own_high), channel_id=1, source_target_pairs={{0,96},{32,64},{64,32},{96,0},{128,224},{160,192},{192,160},{224,1... | collective-permute-start | bytes 1572872 | tf_op jit(solution)/shard_map/ppermute | solution.py:514
  22.3 16.7 %collective-permute-start.3 = (bf16[1024,512]{1,0:T(8,128)(2,1)S(1)}, bf16[1024,512]{1,0:T(8,128)(2,1)S(1)}, u32[]{:S(2)}, u32[]{:S(2)}) collective-permute-start(bf16[1024,512]{1,0:T(8,128)(2,1)S(1)} %copy-done.8), channel_id=1, source_target_pairs={{1,0},{2,1},{3,2},{4,3},{5,4},{6,5},{7,6},{8,7},{9,8},{10,9},{11,1... | collective-permute-start | bytes 3145736 | tf_op jit(solution)/shard_map/ppermute | solution.py:517
  23.6 15.4 %collective-permute-start.4 = (bf16[512,512]{1,0:T(8,128)(2,1)S(1)}, bf16[512,512]{1,0:T(8,128)(2,1)S(1)}, u32[]{:S(2)}, u32[]{:S(2)}) collective-permute-start(bf16[512,512]{1,0:T(8,128)(2,1)S(1)} %get-tuple-element.52.rest_0_), channel_id=1, source_target_pairs={{0,1},{1,2},{2,3},{3,4},{4,5},{5,6},{6,7},{7,8},{8,9},{9,10},{10,1... | collective-permute-start | bytes 1572872 | tf_op jit(solution)/shard_map/ppermute | solution.py:517
  34.7 6.1 %copy-start = (bf16[1,1,512,512]{3,2,1,0:T(8,128)(2,1)S(1)}, bf16[1,1,512,512]{3,2,1,0:T(8,128)(2,1)}, u32[]{:S(2)}) copy-start(bf16[1,1,512,512]{3,2,1,0:T(8,128)(2,1)} %param.11) | copy-start | bytes 1572868
  34.7 14.0 %collective-permute-start.2 = (bf16[512,512]{1,0:T(8,128)(2,1)S(1)}, bf16[512,512]{1,0:T(8,128)(2,1)S(1)}, u32[]{:S(2)}, u32[]{:S(2)}) collective-permute-start(bf16[512,512]{1,0:T(8,128)(2,1)S(1)} %get-tuple-element.49.own_high), channel_id=1, source_target_pairs={{0,128},{32,160},{64,192},{96,224},{128,0},{160,32},{192,64},{224,... | collective-permute-start | bytes 1572872 | tf_op jit(solution)/shard_map/ppermute | solution.py:514
  38.3 0.8 copy-start.4
  39.1 9.6 %copy-start.1 = (bf16[512,512]{1,0:T(8,128)(2,1)}, bf16[512,512]{1,0:T(8,128)(2,1)S(1)}, u32[]{:S(2)}) copy-start(bf16[512,512]{1,0:T(8,128)(2,1)S(1)} %get-tuple-element.54.rest_1_.row_high) | copy-start | bytes 1572868
  39.1 0.8 copy-start.6
  39.9 1.0 copy-start.5
  50.0 14.1 %collective-permute-start.5 = (bf16[512,512]{1,0:T(8,128)(2,1)S(1)}, bf16[512,512]{1,0:T(8,128)(2,1)S(1)}, u32[]{:S(2)}, u32[]{:S(2)}) collective-permute-start(bf16[512,512]{1,0:T(8,128)(2,1)S(1)} %shard_map.107), channel_id=1, source_target_pairs={{0,384},{32,416},{64,448},{96,480},{128,256},{160,288},{192,320},{... | collective-permute-start | bytes 1572872 | tf_op jit(solution)/shard_map/ppermute | solution.py:514
  53.4 0.8 copy-start.2
  54.2 0.8 copy-start.3
  64.1 0.8 copy-start.7
  69.5 8.1 %collective-permute-start.6 = (bf16[512,512]{1,0:T(8,128)(2,1)S(1)}, bf16[512,512]{1,0:T(8,128)(2,1)S(1)}, u32[]{:S(2)}, u32[]{:S(2)}) collective-permute-start(bf16[512,512]{1,0:T(8,128)(2,1)S(1)} %get-tuple-element.63.rest_1_), channel_id=1, source_target_pairs={{1,2},{2,1},{3,4},{4,3},{5,6},{6,5},{7,8},{8,7},{9,10},{10,9},{11,... | collective-permute-start | bytes 1572872 | tf_op jit(solution)/shard_map/ppermute | solution.py:517
  70.2 7.9 %collective-permute-start.7 = (bf16[512,512]{1,0:T(8,128)(2,1)S(1)}, bf16[512,512]{1,0:T(8,128)(2,1)S(1)}, u32[]{:S(2)}, u32[]{:S(2)}) collective-permute-start(bf16[512,512]{1,0:T(8,128)(2,1)S(1)} %get-tuple-element.63.rest_1_), channel_id=1, source_target_pairs={{0,1},{1,0},{2,3},{3,2},{4,5},{5,4},{6,7},{7,6},{8,9},{9,8},{10,11... | collective-permute-start | bytes 1572872 | tf_op jit(solution)/shard_map/ppermute | solution.py:517
  79.2 11.0 %collective-permute-start.8 = (bf16[512,512]{1,0:T(8,128)(2,1)S(1)}, bf16[512,512]{1,0:T(8,128)(2,1)S(1)}, u32[]{:S(2)}, u32[]{:S(2)}) collective-permute-start(bf16[512,512]{1,0:T(8,128)(2,1)S(1)} %get-tuple-element.68.rest_3_), channel_id=1, source_target_pairs={{1,2},{2,1},{3,4},{4,3},{5,6},{6,5},{7,8},{8,7},{9,10},{10,9},{11,... | collective-permute-start | bytes 1572872 | tf_op jit(solution)/shard_map/ppermute | solution.py:517
  79.9 10.7 %collective-permute-start.9 = (bf16[512,512]{1,0:T(8,128)(2,1)S(1)}, bf16[512,512]{1,0:T(8,128)(2,1)S(1)}, u32[]{:S(2)}, u32[]{:S(2)}) collective-permute-start(bf16[512,512]{1,0:T(8,128)(2,1)S(1)} %get-tuple-element.68.rest_3_), channel_id=1, source_target_pairs={{0,1},{1,0},{2,3},{3,2},{4,5},{5,4},{6,7},{7,6},{8,9},{9,8},{10,11... | collective-permute-start | bytes 1572872 | tf_op jit(solution)/shard_map/ppermute | solution.py:517
  91.7 10.6 %collective-permute-start.10 = (bf16[512,512]{1,0:T(8,128)(2,1)S(1)}, bf16[512,512]{1,0:T(8,128)(2,1)S(1)}, u32[]{:S(2)}, u32[]{:S(2)}) collective-permute-start(bf16[512,512]{1,0:T(8,128)(2,1)S(1)} %get-tuple-element.72.rest_5_), channel_id=1, source_target_pairs={{1,2},{2,1},{3,4},{4,3},{5,6},{6,5},{7,8},{8,7},{9,10},{10,9},{11,... | collective-permute-start | bytes 1572872 | tf_op jit(solution)/shard_map/ppermute | solution.py:517
  92.4 10.3 %collective-permute-start.11 = (bf16[512,512]{1,0:T(8,128)(2,1)S(1)}, bf16[512,512]{1,0:T(8,128)(2,1)S(1)}, u32[]{:S(2)}, u32[]{:S(2)}) collective-permute-start(bf16[512,512]{1,0:T(8,128)(2,1)S(1)} %get-tuple-element.72.rest_5_), channel_id=1, source_target_pairs={{0,1},{1,0},{2,3},{3,2},{4,5},{5,4},{6,7},{7,6},{8,9},{9,8},{10,11... | collective-permute-start | bytes 1572872 | tf_op jit(solution)/shard_map/ppermute | solution.py:517
  103.9 8.2 %collective-permute-start.13 = (bf16[512,512]{1,0:T(8,128)(2,1)S(1)}, bf16[512,512]{1,0:T(8,128)(2,1)S(1)}, u32[]{:S(2)}, u32[]{:S(2)}) collective-permute-start(bf16[512,512]{1,0:T(8,128)(2,1)S(1)} %get-tuple-element.76.rest_7_.high), channel_id=1, source_target_pairs={{0,1},{1,0},{2,3},{3,2},{4,5},{5,4},{6,7},{7,6},{8,9},{9,8},{10,11... | collective-permute-start | bytes 1572872 | tf_op jit(solution)/shard_map/ppermute | solution.py:517
  107.9 3.7 %collective-permute-start.12 = (bf16[512,256]{1,0:T(8,128)(2,1)S(1)}, bf16[512,256]{1,0:T(8,128)(2,1)S(1)}, u32[]{:S(2)}, u32[]{:S(2)}) collective-permute-start(bf16[512,256]{1,0:T(8,128)(2,1)S(1)} %get-tuple-element.79), channel_id=1, source_target_pairs={{1,2},{2,1},{3,4},{4,3},{5,6},{6,5},{7,8},{8,7},{9,10},{10,9},{11,... | collective-permute-start | bytes 786440 | tf_op jit(solution)/shard_map/ppermute | solution.py:517

commit v4 on v3

--- a/solution.py
+++ b/solution.py
@@ -14,7 +14,7 @@
 BAND = 32
 DAMP = 2.0**-14
 PEAK = 32
-GRANT = 52
+GRANT = 51
 epsilon = 1e-06
 
 f32, bf16 = jnp.float32, jnp.bfloat16
@@ -80,18 +80,19 @@
     top = over_bands(n, widest, jnp.zeros((8, cols), f32))
     peak = jnp.max(jnp.max(top, axis=0, keepdims=True), axis=1, keepdims=True)
     peak = jnp.where(peak > 0.0, peak, 1.0)
-    peaks = [*peaks, peak]
+    inverse = 1.0 / peak
 
     def products(at, sums):
-        mine = whole(newest, at) / peak
+        mine = whole(newest, at) * inverse
+        others = [whole(f, at) for f in fields[:-1]]
         return tuple(
-            s + jnp.sum(fold(whole(f, at) / p * mine), axis=0)
-            for s, f, p in zip(sums, fields, peaks, strict=True)
+            s + jnp.sum(fold(x * mine), axis=0) for s, x in zip(sums, [*others, mine], strict=True)
         )
 
     sums = over_bands(n, products, tuple(jnp.zeros((8, cols), f32) for _ in fields))
     k = len(fields) - 1
-    return in_lanes(k * (k + 1) // 2, [total(x) for x in sums]) + in_lanes(PEAK + k, [peak])
+    values = [total(x) / p for x, p in zip(sums[:-1], peaks, strict=True)] + [total(sums[-1])]
+    return in_lanes(k * (k + 1) // 2, values) + in_lanes(PEAK + k, [peak])
 
 
 def call(kernel, out, smem=1, loose=0, far=0, scratch=(), out_specs=None, grant=20):
@@ -264,58 +265,48 @@
 
 
 def segment_prefix_kernel(
-    place, whole_got, row_high, row_low, high_far, low_far, high, low, sems
+    place, whole_got, row_high, row_low, high_far, high, sem
 ):
     n = whole_got.shape[0]
 
     @pl.when(lax.rem(place[3], 2) == 0)
     def _():
         high[...] = row_high[...]
-        low[...] = row_low[...]
 
     @pl.when(lax.rem(place[3], 2) == 1)
     def _():
         for c in range(0, n, STEP):
             at = slice(c, c + STEP)
-            high[at, :], low[at, :] = split(chain((whole_got,), (row_high, row_low), c))
-
-    moves = [
-        pltpu.make_async_copy(high, high_far, sems.at[0]),
-        pltpu.make_async_copy(low, low_far, sems.at[1]),
-    ]
-    for move in moves:
-        move.start()
-    for move in moves:
-        move.wait()
+            high[at, :] = chain((whole_got,), (row_high, row_low), c).astype(bf16)
+
+    move = pltpu.make_async_copy(high, high_far, sem)
+    move.start()
+    move.wait()
 
 
 def segment_kernel(
-    place, ahead, high_far, low_far, edge_far, couplings_far, lifted_far,
+    place, ahead, high_far, edge_far, couplings_far, lifted_far,
     left, left_out, next_high, next_low,
-    high, low, edge, couplings, lifted, prefix, turned, turned_wide, sems,
+    high, edge, couplings, lifted, prefix, turned, turned_wide, sems,
 ):
     sizes = (place[1], place[2])
     n = ahead.shape[0]
-    pairs = (
-        (high_far, high), (low_far, low), (edge_far, edge),
-        (lifted_far, lifted), (couplings_far, couplings),
-    )
+    pairs = ((high_far, high), (edge_far, edge), (lifted_far, lifted), (couplings_far, couplings))
     moves = [pltpu.make_async_copy(*pair, sems.at[i]) for i, pair in enumerate(pairs)]
     for move in moves:
         move.start()
     moves[0].wait()
+
+    @pl.when(place[3] < ROW // 2)
+    def _():
+        prefix[...] = high[...]
+
+    @pl.when(place[3] >= ROW // 2)
+    def _():
+        for c in range(0, n, STEP):
+            prefix[c : c + STEP, :] = chain((ahead,), (high,), c).astype(bf16)
+
     moves[1].wait()
-
-    @pl.when(place[3] < ROW // 2)
-    def _():
-        prefix[...] = high[...]
-
-    @pl.when(place[3] >= ROW // 2)
-    def _():
-        for c in range(0, n, STEP):
-            prefix[c : c + STEP, :] = chain((ahead,), (high, low), c).astype(bf16)
-
-    moves[2].wait()
     for c in range(0, n, STEP):
         at = slice(c, c + STEP)
         value = edge[at, :] + wide_dot(edge[at, :].astype(bf16), prefix[...])
@@ -326,8 +317,8 @@
         block = turned_wide[at, :] + left_transposed_dot(prefix[:, at], turned[...])
         left[at, :] = block.astype(bf16)
         left_out[at, :] = block.astype(bf16)
+    moves[2].wait()
     moves[3].wait()
-    moves[4].wait()
     for c in range(0, n, STEP):
         at = slice(c, c + STEP)
         image = wide_dot(left[at, :], lifted[:n, :]) + wide_dot(left[at, :], lifted[n:, :])
@@ -380,29 +371,29 @@
         kept[...] = next_high[:, :half].astype(f32) + next_low[:, :half].astype(f32)
 
 
+def crossing(matrix, got, kept, inverse):
+    inner = jnp.zeros((1, 1), f32)
+    for c in range(0, matrix.shape[0], STEP):
+        at = slice(c, c + STEP)
+        inner += total(wide_dot(matrix[at, :], got[...]) * inverse * (kept[at, :] * inverse))
+    return 2.0 * inner
+
+
 def far_last_kernel(stats_in, far, got, kept, out):
-    n = far.shape[0]
-    peak = lane_entry(stats_in[...], PEAK + DAVIDSON)
-    inner = jnp.zeros((1, 1), f32)
-    for c in range(0, n, STEP):
-        at = slice(c, c + STEP)
-        inner += total(wide_dot(far[at, :], got[...]) / peak * (kept[at, :] / peak))
+    inverse = 1.0 / lane_entry(stats_in[...], PEAK + DAVIDSON)
     k = DAVIDSON + 1
-    out[...] = stats_in[...] + in_lanes(k * (k + 1) // 2, [2.0 * inner])
-
-
-def close_kernel(stats_in, near, field_a, partial, high, low, out):
-    n = near.shape[0]
-    peak = lane_entry(stats_in[...], PEAK + DAVIDSON)
-    inner = jnp.zeros((1, 1), f32)
-    for c in range(0, n, STEP):
-        at = slice(c, c + STEP)
-        image = partial[at, :] + wide_dot(near[at, :], field_a[...])
-        inner += total(image / peak * (whole((high, low), at) / peak))
+    out[...] = stats_in[...] + in_lanes(k * (k + 1) // 2, [crossing(far, got, kept, inverse)])
+
+
+def close_kernel(stats_in, near, got, kept, partial, high, low, out):
+    inverse = 1.0 / lane_entry(stats_in[...], PEAK + DAVIDSON)
+    inner = crossing(near, got, kept, inverse)
+    for c in range(0, near.shape[0], STEP):
+        at = slice(c, c + STEP)
+        inner += total(partial[at, :] * inverse * (whole((high, low), at) * inverse))
     k = DAVIDSON + 1
-    out[...] = jnp.broadcast_to(
-        stats_in[...] + in_lanes(k * (k + 1) // 2, [inner]), out.shape
-    )
+    sums = stats_in[...] + in_lanes(k * (k + 1) // 2, [inner])
+    out[...] = jnp.broadcast_to(sums, out.shape)
 
 
 def solve_kernel(sums, *rest):
@@ -550,35 +541,37 @@
         place, whole_high, whole_low, whole_got, near, row_high
     )
     ahead = seg_send(double_high, x_turn)
-    high, low = call(
+    high = call(
         segment_prefix_kernel,
-        (square, square),
-        out_specs=(HBM, HBM),
+        square,
+        out_specs=HBM,
         grant=GRANT,
-        scratch=[buffer(n, n), buffer(n, n), DMA((2,))],
+        scratch=[buffer(n, n), DMA],
     )(place, whole_got, row_high, row_low)
     left, left_out, *following = call(
         segment_kernel,
         (square, square, square, square),
-        far=5,
+        far=4,
         grant=GRANT,
         scratch=[
-            *[buffer(n, n)] * 2, *[buffer(n, n, f32)] * 2, buffer(2 * n, n), *[buffer(n, n)] * 2,
-            buffer(n, n, f32), DMA((5,)),
+            buffer(n, n), *[buffer(n, n, f32)] * 2, buffer(2 * n, n), *[buffer(n, n)] * 2,
+            buffer(n, n, f32), DMA((4,)),
         ],
-    )(place, ahead, high, low, edge_sym, couplings, lifted)
+    )(place, ahead, high, edge_sym, couplings, lifted)
     fields = [(field,), tuple(following)]
     for k in range(1, DAVIDSON + 1):
         high, low = fields[-1]
         last = k == DAVIDSON
-        field_a = op_send(high, near_swap)
+        field_a = op_send(sent if last else high, near_swap)
         field_b = op_send(sent if last else high, far_swap)
         partial, stats = call(functools.partial(local_kernel, k + 1), (wide, lanes), smem=0)(
             stats, left, right, *sum(fields, ())
         )
         if last:
             stats = call(far_last_kernel, lanes, smem=0)(stats, far, field_b, kept)
-            sums = call(close_kernel, spread, smem=0)(stats, near, field_a, partial, high, low)
+            sums = call(close_kernel, spread, smem=0)(
+                stats, near, field_a, kept, partial, high, low
+            )
             break
         partial = call(far_kernel, wide, smem=0)(partial, far, field_b)
         if k == DAVIDSON - 1:

time: 152 us -> 148 us (0.974)
  blocking collectives: 36.3 us -> 31.6 us
  starting transfers between devices: 43.7 us -> 46.9 us
  Pallas kernels: 36.7 us -> 33.9 us
  waiting for transfers between devices: 27.2 us -> 29.5 us
  local copies, waits for them, and re-layouts: 5.08 us -> 3.15 us
    all_to_all x1, blocking collectives: 36.3 us -> 31.6 us  [op_sum(): return lax.all_to_all(x[:, None], 'op', 0, 0)[:, 0]]
    ppermute x10, starting transfers between devices: 31.1 us -> 34.3 us  [op_send(): return lax.ppermute(x, 'op', route)]
    pallas_call x21, Pallas kernels: 36.7 us -> 33.9 us  [run(): pl.pallas_call(kernel, out_shape=out, in_specs=[SMEM] * smem + [VMEM] * (...]
    ppermute x4, waiting for transfers between devices: 27.2 us -> 29.5 us  [seg_send(): return lax.ppermute(x, 'seg', route)]
    unnamed x18 -> x10, local copies, waits for them, and re-layouts: 4.99 us -> 3.06 us
  transfers between devices with their start and end apart: 14 -> 14, of which waited for: 4 -> 4; matrix products, arithmetic and copies ran while one was open for 0% -> 0% of each run, Pallas kernels for 16% -> 15%
where the time goes in v4:
time: 148 us; the launch traced here: 147 us
  starting transfers between devices  46.9 us (32%)
  Pallas kernels  33.9 us (23%)
  blocking collectives  31.6 us (21%)
  waiting for transfers between devices  29.5 us (20%)
  local copies, waits for them, and re-layouts  3.15 us (2%)
  between operations  2.41 us (2%)
    ppermute x10, starting transfers between devices, op_send(): return lax.ppermute(x, 'op', route)  34.3 us
    pallas_call x21, Pallas kernels, run(): pl.pallas_call(kernel, out_shape=out, in_specs=[SMEM] * smem + [VMEM] * (...  33.9 us
    all_to_all x1, blocking collectives, op_sum(): return lax.all_to_all(x[:, None], 'op', 0, 0)[:, 0]  31.6 us
    ppermute x4, waiting for transfers between devices, seg_send(): return lax.ppermute(x, 'seg', route)  29.5 us
    ppermute x4, starting transfers between devices, seg_send(): return lax.ppermute(x, 'seg', route)  12.6 us
    unnamed x10, local copies, waits for them, and re-layouts  3.06 us
  transfers between devices with their start and end apart: 14, of which 4 were waited for; matrix products, arithmetic and copies ran while one was open for 0% of the time, Pallas kernels for 15%

profile of v4, /device:TPU:6, one launch (start us, length us, event | category | flops | bytes accessed | tf_op | source)
XLA Modules:
  0.0 147.5 jit_solution(9421862897948001414)
XLA Ops:
  0.6 3.5 %collective-permute-start = (bf16[512,512]{1,0:T(8,128)(2,1)}, bf16[512,512]{1,0:T(8,128)(2,1)S(1)}, u32[]{:S(2)}, u32[]{:S(2)}) collective-permute-start(bf16[512,512]{1,0:T(8,128)(2,1)} %bitcast.17), channel_id=1, source_target_pairs={{0,32},{32,0},{64,96},{96,64},{128,160},{160,128},{192,224},{224,1... | collective-permute-start | bytes 1572872 | tf_op jit(solution)/shard_map/ppermute | solution.py:505
  5.4 0.1 stack.15.place
  5.5 1.0 copy-done.1
  6.6 1.0 copy-done.2
  7.6 3.8 %shard_map.102 = (bf16[512,512]{1,0:T(8,128)(2,1)S(1)}, bf16[512,512]{1,0:T(8,128)(2,1)S(1)}, bf16[512,512]{1,0:T(8,128)(2,1)S(1)}, f32[1,128]{1,0:T(1,128)S(1)}...) custom-call(s32[5]{0:T(128)S(1)} %stack.15.place, bf16[512,512]{1,0:T(8,128)(2,1)S(1)} %bitcast.18, ...), custom_call_target="tpu_custom_call" | custom-call | flops 1 | bytes 1 | tf_op jit(solution)/shard_map/pallas_call | solution.py:100
  11.4 0.0 copy-start.4
  11.4 5.0 %collective-permute-done.got.transfer_got = bf16[512,512]{1,0:T(8,128)(2,1)S(1)} collective-permute-done((bf16[512,512]{1,0:T(8,128)(2,1)}, bf16[512,512]{1,0:T(8,128)(2,1)S(1)}, u32[]{:S(2)}, u32[]{:S(2)}) %collective-permute-start) | collective-permute-done | bytes 524320 | tf_op jit(solution)/shard_map/ppermute | solution.py:505
  16.4 1.0 shard_map.103
  17.4 4.9 %collective-permute-start.1 = (bf16[512,512]{1,0:T(8,128)(2,1)S(1)}, bf16[512,512]{1,0:T(8,128)(2,1)S(1)}, u32[]{:S(2)}, u32[]{:S(2)}) collective-permute-start(bf16[512,512]{1,0:T(8,128)(2,1)S(1)} %get-tuple-element.45.own_high), channel_id=1, source_target_pairs={{0,96},{32,64},{64,32},{96,0},{128,224},{160,192},{192,160},{224,1... | collective-permute-start | bytes 1572872 | tf_op jit(solution)/shard_map/ppermute | solution.py:505
  22.3 1.3 collective-permute-start.3
  23.6 3.1 %collective-permute-start.4 = (bf16[512,512]{1,0:T(8,128)(2,1)S(1)}, bf16[512,512]{1,0:T(8,128)(2,1)S(1)}, u32[]{:S(2)}, u32[]{:S(2)}) collective-permute-start(bf16[512,512]{1,0:T(8,128)(2,1)S(1)} %get-tuple-element.50.rest_0_), channel_id=1, source_target_pairs={{0,1},{1,2},{2,3},{3,4},{4,5},{5,6},{6,7},{7,8},{8,9},{9,10},{10,1... | collective-permute-start | bytes 1572872 | tf_op jit(solution)/shard_map/ppermute | solution.py:508
  26.7 6.7 %collective-permute-done.1.got.pair_got = bf16[512,512]{1,0:T(8,128)(2,1)S(1)} collective-permute-done((bf16[512,512]{1,0:T(8,128)(2,1)S(1)}, bf16[512,512]{1,0:T(8,128)(2,1)S(1)}, u32[]{:S(2)}, u32[]{:S(2)}) %collective-permute-start.1) | collective-permute-done | bytes 524320 | tf_op jit(solution)/shard_map/ppermute | solution.py:505
  33.4 1.3 shard_map.104
  34.7 0.0 copy-start
  34.7 2.9 %collective-permute-start.2 = (bf16[512,512]{1,0:T(8,128)(2,1)S(1)}, bf16[512,512]{1,0:T(8,128)(2,1)S(1)}, u32[]{:S(2)}, u32[]{:S(2)}) collective-permute-start(bf16[512,512]{1,0:T(8,128)(2,1)S(1)} %get-tuple-element.47.own_high), channel_id=1, source_target_pairs={{0,128},{32,160},{64,192},{96,224},{128,0},{160,32},{192,64},{224,... | collective-permute-start | bytes 1572872 | tf_op jit(solution)/shard_map/ppermute | solution.py:505
  37.6 0.6 shard_map.106
  38.2 0.0 collective-permute-done.4.below
  38.3 0.0 copy-start.3
  38.3 1.0 copy-done.3
  39.2 3.0 %shard_map.105 = (bf16[512,512]{1,0:T(8,128)(2,1)S(1)}, bf16[512,512]{1,0:T(8,128)(2,1)S(1)}, f32[512,512]{1,0:T(8,128)}) custom-call(s32[5]{0:T(128)S(1)} %stack.15.place, bf16[512,512]{1,0:T(8,128)(2,1)S(1)} %bitcast.15, bf16[1024,512]{1,0:T(8,128)(2,1)} %copy-done.3, bf16[512,512]{1,0:T(8,128)(2,1)S(1)} %collective-permute-done.4.below), custom_call_target="tpu_custom_call" | custom-call | flops 1 | bytes 1 | tf_op jit(solution)/shard_map/pallas_call | solution.py:100
  42.2 6.4 %collective-permute-done.2.got.whole_got = bf16[512,512]{1,0:T(8,128)(2,1)S(1)} collective-permute-done((bf16[512,512]{1,0:T(8,128)(2,1)S(1)}, bf16[512,512]{1,0:T(8,128)(2,1)S(1)}, u32[]{:S(2)}, u32[]{:S(2)}) %collective-permute-start.2) | collective-permute-done | bytes 524320 | tf_op jit(solution)/shard_map/ppermute | solution.py:505
  48.7 1.3 shard_map.107
  50.0 1.3 collective-permute-start.5
  51.3 1.4 shard_map.108.high_far
  52.7 11.4 %collective-permute-done.5.ahead = bf16[512,512]{1,0:T(8,128)(2,1)S(1)} collective-permute-done((bf16[512,512]{1,0:T(8,128)(2,1)S(1)}, bf16[512,512]{1,0:T(8,128)(2,1)S(1)}, u32[]{:S(2)}, u32[]{:S(2)}) %collective-permute-start.5) | collective-permute-done | bytes 524320 | tf_op jit(solution)/shard_map/ppermute | solution.py:505
  64.1 3.4 %shard_map.109 = (bf16[512,512]{1,0:T(8,128)(2,1)S(1)}, bf16[512,512]{1,0:T(8,128)(2,1)}, bf16[512,512]{1,0:T(8,128)(2,1)S(1)}, bf16[512,512]{1,0:T(8,128)(2,1)S(1)}) custom-call(s32[5]{0:T(128)S(1)} %stack.15.place, bf16[512,512]{1,0:T(8,128)(2,1)S(1)} %collective-permute-done.5.ahead, bf16[512,512]{1,0:T(8,128)(2,1)S(1)} %shard_map.108.high_far, ...), custom_call_target="tpu_custom_call" | custom-call | flops 1 | bytes 1 | tf_op jit(solution)/shard_map/pallas_call | solution.py:100
  67.6 0.7 collective-permute-start.6
  68.3 5.2 %collective-permute-start.7 = (bf16[512,512]{1,0:T(8,128)(2,1)S(1)}, bf16[512,512]{1,0:T(8,128)(2,1)S(1)}, u32[]{:S(2)}, u32[]{:S(2)}) collective-permute-start(bf16[512,512]{1,0:T(8,128)(2,1)S(1)} %get-tuple-element.59.rest_1_), channel_id=1, source_target_pairs={{0,1},{1,0},{2,3},{3,2},{4,5},{5,4},{6,7},{7,6},{8,9},{9,8},{10,11... | collective-permute-start | bytes 1572872 | tf_op jit(solution)/shard_map/ppermute | solution.py:508
  73.4 2.2 %shard_map.110 = (f32[512,512]{1,0:T(8,128)S(1)}, f32[1,128]{1,0:T(1,128)S(1)}) custom-call(f32[1,128]{1,0:T(1,128)S(1)} %get-tuple-element.43.stats_in, bf16[512,512]{1,0:T(8,128)(2,1)S(1)} %get-tuple-element.57.left, bf16[512,512]{1,0:T(8,128)(2,1)S(1)} %get-tuple-element.58.right, bf16[512,512]{1,0:T(8,128)(2,1)S(1)} %get-tuple-element.50.rest_0_, ...), custom_call_target="tpu_custom_call" | custom-call | flops 1 | bytes 1 | tf_op jit(solution)/shard_map/pallas_call | solution.py:100
  75.7 0.4 shard_map.111.partial
  76.1 1.1 shard_map.112
  77.2 0.7 collective-permute-start.8
  77.9 7.7 %collective-permute-start.9 = (bf16[512,512]{1,0:T(8,128)(2,1)S(1)}, bf16[512,512]{1,0:T(8,128)(2,1)S(1)}, u32[]{:S(2)}, u32[]{:S(2)}) collective-permute-start(bf16[512,512]{1,0:T(8,128)(2,1)S(1)} %get-tuple-element.64.rest_3_), channel_id=1, source_target_pairs={{0,1},{1,0},{2,3},{3,2},{4,5},{5,4},{6,7},{7,6},{8,9},{9,8},{10,11... | collective-permute-start | bytes 1572872 | tf_op jit(solution)/shard_map/ppermute | solution.py:508
  85.6 2.5 %shard_map.113 = (f32[512,512]{1,0:T(8,128)S(1)}, f32[1,128]{1,0:T(1,128)S(1)}) custom-call(f32[1,128]{1,0:T(1,128)S(1)} %get-tuple-element.61.stats_in, bf16[512,512]{1,0:T(8,128)(2,1)S(1)} %get-tuple-element.57.left, bf16[512,512]{1,0:T(8,128)(2,1)S(1)} %get-tuple-element.58.right, bf16[512,512]{1,0:T(8,128)(2,1)S(1)} %get-tuple-element.50.rest_0_, ...), custom_call_target="tpu_custom_call" | custom-call | flops 1 | bytes 1 | tf_op jit(solution)/shard_map/pallas_call | solution.py:100
  88.1 0.4 shard_map.114.partial
  88.6 1.1 shard_map.115
  89.7 0.7 collective-permute-start.10
  90.4 7.1 %collective-permute-start.11 = (bf16[512,512]{1,0:T(8,128)(2,1)S(1)}, bf16[512,512]{1,0:T(8,128)(2,1)S(1)}, u32[]{:S(2)}, u32[]{:S(2)}) collective-permute-start(bf16[512,512]{1,0:T(8,128)(2,1)S(1)} %get-tuple-element.68.rest_5_), channel_id=1, source_target_pairs={{0,1},{1,0},{2,3},{3,2},{4,5},{5,4},{6,7},{7,6},{8,9},{9,8},{10,11... | collective-permute-start | bytes 1572872 | tf_op jit(solution)/shard_map/ppermute | solution.py:508
  97.5 2.6 %shard_map.116 = (f32[512,512]{1,0:T(8,128)S(1)}, f32[1,128]{1,0:T(1,128)S(1)}) custom-call(f32[1,128]{1,0:T(1,128)S(1)} %get-tuple-element.66.stats_in, bf16[512,512]{1,0:T(8,128)(2,1)S(1)} %get-tuple-element.57.left, bf16[512,512]{1,0:T(8,128)(2,1)S(1)} %get-tuple-element.58.right, bf16[512,512]{1,0:T(8,128)(2,1)S(1)} %get-tuple-element.50.rest_0_, ...), custom_call_target="tpu_custom_call" | custom-call | flops 1 | bytes 1 | tf_op jit(solution)/shard_map/pallas_call | solution.py:100
  100.1 0.4 shard_map.117.partial
  100.6 1.2 shard_map.118
  101.7 0.7 collective-permute-start.12
  102.4 7.2 %collective-permute-start.13 = (bf16[512,256]{1,0:T(8,128)(2,1)S(1)}, bf16[512,256]{1,0:T(8,128)(2,1)S(1)}, u32[]{:S(2)}, u32[]{:S(2)}) collective-permute-start(bf16[512,256]{1,0:T(8,128)(2,1)S(1)} %get-tuple-element.75), channel_id=1, source_target_pairs={{0,1},{1,0},{2,3},{3,2},{4,5},{5,4},{6,7},{7,6},{8,9},{9,8},{10,11... | collective-permute-start | bytes 786440 | tf_op jit(solution)/shard_map/ppermute | solution.py:508
  109.6 2.8 %shard_map.119 = (f32[512,512]{1,0:T(8,128)S(1)}, f32[1,128]{1,0:T(1,128)S(1)}) custom-call(f32[1,128]{1,0:T(1,128)S(1)} %get-tuple-element.70.stats_in, bf16[512,512]{1,0:T(8,128)(2,1)S(1)} %get-tuple-element.57.left, bf16[512,512]{1,0:T(8,128)(2,1)S(1)} %get-tuple-element.58.right, bf16[512,512]{1,0:T(8,128)(2,1)S(1)} %get-tuple-element.50.rest_0_, ...), custom_call_target="tpu_custom_call" | custom-call | flops 1 | bytes 1 | tf_op jit(solution)/shard_map/pallas_call | solution.py:100
  112.4 0.4 shard_map.120.stats_in
  112.8 0.7 shard_map.121
  113.5 31.6 %all_to_all.5 = f32[32,1,128]{2,1,0:T(1,128)S(1)} all-to-all(f32[32,1,128]{2,1,0:T(1,128)S(1)} %bitcast.20), channel_id=1, replica_groups=mesh['seg'=16,'op'=32] {'op'}, dimensions={0} | all-to-all | bytes 32768 | tf_op jit(solution)/shard_map/all_to_all | solution.py:511
  145.1 2.2 %shard_map.122 = (f32[512,512]{1,0:T(8,128)}, f32[1]{0:T(128)}, f32[1]{0:T(128)}) custom-call(f32[32,128]{1,0:T(8,128)S(1)} %bitcast.19, bf16[512,512]{1,0:T(8,128)(2,1)S(1)} %get-tuple-element.50.rest_0_, bf16[512,512]{1,0:T(8,128)(2,1)S(1)} %get-tuple-element.59.rest_1_, bf16[512,512]{1,0:T(8,128)(2,1)S(1)} %get-tuple-element.60.rest_2_, ...), custom_call_target="tpu_custom_call" | custom-call | flops 1 | bytes 1 | tf_op jit(solution)/shard_map/pallas_call | solution.py:100
  (13 shorter events, 0.0 us)
Async XLA Ops:
  0.6 15.8 %collective-permute-start = (bf16[512,512]{1,0:T(8,128)(2,1)}, bf16[512,512]{1,0:T(8,128)(2,1)S(1)}, u32[]{:S(2)}, u32[]{:S(2)}) collective-permute-start(bf16[512,512]{1,0:T(8,128)(2,1)} %bitcast.17), channel_id=1, source_target_pairs={{0,32},{32,0},{64,96},{96,64},{128,160},{160,128},{192,224},{224,1... | collective-permute-start | bytes 1572872 | tf_op jit(solution)/shard_map/ppermute | solution.py:505
  5.5 1.0 copy-start.1
  6.6 1.0 copy-start.2
  11.4 10.9 %copy-start.4 = (bf16[1024,512]{1,0:T(8,128)(2,1)S(1)}, bf16[1024,512]{1,0:T(8,128)(2,1)}, u32[]{:S(2)}) copy-start(bf16[1024,512]{1,0:T(8,128)(2,1)} %get-tuple-element.49) | copy-start | bytes 3145732
  17.4 16.0 %collective-permute-start.1 = (bf16[512,512]{1,0:T(8,128)(2,1)S(1)}, bf16[512,512]{1,0:T(8,128)(2,1)S(1)}, u32[]{:S(2)}, u32[]{:S(2)}) collective-permute-start(bf16[512,512]{1,0:T(8,128)(2,1)S(1)} %get-tuple-element.45.own_high), channel_id=1, source_target_pairs={{0,96},{32,64},{64,32},{96,0},{128,224},{160,192},{192,160},{224,1... | collective-permute-start | bytes 1572872 | tf_op jit(solution)/shard_map/ppermute | solution.py:505
  22.3 15.9 %collective-permute-start.3 = (bf16[1024,512]{1,0:T(8,128)(2,1)S(1)}, bf16[1024,512]{1,0:T(8,128)(2,1)S(1)}, u32[]{:S(2)}, u32[]{:S(2)}) collective-permute-start(bf16[1024,512]{1,0:T(8,128)(2,1)S(1)} %copy-done.4), channel_id=1, source_target_pairs={{1,0},{2,1},{3,2},{4,3},{5,4},{6,5},{7,6},{8,7},{9,8},{10,9},{11,1... | collective-permute-start | bytes 3145736 | tf_op jit(solution)/shard_map/ppermute | solution.py:508
  23.6 14.6 %collective-permute-start.4 = (bf16[512,512]{1,0:T(8,128)(2,1)S(1)}, bf16[512,512]{1,0:T(8,128)(2,1)S(1)}, u32[]{:S(2)}, u32[]{:S(2)}) collective-permute-start(bf16[512,512]{1,0:T(8,128)(2,1)S(1)} %get-tuple-element.50.rest_0_), channel_id=1, source_target_pairs={{0,1},{1,2},{2,3},{3,4},{4,5},{5,6},{6,7},{7,8},{8,9},{9,10},{10,1... | collective-permute-start | bytes 1572872 | tf_op jit(solution)/shard_map/ppermute | solution.py:508
  34.7 4.5 %copy-start = (bf16[1,1,512,512]{3,2,1,0:T(8,128)(2,1)S(1)}, bf16[1,1,512,512]{3,2,1,0:T(8,128)(2,1)}, u32[]{:S(2)}) copy-start(bf16[1,1,512,512]{3,2,1,0:T(8,128)(2,1)} %param.11) | copy-start | bytes 1572868
  34.7 14.0 %collective-permute-start.2 = (bf16[512,512]{1,0:T(8,128)(2,1)S(1)}, bf16[512,512]{1,0:T(8,128)(2,1)S(1)}, u32[]{:S(2)}, u32[]{:S(2)}) collective-permute-start(bf16[512,512]{1,0:T(8,128)(2,1)S(1)} %get-tuple-element.47.own_high), channel_id=1, source_target_pairs={{0,128},{32,160},{64,192},{96,224},{128,0},{160,32},{192,64},{224,... | collective-permute-start | bytes 1572872 | tf_op jit(solution)/shard_map/ppermute | solution.py:505
  38.3 1.0 copy-start.3
  50.0 14.1 %collective-permute-start.5 = (bf16[512,512]{1,0:T(8,128)(2,1)S(1)}, bf16[512,512]{1,0:T(8,128)(2,1)S(1)}, u32[]{:S(2)}, u32[]{:S(2)}) collective-permute-start(bf16[512,512]{1,0:T(8,128)(2,1)S(1)} %shard_map.107), channel_id=1, source_target_pairs={{0,384},{32,416},{64,448},{96,480},{128,256},{160,288},{192,320},{... | collective-permute-start | bytes 1572872 | tf_op jit(solution)/shard_map/ppermute | solution.py:505
  67.6 8.1 %collective-permute-start.6 = (bf16[512,512]{1,0:T(8,128)(2,1)S(1)}, bf16[512,512]{1,0:T(8,128)(2,1)S(1)}, u32[]{:S(2)}, u32[]{:S(2)}) collective-permute-start(bf16[512,512]{1,0:T(8,128)(2,1)S(1)} %get-tuple-element.59.rest_1_), channel_id=1, source_target_pairs={{1,2},{2,1},{3,4},{4,3},{5,6},{6,5},{7,8},{8,7},{9,10},{10,9},{11,... | collective-permute-start | bytes 1572872 | tf_op jit(solution)/shard_map/ppermute | solution.py:508
  68.3 7.8 %collective-permute-start.7 = (bf16[512,512]{1,0:T(8,128)(2,1)S(1)}, bf16[512,512]{1,0:T(8,128)(2,1)S(1)}, u32[]{:S(2)}, u32[]{:S(2)}) collective-permute-start(bf16[512,512]{1,0:T(8,128)(2,1)S(1)} %get-tuple-element.59.rest_1_), channel_id=1, source_target_pairs={{0,1},{1,0},{2,3},{3,2},{4,5},{5,4},{6,7},{7,6},{8,9},{9,8},{10,11... | collective-permute-start | bytes 1572872 | tf_op jit(solution)/shard_map/ppermute | solution.py:508
  77.2 10.9 %collective-permute-start.8 = (bf16[512,512]{1,0:T(8,128)(2,1)S(1)}, bf16[512,512]{1,0:T(8,128)(2,1)S(1)}, u32[]{:S(2)}, u32[]{:S(2)}) collective-permute-start(bf16[512,512]{1,0:T(8,128)(2,1)S(1)} %get-tuple-element.64.rest_3_), channel_id=1, source_target_pairs={{1,2},{2,1},{3,4},{4,3},{5,6},{6,5},{7,8},{8,7},{9,10},{10,9},{11,... | collective-permute-start | bytes 1572872 | tf_op jit(solution)/shard_map/ppermute | solution.py:508
  77.9 10.7 %collective-permute-start.9 = (bf16[512,512]{1,0:T(8,128)(2,1)S(1)}, bf16[512,512]{1,0:T(8,128)(2,1)S(1)}, u32[]{:S(2)}, u32[]{:S(2)}) collective-permute-start(bf16[512,512]{1,0:T(8,128)(2,1)S(1)} %get-tuple-element.64.rest_3_), channel_id=1, source_target_pairs={{0,1},{1,0},{2,3},{3,2},{4,5},{5,4},{6,7},{7,6},{8,9},{9,8},{10,11... | collective-permute-start | bytes 1572872 | tf_op jit(solution)/shard_map/ppermute | solution.py:508
  89.7 10.4 %collective-permute-start.10 = (bf16[512,512]{1,0:T(8,128)(2,1)S(1)}, bf16[512,512]{1,0:T(8,128)(2,1)S(1)}, u32[]{:S(2)}, u32[]{:S(2)}) collective-permute-start(bf16[512,512]{1,0:T(8,128)(2,1)S(1)} %get-tuple-element.68.rest_5_), channel_id=1, source_target_pairs={{1,2},{2,1},{3,4},{4,3},{5,6},{6,5},{7,8},{8,7},{9,10},{10,9},{11,... | collective-permute-start | bytes 1572872 | tf_op jit(solution)/shard_map/ppermute | solution.py:508
  90.4 10.2 %collective-permute-start.11 = (bf16[512,512]{1,0:T(8,128)(2,1)S(1)}, bf16[512,512]{1,0:T(8,128)(2,1)S(1)}, u32[]{:S(2)}, u32[]{:S(2)}) collective-permute-start(bf16[512,512]{1,0:T(8,128)(2,1)S(1)} %get-tuple-element.68.rest_5_), channel_id=1, source_target_pairs={{0,1},{1,0},{2,3},{3,2},{4,5},{5,4},{6,7},{7,6},{8,9},{9,8},{10,11... | collective-permute-start | bytes 1572872 | tf_op jit(solution)/shard_map/ppermute | solution.py:508
  101.7 10.7 %collective-permute-start.12 = (bf16[512,256]{1,0:T(8,128)(2,1)S(1)}, bf16[512,256]{1,0:T(8,128)(2,1)S(1)}, u32[]{:S(2)}, u32[]{:S(2)}) collective-permute-start(bf16[512,256]{1,0:T(8,128)(2,1)S(1)} %get-tuple-element.75), channel_id=1, source_target_pairs={{1,2},{2,1},{3,4},{4,3},{5,6},{6,5},{7,8},{8,7},{9,10},{10,9},{11,... | collective-permute-start | bytes 786440 | tf_op jit(solution)/shard_map/ppermute | solution.py:508
  102.4 10.4 %collective-permute-start.13 = (bf16[512,256]{1,0:T(8,128)(2,1)S(1)}, bf16[512,256]{1,0:T(8,128)(2,1)S(1)}, u32[]{:S(2)}, u32[]{:S(2)}) collective-permute-start(bf16[512,256]{1,0:T(8,128)(2,1)S(1)} %get-tuple-element.75), channel_id=1, source_target_pairs={{0,1},{1,0},{2,3},{3,2},{4,5},{5,4},{6,7},{7,6},{8,9},{9,8},{10,11... | collective-permute-start | bytes 786440 | tf_op jit(solution)/shard_map/ppermute | solution.py:508

commit v5 on v4

--- a/solution.py
+++ b/solution.py
@@ -508,7 +508,8 @@
         return lax.ppermute(x, "op", route)
 
     def op_sum(x):
-        return lax.all_to_all(x[:, None], "op", 0, 0)[:, 0]
+        order = [*range(sectors // 2, sectors), *range(sectors // 2)]
+        return lax.all_to_all(x[:, None], "op", 0, 0, axis_index_groups=[order])[:, 0]
 
     transfer_got = seg_send(transfer, y_pair)
     held, field, right, stats, bundle, edge_sym, lifted = call(

time: 148 us -> 140 us (0.946)
  blocking collectives: 31.6 us -> 23.8 us
    all_to_all x1, blocking collectives: 31.6 us -> 23.8 us  [op_sum(): lax.all_to_all(x[:, None], 'op', 0, 0, axis_index_groups=[order])[:, 0]]
  transfers between devices with their start and end apart: 14 -> 14, of which waited for: 4 -> 4; matrix products, arithmetic and copies ran while one was open for 0% -> 0% of each run, Pallas kernels for 15% -> 16%
where the time goes in v5:
time: 140 us
  starting transfers between devices  46.9 us (34%)
  Pallas kernels  33.9 us (24%)
  waiting for transfers between devices  29.5 us (21%)
  blocking collectives  23.8 us (17%)
  local copies, waits for them, and re-layouts  3.15 us (2%)
  between operations  2.41 us (2%)
    ppermute x10, starting transfers between devices, op_send(): return lax.ppermute(x, 'op', route)  34.3 us
    pallas_call x21, Pallas kernels, run(): pl.pallas_call(kernel, out_shape=out, in_specs=[SMEM] * smem + [VMEM] * (...  33.9 us
    ppermute x4, waiting for transfers between devices, seg_send(): return lax.ppermute(x, 'seg', route)  29.5 us
    all_to_all x1, blocking collectives, op_sum(): lax.all_to_all(x[:, None], 'op', 0, 0, axis_index_groups=[order])[:, 0]  23.8 us
    ppermute x4, starting transfers between devices, seg_send(): return lax.ppermute(x, 'seg', route)  12.6 us
    unnamed x10, local copies, waits for them, and re-layouts  3.06 us
  transfers between devices with their start and end apart: 14, of which 4 were waited for; matrix products, arithmetic and copies ran while one was open for 0% of the time, Pallas kernels for 16%

profile of v5, /device:TPU:6, one launch (start us, length us, event | category | flops | bytes accessed | tf_op | source)
XLA Modules:
  0.0 139.7 jit_solution(17039515337331007918)
XLA Ops:
  0.6 3.5 %collective-permute-start = (bf16[512,512]{1,0:T(8,128)(2,1)}, bf16[512,512]{1,0:T(8,128)(2,1)S(1)}, u32[]{:S(2)}, u32[]{:S(2)}) collective-permute-start(bf16[512,512]{1,0:T(8,128)(2,1)} %bitcast.17), channel_id=1, source_target_pairs={{0,32},{32,0},{64,96},{96,64},{128,160},{160,128},{192,224},{224,1... | collective-permute-start | bytes 1572872 | tf_op jit(solution)/shard_map/ppermute | solution.py:505
  5.4 0.1 stack.15.place
  5.5 1.0 copy-done.1
  6.6 1.0 copy-done.2
  7.6 3.8 %shard_map.102 = (bf16[512,512]{1,0:T(8,128)(2,1)S(1)}, bf16[512,512]{1,0:T(8,128)(2,1)S(1)}, bf16[512,512]{1,0:T(8,128)(2,1)S(1)}, f32[1,128]{1,0:T(1,128)S(1)}...) custom-call(s32[5]{0:T(128)S(1)} %stack.15.place, bf16[512,512]{1,0:T(8,128)(2,1)S(1)} %bitcast.18, ...), custom_call_target="tpu_custom_call" | custom-call | flops 1 | bytes 1 | tf_op jit(solution)/shard_map/pallas_call | solution.py:100
  11.4 0.0 copy-start.4
  11.4 5.0 %collective-permute-done.got.transfer_got = bf16[512,512]{1,0:T(8,128)(2,1)S(1)} collective-permute-done((bf16[512,512]{1,0:T(8,128)(2,1)}, bf16[512,512]{1,0:T(8,128)(2,1)S(1)}, u32[]{:S(2)}, u32[]{:S(2)}) %collective-permute-start) | collective-permute-done | bytes 524320 | tf_op jit(solution)/shard_map/ppermute | solution.py:505
  16.4 1.0 shard_map.103
  17.4 4.9 %collective-permute-start.1 = (bf16[512,512]{1,0:T(8,128)(2,1)S(1)}, bf16[512,512]{1,0:T(8,128)(2,1)S(1)}, u32[]{:S(2)}, u32[]{:S(2)}) collective-permute-start(bf16[512,512]{1,0:T(8,128)(2,1)S(1)} %get-tuple-element.45.own_high), channel_id=1, source_target_pairs={{0,96},{32,64},{64,32},{96,0},{128,224},{160,192},{192,160},{224,1... | collective-permute-start | bytes 1572872 | tf_op jit(solution)/shard_map/ppermute | solution.py:505
  22.3 1.3 collective-permute-start.3
  23.6 3.1 %collective-permute-start.4 = (bf16[512,512]{1,0:T(8,128)(2,1)S(1)}, bf16[512,512]{1,0:T(8,128)(2,1)S(1)}, u32[]{:S(2)}, u32[]{:S(2)}) collective-permute-start(bf16[512,512]{1,0:T(8,128)(2,1)S(1)} %get-tuple-element.50.rest_0_), channel_id=1, source_target_pairs={{0,1},{1,2},{2,3},{3,4},{4,5},{5,6},{6,7},{7,8},{8,9},{9,10},{10,1... | collective-permute-start | bytes 1572872 | tf_op jit(solution)/shard_map/ppermute | solution.py:508
  26.7 6.7 %collective-permute-done.1.got.pair_got = bf16[512,512]{1,0:T(8,128)(2,1)S(1)} collective-permute-done((bf16[512,512]{1,0:T(8,128)(2,1)S(1)}, bf16[512,512]{1,0:T(8,128)(2,1)S(1)}, u32[]{:S(2)}, u32[]{:S(2)}) %collective-permute-start.1) | collective-permute-done | bytes 524320 | tf_op jit(solution)/shard_map/ppermute | solution.py:505
  33.4 1.3 shard_map.104
  34.7 0.0 copy-start
  34.7 2.9 %collective-permute-start.2 = (bf16[512,512]{1,0:T(8,128)(2,1)S(1)}, bf16[512,512]{1,0:T(8,128)(2,1)S(1)}, u32[]{:S(2)}, u32[]{:S(2)}) collective-permute-start(bf16[512,512]{1,0:T(8,128)(2,1)S(1)} %get-tuple-element.47.own_high), channel_id=1, source_target_pairs={{0,128},{32,160},{64,192},{96,224},{128,0},{160,32},{192,64},{224,... | collective-permute-start | bytes 1572872 | tf_op jit(solution)/shard_map/ppermute | solution.py:505
  37.6 0.6 shard_map.106
  38.2 0.0 collective-permute-done.4.below
  38.3 0.0 copy-start.3
  38.3 1.0 copy-done.3
  39.2 3.0 %shard_map.105 = (bf16[512,512]{1,0:T(8,128)(2,1)S(1)}, bf16[512,512]{1,0:T(8,128)(2,1)S(1)}, f32[512,512]{1,0:T(8,128)}) custom-call(s32[5]{0:T(128)S(1)} %stack.15.place, bf16[512,512]{1,0:T(8,128)(2,1)S(1)} %bitcast.15, bf16[1024,512]{1,0:T(8,128)(2,1)} %copy-done.3, bf16[512,512]{1,0:T(8,128)(2,1)S(1)} %collective-permute-done.4.below), custom_call_target="tpu_custom_call" | custom-call | flops 1 | bytes 1 | tf_op jit(solution)/shard_map/pallas_call | solution.py:100
  42.2 6.4 %collective-permute-done.2.got.whole_got = bf16[512,512]{1,0:T(8,128)(2,1)S(1)} collective-permute-done((bf16[512,512]{1,0:T(8,128)(2,1)S(1)}, bf16[512,512]{1,0:T(8,128)(2,1)S(1)}, u32[]{:S(2)}, u32[]{:S(2)}) %collective-permute-start.2) | collective-permute-done | bytes 524320 | tf_op jit(solution)/shard_map/ppermute | solution.py:505
  48.7 1.3 shard_map.107
  50.0 1.3 collective-permute-start.5
  51.3 1.4 shard_map.108.high_far
  52.7 11.4 %collective-permute-done.5.ahead = bf16[512,512]{1,0:T(8,128)(2,1)S(1)} collective-permute-done((bf16[512,512]{1,0:T(8,128)(2,1)S(1)}, bf16[512,512]{1,0:T(8,128)(2,1)S(1)}, u32[]{:S(2)}, u32[]{:S(2)}) %collective-permute-start.5) | collective-permute-done | bytes 524320 | tf_op jit(solution)/shard_map/ppermute | solution.py:505
  64.1 3.4 %shard_map.109 = (bf16[512,512]{1,0:T(8,128)(2,1)S(1)}, bf16[512,512]{1,0:T(8,128)(2,1)}, bf16[512,512]{1,0:T(8,128)(2,1)S(1)}, bf16[512,512]{1,0:T(8,128)(2,1)S(1)}) custom-call(s32[5]{0:T(128)S(1)} %stack.15.place, bf16[512,512]{1,0:T(8,128)(2,1)S(1)} %collective-permute-done.5.ahead, bf16[512,512]{1,0:T(8,128)(2,1)S(1)} %shard_map.108.high_far, ...), custom_call_target="tpu_custom_call" | custom-call | flops 1 | bytes 1 | tf_op jit(solution)/shard_map/pallas_call | solution.py:100
  67.6 0.7 collective-permute-start.6
  68.3 5.2 %collective-permute-start.7 = (bf16[512,512]{1,0:T(8,128)(2,1)S(1)}, bf16[512,512]{1,0:T(8,128)(2,1)S(1)}, u32[]{:S(2)}, u32[]{:S(2)}) collective-permute-start(bf16[512,512]{1,0:T(8,128)(2,1)S(1)} %get-tuple-element.59.rest_1_), channel_id=1, source_target_pairs={{0,1},{1,0},{2,3},{3,2},{4,5},{5,4},{6,7},{7,6},{8,9},{9,8},{10,11... | collective-permute-start | bytes 1572872 | tf_op jit(solution)/shard_map/ppermute | solution.py:508
  73.4 2.2 %shard_map.110 = (f32[512,512]{1,0:T(8,128)S(1)}, f32[1,128]{1,0:T(1,128)S(1)}) custom-call(f32[1,128]{1,0:T(1,128)S(1)} %get-tuple-element.43.stats_in, bf16[512,512]{1,0:T(8,128)(2,1)S(1)} %get-tuple-element.57.left, bf16[512,512]{1,0:T(8,128)(2,1)S(1)} %get-tuple-element.58.right, bf16[512,512]{1,0:T(8,128)(2,1)S(1)} %get-tuple-element.50.rest_0_, ...), custom_call_target="tpu_custom_call" | custom-call | flops 1 | bytes 1 | tf_op jit(solution)/shard_map/pallas_call | solution.py:100
  75.7 0.4 shard_map.111.partial
  76.1 1.1 shard_map.112
  77.2 0.7 collective-permute-start.8
  77.9 7.7 %collective-permute-start.9 = (bf16[512,512]{1,0:T(8,128)(2,1)S(1)}, bf16[512,512]{1,0:T(8,128)(2,1)S(1)}, u32[]{:S(2)}, u32[]{:S(2)}) collective-permute-start(bf16[512,512]{1,0:T(8,128)(2,1)S(1)} %get-tuple-element.64.rest_3_), channel_id=1, source_target_pairs={{0,1},{1,0},{2,3},{3,2},{4,5},{5,4},{6,7},{7,6},{8,9},{9,8},{10,11... | collective-permute-start | bytes 1572872 | tf_op jit(solution)/shard_map/ppermute | solution.py:508
  85.6 2.5 %shard_map.113 = (f32[512,512]{1,0:T(8,128)S(1)}, f32[1,128]{1,0:T(1,128)S(1)}) custom-call(f32[1,128]{1,0:T(1,128)S(1)} %get-tuple-element.61.stats_in, bf16[512,512]{1,0:T(8,128)(2,1)S(1)} %get-tuple-element.57.left, bf16[512,512]{1,0:T(8,128)(2,1)S(1)} %get-tuple-element.58.right, bf16[512,512]{1,0:T(8,128)(2,1)S(1)} %get-tuple-element.50.rest_0_, ...), custom_call_target="tpu_custom_call" | custom-call | flops 1 | bytes 1 | tf_op jit(solution)/shard_map/pallas_call | solution.py:100
  88.1 0.4 shard_map.114.partial
  88.6 1.1 shard_map.115
  89.7 0.7 collective-permute-start.10
  90.4 7.1 %collective-permute-start.11 = (bf16[512,512]{1,0:T(8,128)(2,1)S(1)}, bf16[512,512]{1,0:T(8,128)(2,1)S(1)}, u32[]{:S(2)}, u32[]{:S(2)}) collective-permute-start(bf16[512,512]{1,0:T(8,128)(2,1)S(1)} %get-tuple-element.68.rest_5_), channel_id=1, source_target_pairs={{0,1},{1,0},{2,3},{3,2},{4,5},{5,4},{6,7},{7,6},{8,9},{9,8},{10,11... | collective-permute-start | bytes 1572872 | tf_op jit(solution)/shard_map/ppermute | solution.py:508
  97.5 2.6 %shard_map.116 = (f32[512,512]{1,0:T(8,128)S(1)}, f32[1,128]{1,0:T(1,128)S(1)}) custom-call(f32[1,128]{1,0:T(1,128)S(1)} %get-tuple-element.66.stats_in, bf16[512,512]{1,0:T(8,128)(2,1)S(1)} %get-tuple-element.57.left, bf16[512,512]{1,0:T(8,128)(2,1)S(1)} %get-tuple-element.58.right, bf16[512,512]{1,0:T(8,128)(2,1)S(1)} %get-tuple-element.50.rest_0_, ...), custom_call_target="tpu_custom_call" | custom-call | flops 1 | bytes 1 | tf_op jit(solution)/shard_map/pallas_call | solution.py:100
  100.1 0.4 shard_map.117.partial
  100.6 1.2 shard_map.118
  101.7 0.7 collective-permute-start.12
  102.4 7.2 %collective-permute-start.13 = (bf16[512,256]{1,0:T(8,128)(2,1)S(1)}, bf16[512,256]{1,0:T(8,128)(2,1)S(1)}, u32[]{:S(2)}, u32[]{:S(2)}) collective-permute-start(bf16[512,256]{1,0:T(8,128)(2,1)S(1)} %get-tuple-element.75), channel_id=1, source_target_pairs={{0,1},{1,0},{2,3},{3,2},{4,5},{5,4},{6,7},{7,6},{8,9},{9,8},{10,11... | collective-permute-start | bytes 786440 | tf_op jit(solution)/shard_map/ppermute | solution.py:508
  109.6 2.8 %shard_map.119 = (f32[512,512]{1,0:T(8,128)S(1)}, f32[1,128]{1,0:T(1,128)S(1)}) custom-call(f32[1,128]{1,0:T(1,128)S(1)} %get-tuple-element.70.stats_in, bf16[512,512]{1,0:T(8,128)(2,1)S(1)} %get-tuple-element.57.left, bf16[512,512]{1,0:T(8,128)(2,1)S(1)} %get-tuple-element.58.right, bf16[512,512]{1,0:T(8,128)(2,1)S(1)} %get-tuple-element.50.rest_0_, ...), custom_call_target="tpu_custom_call" | custom-call | flops 1 | bytes 1 | tf_op jit(solution)/shard_map/pallas_call | solution.py:100
  112.4 0.4 shard_map.120.stats_in
  112.8 0.7 shard_map.121
  113.5 23.8 %all_to_all.5 = f32[32,1,128]{2,1,0:T(1,128)S(1)} all-to-all(f32[32,1,128]{2,1,0:T(1,128)S(1)} %bitcast.20), channel_id=1, replica_groups={{16,17,18,19,20,21,22,23,24,25,26,27,28,29,30,31,0,1,2,3,4,5,6,7,8,9,10..., dimensions={0} | all-to-all | bytes 32768 | tf_op jit(solution)/shard_map/all_to_all | solution.py:512
  137.3 2.2 %shard_map.122 = (f32[512,512]{1,0:T(8,128)}, f32[1]{0:T(128)}, f32[1]{0:T(128)}) custom-call(f32[32,128]{1,0:T(8,128)S(1)} %bitcast.19, bf16[512,512]{1,0:T(8,128)(2,1)S(1)} %get-tuple-element.50.rest_0_, bf16[512,512]{1,0:T(8,128)(2,1)S(1)} %get-tuple-element.59.rest_1_, bf16[512,512]{1,0:T(8,128)(2,1)S(1)} %get-tuple-element.60.rest_2_, ...), custom_call_target="tpu_custom_call" | custom-call | flops 1 | bytes 1 | tf_op jit(solution)/shard_map/pallas_call | solution.py:100
  (13 shorter events, 0.0 us)
Async XLA Ops:
  0.6 15.8 %collective-permute-start = (bf16[512,512]{1,0:T(8,128)(2,1)}, bf16[512,512]{1,0:T(8,128)(2,1)S(1)}, u32[]{:S(2)}, u32[]{:S(2)}) collective-permute-start(bf16[512,512]{1,0:T(8,128)(2,1)} %bitcast.17), channel_id=1, source_target_pairs={{0,32},{32,0},{64,96},{96,64},{128,160},{160,128},{192,224},{224,1... | collective-permute-start | bytes 1572872 | tf_op jit(solution)/shard_map/ppermute | solution.py:505
  5.5 1.0 copy-start.1
  6.6 1.0 copy-start.2
  11.4 10.9 %copy-start.4 = (bf16[1024,512]{1,0:T(8,128)(2,1)S(1)}, bf16[1024,512]{1,0:T(8,128)(2,1)}, u32[]{:S(2)}) copy-start(bf16[1024,512]{1,0:T(8,128)(2,1)} %get-tuple-element.49) | copy-start | bytes 3145732
  17.4 16.0 %collective-permute-start.1 = (bf16[512,512]{1,0:T(8,128)(2,1)S(1)}, bf16[512,512]{1,0:T(8,128)(2,1)S(1)}, u32[]{:S(2)}, u32[]{:S(2)}) collective-permute-start(bf16[512,512]{1,0:T(8,128)(2,1)S(1)} %get-tuple-element.45.own_high), channel_id=1, source_target_pairs={{0,96},{32,64},{64,32},{96,0},{128,224},{160,192},{192,160},{224,1... | collective-permute-start | bytes 1572872 | tf_op jit(solution)/shard_map/ppermute | solution.py:505
  22.3 15.9 %collective-permute-start.3 = (bf16[1024,512]{1,0:T(8,128)(2,1)S(1)}, bf16[1024,512]{1,0:T(8,128)(2,1)S(1)}, u32[]{:S(2)}, u32[]{:S(2)}) collective-permute-start(bf16[1024,512]{1,0:T(8,128)(2,1)S(1)} %copy-done.4), channel_id=1, source_target_pairs={{1,0},{2,1},{3,2},{4,3},{5,4},{6,5},{7,6},{8,7},{9,8},{10,9},{11,1... | collective-permute-start | bytes 3145736 | tf_op jit(solution)/shard_map/ppermute | solution.py:508
  23.6 14.6 %collective-permute-start.4 = (bf16[512,512]{1,0:T(8,128)(2,1)S(1)}, bf16[512,512]{1,0:T(8,128)(2,1)S(1)}, u32[]{:S(2)}, u32[]{:S(2)}) collective-permute-start(bf16[512,512]{1,0:T(8,128)(2,1)S(1)} %get-tuple-element.50.rest_0_), channel_id=1, source_target_pairs={{0,1},{1,2},{2,3},{3,4},{4,5},{5,6},{6,7},{7,8},{8,9},{9,10},{10,1... | collective-permute-start | bytes 1572872 | tf_op jit(solution)/shard_map/ppermute | solution.py:508
  34.7 4.5 %copy-start = (bf16[1,1,512,512]{3,2,1,0:T(8,128)(2,1)S(1)}, bf16[1,1,512,512]{3,2,1,0:T(8,128)(2,1)}, u32[]{:S(2)}) copy-start(bf16[1,1,512,512]{3,2,1,0:T(8,128)(2,1)} %param.11) | copy-start | bytes 1572868
  34.7 14.0 %collective-permute-start.2 = (bf16[512,512]{1,0:T(8,128)(2,1)S(1)}, bf16[512,512]{1,0:T(8,128)(2,1)S(1)}, u32[]{:S(2)}, u32[]{:S(2)}) collective-permute-start(bf16[512,512]{1,0:T(8,128)(2,1)S(1)} %get-tuple-element.47.own_high), channel_id=1, source_target_pairs={{0,128},{32,160},{64,192},{96,224},{128,0},{160,32},{192,64},{224,... | collective-permute-start | bytes 1572872 | tf_op jit(solution)/shard_map/ppermute | solution.py:505
  38.3 1.0 copy-start.3
  50.0 14.1 %collective-permute-start.5 = (bf16[512,512]{1,0:T(8,128)(2,1)S(1)}, bf16[512,512]{1,0:T(8,128)(2,1)S(1)}, u32[]{:S(2)}, u32[]{:S(2)}) collective-permute-start(bf16[512,512]{1,0:T(8,128)(2,1)S(1)} %shard_map.107), channel_id=1, source_target_pairs={{0,384},{32,416},{64,448},{96,480},{128,256},{160,288},{192,320},{... | collective-permute-start | bytes 1572872 | tf_op jit(solution)/shard_map/ppermute | solution.py:505
  67.6 8.1 %collective-permute-start.6 = (bf16[512,512]{1,0:T(8,128)(2,1)S(1)}, bf16[512,512]{1,0:T(8,128)(2,1)S(1)}, u32[]{:S(2)}, u32[]{:S(2)}) collective-permute-start(bf16[512,512]{1,0:T(8,128)(2,1)S(1)} %get-tuple-element.59.rest_1_), channel_id=1, source_target_pairs={{1,2},{2,1},{3,4},{4,3},{5,6},{6,5},{7,8},{8,7},{9,10},{10,9},{11,... | collective-permute-start | bytes 1572872 | tf_op jit(solution)/shard_map/ppermute | solution.py:508
  68.3 7.8 %collective-permute-start.7 = (bf16[512,512]{1,0:T(8,128)(2,1)S(1)}, bf16[512,512]{1,0:T(8,128)(2,1)S(1)}, u32[]{:S(2)}, u32[]{:S(2)}) collective-permute-start(bf16[512,512]{1,0:T(8,128)(2,1)S(1)} %get-tuple-element.59.rest_1_), channel_id=1, source_target_pairs={{0,1},{1,0},{2,3},{3,2},{4,5},{5,4},{6,7},{7,6},{8,9},{9,8},{10,11... | collective-permute-start | bytes 1572872 | tf_op jit(solution)/shard_map/ppermute | solution.py:508
  77.2 10.9 %collective-permute-start.8 = (bf16[512,512]{1,0:T(8,128)(2,1)S(1)}, bf16[512,512]{1,0:T(8,128)(2,1)S(1)}, u32[]{:S(2)}, u32[]{:S(2)}) collective-permute-start(bf16[512,512]{1,0:T(8,128)(2,1)S(1)} %get-tuple-element.64.rest_3_), channel_id=1, source_target_pairs={{1,2},{2,1},{3,4},{4,3},{5,6},{6,5},{7,8},{8,7},{9,10},{10,9},{11,... | collective-permute-start | bytes 1572872 | tf_op jit(solution)/shard_map/ppermute | solution.py:508
  77.9 10.7 %collective-permute-start.9 = (bf16[512,512]{1,0:T(8,128)(2,1)S(1)}, bf16[512,512]{1,0:T(8,128)(2,1)S(1)}, u32[]{:S(2)}, u32[]{:S(2)}) collective-permute-start(bf16[512,512]{1,0:T(8,128)(2,1)S(1)} %get-tuple-element.64.rest_3_), channel_id=1, source_target_pairs={{0,1},{1,0},{2,3},{3,2},{4,5},{5,4},{6,7},{7,6},{8,9},{9,8},{10,11... | collective-permute-start | bytes 1572872 | tf_op jit(solution)/shard_map/ppermute | solution.py:508
  89.7 10.4 %collective-permute-start.10 = (bf16[512,512]{1,0:T(8,128)(2,1)S(1)}, bf16[512,512]{1,0:T(8,128)(2,1)S(1)}, u32[]{:S(2)}, u32[]{:S(2)}) collective-permute-start(bf16[512,512]{1,0:T(8,128)(2,1)S(1)} %get-tuple-element.68.rest_5_), channel_id=1, source_target_pairs={{1,2},{2,1},{3,4},{4,3},{5,6},{6,5},{7,8},{8,7},{9,10},{10,9},{11,... | collective-permute-start | bytes 1572872 | tf_op jit(solution)/shard_map/ppermute | solution.py:508
  90.4 10.2 %collective-permute-start.11 = (bf16[512,512]{1,0:T(8,128)(2,1)S(1)}, bf16[512,512]{1,0:T(8,128)(2,1)S(1)}, u32[]{:S(2)}, u32[]{:S(2)}) collective-permute-start(bf16[512,512]{1,0:T(8,128)(2,1)S(1)} %get-tuple-element.68.rest_5_), channel_id=1, source_target_pairs={{0,1},{1,0},{2,3},{3,2},{4,5},{5,4},{6,7},{7,6},{8,9},{9,8},{10,11... | collective-permute-start | bytes 1572872 | tf_op jit(solution)/shard_map/ppermute | solution.py:508
  101.7 10.7 %collective-permute-start.12 = (bf16[512,256]{1,0:T(8,128)(2,1)S(1)}, bf16[512,256]{1,0:T(8,128)(2,1)S(1)}, u32[]{:S(2)}, u32[]{:S(2)}) collective-permute-start(bf16[512,256]{1,0:T(8,128)(2,1)S(1)} %get-tuple-element.75), channel_id=1, source_target_pairs={{1,2},{2,1},{3,4},{4,3},{5,6},{6,5},{7,8},{8,7},{9,10},{10,9},{11,... | collective-permute-start | bytes 786440 | tf_op jit(solution)/shard_map/ppermute | solution.py:508
  102.4 10.4 %collective-permute-start.13 = (bf16[512,256]{1,0:T(8,128)(2,1)S(1)}, bf16[512,256]{1,0:T(8,128)(2,1)S(1)}, u32[]{:S(2)}, u32[]{:S(2)}) collective-permute-start(bf16[512,256]{1,0:T(8,128)(2,1)S(1)} %get-tuple-element.75), channel_id=1, source_target_pairs={{0,1},{1,0},{2,3},{3,2},{4,5},{5,4},{6,7},{7,6},{8,9},{9,8},{10,11... | collective-permute-start | bytes 786440 | tf_op jit(solution)/shard_map/ppermute | solution.py:508
